TPU v7x, 32 devices: a whole 2x2x4 slice. The times are simulated.
32 devices in a mesh: band: 4 (over z), tile: 8 (over y, x, core).
Axes of the slice: x: 2, y: 2, z: 4, core: 2. Of those that a mesh axis runs over, the one named last changes fastest.
Arguments:
- pixel_map: bfloat16 [4, 384, 4, 128], P('band', 'tile'), may hold values from -6 to 6
- interp_bands: bfloat16 [2, 2, 128, 128], replicated, may hold values from -0.375 to 0.375
- conv1_weight: bfloat16 [16, 4, 3, 3], replicated, may hold values from -1 to 1
- conv1_bias: float32 [16], replicated, may hold values from -3 to 3
- conv2_weight: bfloat16 [16, 16, 3, 3], replicated, may hold values from -0.5 to 0.5
- send_rows: int32 [4, 8, 8, 32], P('band', 'tile'), may hold values from 0 to 47
- patch_slots: int32 [4, 8, 129], P('band', 'tile'), may hold values from 0 to 255
- patch_rows: int32 [4, 8], P('band', 'tile'), may hold values from 64 to 128, as said below
- cotangent: bfloat16 [4, 8, 16, 128, 128], P('band', 'tile'), may hold values from -18 to 18
Outputs:
- grad_map: float32 [4, 384, 4, 128], P('band', 'tile')
- grad_conv1: float32 [16, 4, 3, 3], replicated
- grad_bias: float32 [16], replicated
- grad_conv2: float32 [16, 16, 3, 3], replicated
Inputs may be any that keep to these rules, and one draw needn't show every extreme that they name: `patch_rows`: every draw has a patch with all 128 rows valid.
All inputs are finite; a program needn't handle non-finite values.
Results may differ from a plain program's by a relative error of at most 0.0044.
Values may be sent and summed in bfloat16 or wider, within the bound.
No kernel may reach another device: no remote copies, remote signals or barrier semaphores. Data moves between devices by JAX's collectives and lax.ppermute only.
A program may use at most 128 MiB of HBM per device.

v0:
```python
import jax
import jax.numpy as jnp
from jax import lax
from jax.sharding import PartitionSpec as P


def conv_same(images, kernel):
    return lax.conv_general_dilated(
        images,
        kernel,
        (1, 1),
        ((1, 1), (1, 1)),
        dimension_numbers=("NCHW", "OIHW", "NCHW"),
        preferred_element_type=jnp.float32,
    )


def kernel_grad(images, upstream):
    result = lax.conv_general_dilated(
        images,
        upstream,
        (1, 1),
        ((1, 1), (1, 1)),
        dimension_numbers=("CNHW", "IOHW", "NCHW"),
        preferred_element_type=jnp.float32,
    )
    return jnp.transpose(result, (1, 0, 2, 3))


def flipped(weights):
    return jnp.flip(jnp.transpose(weights, (1, 0, 2, 3)), (2, 3))


def patch_grads(sources, matrices, row_valid, upstream, conv1_weight, conv1_bias, conv2_weight):
    patch_count, row_length = (sources.shape[0], sources.shape[3])
    paired = jnp.concatenate([sources[:, :-1], sources[:, 1:]], axis=3)
    stacked = matrices.reshape(2 * row_length, row_length)
    rows_out = jnp.dot(
        paired.reshape(-1, 2 * row_length), stacked, preferred_element_type=jnp.float32
    )
    rows_out = rows_out.reshape(patch_count, row_length, -1, row_length)
    rows_out = jnp.where(row_valid[:, :, None, None], rows_out, 0.0)
    patch_image = jnp.transpose(rows_out.astype(jnp.bfloat16), (0, 2, 1, 3))
    pre_act = conv_same(patch_image, conv1_weight) + conv1_bias[None, :, None, None]
    gating = jax.nn.sigmoid(pre_act)
    hidden = (pre_act * gating).astype(jnp.bfloat16)
    grad_w2 = kernel_grad(hidden, upstream)
    grad_hidden = conv_same(upstream, flipped(conv2_weight))
    grad_pre = (grad_hidden * gating * (1.0 + pre_act * (1.0 - gating))).astype(jnp.bfloat16)
    grad_w1 = kernel_grad(patch_image, grad_pre)
    grad_b1 = jnp.sum(grad_pre, axis=(0, 2, 3), dtype=jnp.float32)
    grad_image = conv_same(grad_pre, flipped(conv1_weight))
    grad_rows = jnp.transpose(grad_image, (0, 2, 1, 3))
    grad_rows = jnp.where(row_valid[:, :, None, None], grad_rows, 0.0).astype(jnp.bfloat16)
    paired_grad = jnp.dot(
        grad_rows.reshape(-1, row_length), stacked.T, preferred_element_type=jnp.float32
    )
    paired_grad = paired_grad.reshape(patch_count, row_length, -1, 2 * row_length)
    lower = paired_grad[..., :row_length]
    higher = paired_grad[..., row_length:]
    zero_row = jnp.zeros_like(lower[:, :1])
    grad_src = jnp.concatenate([lower, zero_row], axis=1) + jnp.concatenate(
        [zero_row, higher], axis=1
    )
    return (grad_src, grad_w1, grad_b1, grad_w2)


def shards(
    pixel_map,
    interp_bands,
    conv1_weight,
    conv1_bias,
    conv2_weight,
    send_rows,
    patch_slots,
    patch_rows,
    cotangent,
):
    tile_count = lax.axis_size("tile")
    band_count = lax.axis_size("band")
    band_index = lax.axis_index("band")
    owned_blocks = pixel_map[0]
    block_count, freq_count, row_length = owned_blocks.shape
    send_lists = send_rows[0, 0]
    capacity = send_lists.shape[1]
    slot_ids = patch_slots[0]
    patch_count, source_count = slot_ids.shape
    outgoing = jnp.take(owned_blocks, send_lists.reshape(-1), axis=0)
    received = lax.all_to_all(outgoing, "tile", split_axis=0, concat_axis=0, tiled=True)
    sources = jnp.take(received, slot_ids.reshape(-1), axis=0)
    sources = sources.reshape(patch_count, source_count, freq_count, row_length)
    is_polar = jnp.logical_or(
        band_index < band_count // 4, band_index >= band_count - band_count // 4
    )
    matrices = jnp.where(is_polar, interp_bands[0], interp_bands[1])
    row_valid = jnp.arange(row_length)[None, :] < patch_rows[0][:, None]
    grad_src, grad_w1, grad_b1, grad_w2 = patch_grads(
        sources, matrices, row_valid, cotangent[0], conv1_weight, conv1_bias, conv2_weight
    )
    norm_scale = float(band_count * tile_count * patch_count * row_length * row_length) ** (-0.5)
    summed = lax.psum(
        (grad_w1 * norm_scale, grad_b1 * norm_scale, grad_w2 * norm_scale), ("band", "tile")
    )
    flat_grads = grad_src.reshape(-1, freq_count, row_length)
    slot_grads = jax.ops.segment_sum(
        flat_grads, slot_ids.reshape(-1), num_segments=tile_count * capacity
    )
    returned = lax.all_to_all(slot_grads, "tile", split_axis=0, concat_axis=0, tiled=True)
    selector = (
        send_lists.reshape(-1)[None, :] == jnp.arange(block_count, dtype=jnp.int32)[:, None]
    ).astype(jnp.float32)
    grad_blocks = jnp.dot(
        selector, returned.reshape(tile_count * capacity, -1), precision=lax.Precision.HIGHEST
    )
    grad_blocks = grad_blocks.reshape(block_count, freq_count, row_length)
    return (grad_blocks[None], summed[0], summed[1], summed[2])


def solution(mesh):
    in_specs = (
        P("band", "tile", None, None),
        P(),
        P(),
        P(),
        P(),
        P("band", "tile", None, None),
        P("band", "tile", None),
        P("band", "tile"),
        P("band", "tile", None, None, None),
    )
    out_specs = (P("band", "tile", None, None), P(), P(), P())
    return jax.shard_map(shards, mesh=mesh, in_specs=in_specs, out_specs=out_specs, check_vma=False)
```

profile of v0, /device:TPU:0, one launch (start us, length us, event | category | flops | bytes accessed | tf_op | source)
XLA Modules:
  0.0 291.6 jit_solution(4437472849832912835)
XLA Ops:
  0.6 0.0 copy-start
  0.6 0.8 reshape_squeeze.7
  1.4 0.8 eq.31
  2.2 0.5 copy-done.9
  2.8 1.0 gather_fusion
  3.7 1.1 broadcast_select_fusion.2
  4.8 5.2 %all-to-all-start = ((bf16[256,4,128]{2,1,0:T(4,128)(2,1)}), bf16[256,4,128]{2,1,0:T(4,128)(2,1)S(1)}, u32[]{:S(2)}, u32[]{:S(2)}) async-start(bf16[256,4,128]{2,1,0:T(4,128)(2,1)} %broadcast_select_fusion.2), calls=%async_computation | async-start | bytes 524288 | tf_op jit(solution)/shard_map/all_to_all | solution.py:89
  10.0 0.7 compare_select_fusion
  10.7 0.7 compare_and_fusion.1
  12.0 1.5 copy.145
  13.5 0.1 fusion.90
  13.7 0.0 copy-start.8
  13.7 3.9 %copy.147 = bf16[16,128,1,8,17]{0,3,4,1,2:T(8,128)(2,1)} copy(bf16[16,128,1,8,17]{1,0,4,3,2:T(8,128)(2,1)S(1)} %bitcast.104) | data formatting | bytes 1114112 | tf_op jit(solution)/shard_map/conv_general_dilated | solution.py:8
  17.5 1.2 slice.41
  18.7 0.0 copy-start.15
  18.7 3.8 %copy.167 = bf16[16,128,8,17,1]{0,2,4,3,1:T(8,128)(2,1)} copy(bf16[16,128,8,17,1]{1,0,3,2,4:T(8,128)(2,1)S(1)} %bitcast.103) | data formatting | bytes 1114112 | tf_op jit(solution)/shard_map/squeeze | solution.py:98
  22.6 0.0 all-to-all-done
  22.6 0.8 gather_fusion.1
  23.4 0.1 bitcast_select_fusion
  23.5 0.2 fusion.54
  23.8 0.1 copy.178
  23.9 0.1 fusion.95
  24.0 0.8 fusion.92
  24.8 2.2 copy.152
  27.1 0.2 slice.44
  27.3 0.0 slice-start.1
  27.3 0.0 copy-start.12
  27.3 0.0 copy-start.13
  27.3 0.0 copy-start.14
  27.3 7.2 %fusion.38 = f32[128,8,17,16]{3,1,2,0:T(8,128)S(1)} fusion(bf16[16,4,3,3]{0,1,3,2:T(4,128)(2,1)S(1)} %copy-done.15, bf16[128,4,1,7,2]{3,1,4,0,2:T(4,128)(2,1)S(1)} %slice.44, bf16[128,4,1,8,17]{3,1,4,0,2:T(4,128)(2,1)S(1)} %copy.152), kind=kOutput, calls=%fused_computation.54 | convolution fusion | flops 20416512 | bytes 1268864 | tf_op jit(solution)/shard_map/conv_general_dilated | solution.py:8
  34.6 9.9 %select_reduce_fusion = (f32[16]{0:T(128)S(1)}, bf16[128,8,17,16]{3,1,2,0:T(8,128)(2,1)S(1)}) fusion(pred[8,17]{0,1:T(8,128)(4,1)S(1)} %copy-done.12, f32[16]{0:T(128)S(1)} %copy-done.13, f32[128,8,17,16]{3,1,2,0:T(8,128)S(1)} %fusion.38, bf16[16,16,3,3]{1,0,3,2:T(8,128)(2,1)S(1)} %copy-done.14, bf16[16,128,1,7,2]{0,3,4,1,2:T(8,128)(2,1)S(1)} %slice.41, ...), kind=kOutput, calls=%fused_computation.14 | convolution fusion | flops 85843952 | bytes 2290440 | tf_op jit(solution)/shard_map/conv_general_dilated | solution.py:8
  44.5 3.9 %fusion.32 = (bf16[128,8,17,16]{3,1,2,0:T(8,128)(2,1)S(1)}, bf16[128,1,8,17,16]{4,2,3,0,1:T(8,128)(2,1)S(1)}) fusion(f32[16]{0:T(128)S(1)} %copy-done.13, f32[128,8,17,16]{3,1,2,0:T(8,128)S(1)} %fusion.38, pred[8,17]{0,1:T(8,128)(4,1)S(1)} %copy-done.12, bf16[128,8,17,16]{3,1,2,0:T(8,128)(2,1)S(1)} %get-tuple-element.52), kind=kLoop, calls=%fused_computation.47 | loop fusion | flops 2506752 | bytes 2785480 | tf_op jit(solution)/shard_map/convert_element_type | solution.py:46
  48.4 0.1 fusion.88
  48.5 4.4 %fusion.87 = (bf16[128,1,8,16,16]{4,2,3,0,1:T(8,128)(2,1)}, bf16[128,1,8,16,16]{4,2,3,0,1:T(8,128)(2,1)}) fusion(bf16[128,1,8,17,16]{4,2,3,0,1:T(8,128)(2,1)S(1)} %bitcast.99), kind=kLoop, calls=%fused_computation.111 | loop fusion | bytes 2097152 | tf_op jit(solution)/shard_map/convert_element_type | solution.py:46
  52.9 0.7 copy-done.2
  53.6 0.1 fusion.89
  53.7 117.9 %fusion.10 = bf16[128,8,17,4]{1,3,2,0:T(4,128)(2,1)S(1)} fusion(bf16[16,4,3,3]{0,1,3,2:T(4,128)(2,1)S(1)} %copy-done.15, bf16[128,1,7,1,16]{4,2,3,0,1:T(8,128)(2,1)S(1)} %get-tuple-element.36, bf16[128,1,7,1,16]{4,2,3,0,1:T(8,128)(2,1)S(1)} %get-tuple-element.35, bf16[128,1,8,17,16]{4,2,3,0,1:T(8,128)(2,1)S(1)} %get-tuple-element.50), kind=kOutput, calls=%fused_computation.25 | convolution fusion | flops 23062528 | bytes 754816 | tf_op jit(solution)/shard_map/transpose | solution.py:53
  171.6 0.0 copy-start.11
  171.6 2.0 copy.153
  173.7 0.1 copy.154
  173.8 0.1 copy.173
  173.9 0.2 convolution_bitcast_fusion
  174.2 0.1 copy.156
  174.3 0.9 broadcast_in_dim.49
  175.2 14.4 %scatter_fusion = f32[256,4,128]{2,1,0:T(4,128)} fusion(f32[256,4,128]{2,1,0:T(4,128)} %broadcast_in_dim.49, s32[129]{0:T(256)S(1)} %bitcast.114, f32[129,4,128]{2,1,0:T(4,128)S(1)} %copy.156), kind=kCustom, calls=%fused_computation.2 | custom fusion | flops 66048 | bytes 793092 | tf_op jit(solution)/shard_map/scatter-add | solution.py:105
  189.6 4.2 %all-to-all-start.1 = ((f32[256,4,128]{2,1,0:T(4,128)}), f32[256,4,128]{2,1,0:T(4,128)S(1)}, u32[]{:S(2)}, u32[]{:S(2)}) async-start(f32[256,4,128]{2,1,0:T(4,128)} %scatter_fusion), calls=%async_computation.1 | async-start | bytes 1048576 | tf_op jit(solution)/shard_map/all_to_all | solution.py:108
  193.8 0.2 copy.177
  194.0 3.1 %copy.176 = bf16[128,4,1,8,16]{3,1,4,0,2:T(4,128)(2,1)S(1)} copy(bf16[128,4,1,8,16]{0,1,4,3,2:T(4,128)(2,1)} %get-tuple-element.42) | data formatting | bytes 262144
  197.1 4.1 %copy.175 = bf16[128,4,1,8,16]{3,1,4,0,2:T(4,128)(2,1)} copy(bf16[128,4,1,8,16]{0,1,4,3,2:T(4,128)(2,1)} %get-tuple-element.41) | data formatting | bytes 262144
  201.2 0.8 copy.174
  202.0 2.6 copy.164
  204.7 4.2 %fusion.28 = bf16[128,8,17,16,1]{3,1,2,0,4:T(8,128)(2,1)} fusion(bf16[128,1,7,1,16]{4,2,3,0,1:T(8,128)(2,1)S(1)} %get-tuple-element.34, bf16[128,1,8,16,16]{4,2,3,0,1:T(8,128)(2,1)} %get-tuple-element.32), kind=kLoop, calls=%fused_computation.41 | loop fusion | flops 1671168 | bytes 1110016 | tf_op jit(solution)/shard_map/convert_element_type | solution.py:46
  208.9 2.6 fusion.30
  211.5 4.0 %fusion.46 = (bf16[128,4,8,17,1]{2,1,4,3,0:T(4,128)(2,1)}, bf16[128,4,8,17,1]{2,1,4,3,0:T(4,128)(2,1)}) fusion(bf16[128,4,1,7,1]{3,1,4,0,2:T(4,128)(2,1)S(1)} %copy.177, bf16[128,4,1,8,16]{3,1,4,0,2:T(4,128)(2,1)S(1)} %copy.176, bf16[128,4,1,8,16]{3,1,4,0,2:T(4,128)(2,1)S(1)} %copy-done.4, bf16[128,4,1,7,1]{3,1,4,0,2:T(4,128)(2,1)S(1)} %copy-done.7), kind=kLoop, calls=%fused_computation.61 | loop fusion | flops 835584 | bytes 555008 | tf_op jit(solution)/shard_map/convert_element_type | solution.py:43
  215.5 16.7 %fusion.58 = f32[16,16,3,3]{0,1,3,2:T(8,128)S(1)} fusion(bf16[16,128,8,17,1]{0,2,4,3,1:T(8,128)(2,1)} %copy.167, bf16[128,8,17,16,1]{3,1,2,0,4:T(8,128)(2,1)} %fusion.28, bf16[128,8,17,16,1]{3,1,2,0,4:T(8,128)(2,1)} %bitcast.100, bf16[128,8,17,16,1]{3,1,2,0,4:T(8,128)(2,1)} %fusion.30), kind=kOutput, calls=%fused_computation.72 | convolution fusion | flops 81471744 | bytes 2237440 | tf_op jit(solution)/shard_map/transpose | solution.py:27
  232.3 0.0 copy-start.10
  232.3 0.0 copy-start.1
  232.3 14.7 %fusion.64 = f32[16,4,3,3]{0,1,3,2:T(4,128)S(1)} fusion(bf16[128,8,17,16]{3,1,2,0:T(8,128)(2,1)} %copy-done.5, pred[8,17]{0,1:T(8,128)(4,1)S(1)} %copy-done.12, bf16[128,4,8,17,1]{2,1,4,3,0:T(4,128)(2,1)} %get-tuple-element.53, bf16[128,4,8,17,1]{2,1,4,3,0:T(4,128)(2,1)S(1)} %copy-done.6, bf16[128,4,8,17,1]{2,1,4,3,0:T(4,128)(2,1)} %get-tuple-element.54), kind=kOutput, calls=%fused_computation.74 | convolution fusion | flops 21482048 | bytes 977288 | tf_op jit(solution)/shard_map/transpose | solution.py:27
  247.0 42.3 %all-reduce.2 = (f32[16,4,3,3]{0,1,3,2:T(4,128)}, f32[16]{0:T(128)}, f32[16,16,3,3]{0,1,3,2:T(8,128)S(1)}) all-reduce(f32[16,4,3,3]{0,1,3,2:T(4,128)S(1)} %fusion.64, f32[16]{0:T(128)S(1)} %broadcast_multiply_fusion, f32[16,16,3,3]{0,1,3,2:T(8,128)S(1)} %fusion.58), channel_id=1, replica_groups=mesh['band'=4,'tile'=8] {'band','tile'}, use_global_device_ids=true, to_apply=%region_1.2 | all-reduce | flops 2896 | bytes 23168 | tf_op jit(solution)/shard_map/psum | solution.py:101
  289.3 0.7 copy.169
  290.1 0.0 all-to-all-done.1
  290.1 0.2 copy.172
  290.3 0.4 convolution_bitcast_fusion.1
  290.7 0.7 copy.168
  (38 shorter events, 0.3 us)
Async XLA Ops:
  0.6 2.1 copy-start
  2.2 0.6 copy-start.9
  4.8 17.8 %all-to-all-start = ((bf16[256,4,128]{2,1,0:T(4,128)(2,1)}), bf16[256,4,128]{2,1,0:T(4,128)(2,1)S(1)}, u32[]{:S(2)}, u32[]{:S(2)}) async-start(bf16[256,4,128]{2,1,0:T(4,128)(2,1)} %broadcast_select_fusion.2), calls=%async_computation | async-start | bytes 524288 | tf_op jit(solution)/shard_map/all_to_all | solution.py:89
  13.7 8.9 %copy-start.8 = (bf16[2,2,128,128]{3,2,1,0:T(8,128)(2,1)S(1)}, bf16[2,2,128,128]{3,2,1,0:T(8,128)(2,1)}, u32[]{:S(2)}) copy-start(bf16[2,2,128,128]{3,2,1,0:T(8,128)(2,1)} %param.10) | copy-start | bytes 393220
  18.7 8.5 %copy-start.15 = (bf16[16,4,3,3]{0,1,3,2:T(4,128)(2,1)S(1)}, bf16[16,4,3,3]{0,1,3,2:T(4,128)(2,1)}, u32[]{:S(2)}) copy-start(bf16[16,4,3,3]{0,1,3,2:T(4,128)(2,1)} %param.11) | copy-start | bytes 3460
  27.0 7.5 %slice-start = ((s8[4456448]{0:T(1024)(128)(4,1)}), s8[4194304]{0:T(1024)(128)(4,1)S(1)}, s32[]{:S(2)}) async-start(s8[4456448]{0:T(1024)(128)(4,1)} %bitcast.101), calls=%async_computation.2 | async-start | bytes 8388608
  27.3 7.3 %slice-start.1 = ((s8[4456448]{0:T(1024)(128)(4,1)}), s8[262144]{0:T(1024)(128)(4,1)S(1)}, s32[]{:S(2)}) async-start(s8[4456448]{0:T(1024)(128)(4,1)} %bitcast.101), calls=%async_computation.3 | async-start | bytes 524288
  27.3 7.3 %copy-start.12 = (pred[8,17]{0,1:T(8,128)(4,1)S(1)}, pred[8,17]{0,1:T(8,128)(4,1)}, u32[]{:S(2)}) copy-start(pred[8,17]{0,1:T(8,128)(4,1)} %constant.80) | copy-start | bytes 412
  27.3 7.3 %copy-start.13 = (f32[16]{0:T(128)S(1)}, f32[16]{0:T(128)}, u32[]{:S(2)}) copy-start(f32[16]{0:T(128)} %param.12) | copy-start | bytes 196
  27.3 7.3 %copy-start.14 = (bf16[16,16,3,3]{1,0,3,2:T(8,128)(2,1)S(1)}, bf16[16,16,3,3]{1,0,3,2:T(8,128)(2,1)}, u32[]{:S(2)}) copy-start(bf16[16,16,3,3]{1,0,3,2:T(8,128)(2,1)} %param.13) | copy-start | bytes 13828
  44.5 3.9 %copy-start.5 = (bf16[128,8,17,16]{3,1,2,0:T(8,128)(2,1)}, bf16[128,8,17,16]{3,1,2,0:T(8,128)(2,1)S(1)}, u32[]{:S(2)}) copy-start(bf16[128,8,17,16]{3,1,2,0:T(8,128)(2,1)S(1)} %get-tuple-element.52) | copy-start | bytes 1671172
  48.4 5.2 %copy-start.2 = (bf16[128,8,17,16]{3,1,2,0:T(8,128)(2,1)}, bf16[128,8,17,16]{3,1,2,0:T(8,128)(2,1)S(1)}, u32[]{:S(2)}) copy-start(bf16[128,8,17,16]{3,1,2,0:T(8,128)(2,1)S(1)} %get-tuple-element.49) | copy-start | bytes 1671172
  171.6 3.6 %copy-start.11 = (s32[1,1,129]{2,1,0:T(1,128)S(1)}, s32[1,1,129]{2,1,0:T(1,128)}, u32[]{:S(2)}) copy-start(s32[1,1,129]{2,1,0:T(1,128)} %param.15) | copy-start | bytes 1552
  189.6 100.5 %all-to-all-start.1 = ((f32[256,4,128]{2,1,0:T(4,128)}), f32[256,4,128]{2,1,0:T(4,128)S(1)}, u32[]{:S(2)}, u32[]{:S(2)}) async-start(f32[256,4,128]{2,1,0:T(4,128)} %scatter_fusion), calls=%async_computation.1 | async-start | bytes 1048576 | tf_op jit(solution)/shard_map/all_to_all | solution.py:108
  204.7 4.2 %copy-start.3 = (bf16[128,1,8,16,16]{4,2,3,0,1:T(8,128)(2,1)S(1)}, bf16[128,1,8,16,16]{4,2,3,0,1:T(8,128)(2,1)}, u32[]{:S(2)}) copy-start(bf16[128,1,8,16,16]{4,2,3,0,1:T(8,128)(2,1)} %get-tuple-element.31) | copy-start | bytes 1572868
  208.9 2.6 copy-start.4
  208.9 2.6 copy-start.7
  215.5 16.8 %copy-start.6 = (bf16[128,4,8,17,1]{2,1,4,3,0:T(4,128)(2,1)S(1)}, bf16[128,4,8,17,1]{2,1,4,3,0:T(4,128)(2,1)}, u32[]{:S(2)}) copy-start(bf16[128,4,8,17,1]{2,1,4,3,0:T(4,128)(2,1)} %copy.164) | copy-start | bytes 417796
  232.3 58.0 %copy-start.10 = (s32[256]{0:T(256)S(1)}, s32[256]{0:T(256)}, u32[]{:S(2)}) copy-start(s32[256]{0:T(256)} %copy-done.9) | copy-start | bytes 3076
  232.3 59.1 %copy-start.1 = (bf16[1,48,4,128]{3,2,1,0:T(4,128)(2,1)S(1)}, bf16[1,48,4,128]{3,2,1,0:T(4,128)(2,1)}, u32[]{:S(2)}) copy-start(bf16[1,48,4,128]{3,2,1,0:T(4,128)(2,1)} %param.9) | copy-start | bytes 147460
where the time goes:
time: 297 us; the launch traced here: 292 us
  matrix products  167 us (56%)
  blocking collectives  42.3 us (14%)
  local copies, waits for them, and re-layouts  38.8 us (13%)
  other arithmetic  31.8 us (11%)
  starting transfers between devices  9.41 us (3%)
    transpose x1, matrix products, patch_grads(): grad_rows = jnp.transpose(grad_image, (0, 2, 1, 3))  118 us
    psum x1, blocking collectives, shards(): lax.psum((grad_w1 * norm_scale, grad_b1 * norm_scale, grad_w2 * norm_scal...  42.3 us
    transpose x2, matrix products, kernel_grad(): return jnp.transpose(result, (1, 0, 2, 3))  31.5 us
    conv_general_dilated x2, matrix products, conv_same(): lax.conv_general_dilated(images, kernel, (1, 1), ((1, 1), (1, 1)), dimens...  17.1 us
    scatter-add x1, other arithmetic, shards(): jax.ops.segment_sum(flat_grads, slot_ids.reshape(-1), num_segments=tile_c...  14.4 us
    unnamed x45, local copies, waits for them, and re-layouts  12.6 us
    convert_element_type x3, other arithmetic, patch_grads(): hidden = (pre_act * gating).astype(jnp.bfloat16)  10.7 us
    conv_general_dilated x4, local copies, waits for them, and re-layouts, conv_same(): lax.conv_general_dilated(images, kernel, (1, 1), ((1, 1), (1, 1)), dimens...  7.52 us
  transfers between devices with their start and end apart: 2, of which 0 were waited for; matrix products, arithmetic and copies ran while one was open for 23% of the time, Pallas kernels for 0%

commit v1 on v0

v1 whole, which is shorter than its diff:
```python
import functools

import jax
import jax.numpy as jnp
from jax import lax
from jax.experimental import pallas as pl
from jax.experimental.pallas import tpu as pltpu
from jax.sharding import PartitionSpec as P

BF = jnp.bfloat16
F32 = jnp.float32
I32 = jnp.int32
S = 128
FREQ = 4
CH = 16
R = 8
NB = S // R
WIN = (R + 2) * CH
XW = 48
LANES = NB * S
SRC = 144
VMEM_LIMIT = 48 * 1024 * 1024


def iota(shape, axis):
    return lax.broadcasted_iota(I32, shape, axis)


def dot(a, b):
    return lax.dot_general(a, b, (((1,), (0,)), ((), ())), preferred_element_type=F32)


def dot_t(a, b):
    return lax.dot_general(a, b, (((1,), (1,)), ((), ())), preferred_element_type=F32)


def third(k):
    return (k * 171) >> 9


def shifted(rows, step):
    lane = iota(rows.shape, 1)
    if step == 1:
        return jnp.where(lane == S - 1, 0.0, pltpu.roll(rows, S - 1, 1))
    return jnp.where(lane == 0, 0.0, pltpu.roll(rows, 1, 1))


def store_window(ref, base, y, tile):
    block, r = divmod(y, R)
    ref[base + (r + 1) * CH : base + (r + 2) * CH, block * S : (block + 1) * S] = tile
    if r == 0 and block > 0:
        ref[base + (R + 1) * CH : base + WIN, (block - 1) * S : block * S] = tile
    if r == R - 1 and block < NB - 1:
        ref[base : base + CH, (block + 1) * S : (block + 2) * S] = tile


def zero_edges(ref, base):
    zero = jnp.zeros((CH, S), BF)
    ref[base : base + CH, 0:S] = zero
    ref[base + (R + 1) * CH : base + WIN, LANES - S : LANES] = zero


def outgoing_kernel(rows_ref, map_ref, out_ref):
    owners, capacity = rows_ref.shape
    for t in range(owners):
        for c in range(capacity):
            out_ref[t * capacity + c] = map_ref[rows_ref[t, c]]


def prepare_kernel(
    polar_ref,
    cot_ref,
    w1_ref,
    w1t_ref,
    w2t_ref,
    bias_ref,
    interp_ref,
    slots_ref,
    send_ref,
    cb_ref,
    gh_ref,
    t1_ref,
    bcol_ref,
    t3_ref,
    ms_ref,
    mt_ref,
    oh_ref,
    sel_ref,
    plane,
    lists,
    t2_ref,
):
    owners, capacity = send_ref.shape
    chunk = capacity + CH
    nsrc = slots_ref.shape[1]
    for o in range(CH):
        plane[o * S : (o + 1) * S, :] = cot_ref[o * S : (o + 1) * S, :].astype(F32)
    for dx in range(3):
        zero_edges(cb_ref, dx * WIN)
    for y in range(S):
        rows = plane[pl.ds(y, CH, stride=S), :]
        store_window(cb_ref, 0, y, shifted(rows, 1).astype(BF))
        store_window(cb_ref, WIN, y, rows.astype(BF))
        store_window(cb_ref, 2 * WIN, y, shifted(rows, -1).astype(BF))

    pick = ((iota((R * CH, CH), 0) & 15) == iota((R * CH, CH), 1)).astype(BF)
    spread = dot(pick, w2t_ref[...]).astype(BF)
    row, col = iota((R * CH, 3 * WIN), 0), iota((R * CH, 3 * WIN), 1)
    gap = ((col - jnp.where(col >= 2 * WIN, 2 * WIN, jnp.where(col >= WIN, WIN, 0))) >> 4) - (row >> 4)
    k, kcol = iota((CH * 9, 3 * WIN), 0), iota((CH * 9, 3 * WIN), 1)
    kdx = jnp.where(kcol >= 2 * WIN, 2, jnp.where(kcol >= WIN, 1, 0))
    source = (kcol & 15) * 9 + kdx
    banded = jnp.zeros((R * CH, 3 * WIN), F32)
    for dy in range(3):
        term = dot(spread, (k == source + dy * 3).astype(BF))
        banded = jnp.where(gap == 2 - dy, term, banded)
    t2_ref[...] = banded.astype(BF)
    for n in range(0, LANES, 512):
        gh_ref[:, n : n + 512] = dot(t2_ref[...], cb_ref[:, n : n + 512])

    spread = dot(pick, w1_ref[...]).astype(BF)
    width = 3 * XW + CH
    row, col = iota((R * CH, width), 0), iota((R * CH, width), 1)
    cdx = jnp.where(col >= 3 * XW, 3, jnp.where(col >= 2 * XW, 2, jnp.where(col >= XW, 1, 0)))
    gap = ((col - cdx * XW) >> 2) - (row >> 4)
    gap = jnp.where(cdx == 3, -1, gap)
    k, kcol = iota((FREQ * 9, width), 0), iota((FREQ * 9, width), 1)
    kdx = jnp.where(kcol >= 3 * XW, 3, jnp.where(kcol >= 2 * XW, 2, jnp.where(kcol >= XW, 1, 0)))
    source = (kcol & 3) * 9 + kdx
    banded = jnp.zeros((R * CH, width), F32)
    for dy in range(3):
        term = dot(spread, (k == source + dy * 3).astype(BF))
        banded = jnp.where(gap == dy, term, banded)
    t1_ref[...] = banded.astype(BF)
    where_bias = (iota((R * CH, CH), 0) & 15) == iota((R * CH, CH), 1)
    column = jnp.sum(jnp.where(where_bias, bias_ref[...], 0.0), axis=1, keepdims=True)
    bcol_ref[...] = jnp.broadcast_to(column, (R * CH, S))

    part = R * FREQ
    tall = 3 * part
    pick = ((iota((tall, FREQ), 0) & 3) == iota((tall, FREQ), 1)).astype(BF)
    spread = dot(pick, w1t_ref[...])
    row, k = iota((tall, CH * 9), 0), iota((tall, CH * 9), 1)
    rdx = jnp.where(row >= 2 * part, 2, jnp.where(row >= part, 1, 0))
    spread = jnp.where(k - 3 * third(k) == rdx, spread, 0.0).astype(BF)
    row, col = iota((tall, WIN), 0), iota((tall, WIN), 1)
    gap = (col >> 4) - ((row & (part - 1)) >> 2)
    k, kcol = third(iota((CH * 9, WIN), 0)), iota((CH * 9, WIN), 1)
    banded = jnp.zeros((tall, WIN), F32)
    for dy in range(3):
        term = dot(spread, (k == (kcol & 15) * 3 + dy).astype(BF))
        banded = jnp.where(gap == 2 - dy, term, banded)
    t3_ref[...] = banded.astype(BF)

    for half in range(2):
        matrix = jnp.where(
            polar_ref[0] == 1, interp_ref[0, half].astype(F32), interp_ref[1, half].astype(F32)
        )
        at = slice(half * S, (half + 1) * S)
        ms_ref[at, 0:S] = shifted(matrix, -1).astype(BF)
        ms_ref[at, S : 2 * S] = matrix.astype(BF)
        ms_ref[at, 2 * S : 3 * S] = shifted(matrix, 1).astype(BF)
        mt_ref[at, :] = matrix.T.astype(BF)

    slots = jnp.concatenate([slots_ref[...], jnp.full((1, SRC - nsrc), -1, I32)], axis=1)
    for t in range(owners):
        c = iota((chunk, SRC), 0)
        hit = (c + t * capacity == slots) & (c < capacity)
        oh_ref[t * chunk : (t + 1) * chunk, :] = jnp.where(hit, 1.0, 0.0).astype(BF)
        lists[0:1, t * chunk : t * chunk + capacity] = send_ref[t : t + 1, :]
        lists[0:1, t * chunk + capacity : (t + 1) * chunk] = (
            iota((1, CH), 1) + sel_ref.shape[0] - CH
        )
    hit = lists[...] == iota(sel_ref.shape, 0)
    sel_ref[...] = jnp.where(hit, 1.0, 0.0).astype(BF)


def patch_kernel(
    slots_ref,
    rows_ref,
    recv_ref,
    ms_ref,
    t1_ref,
    bcol_ref,
    gh_ref,
    cb_ref,
    w_ref,
    gp_ref,
    src,
    img,
    xb,
    hb,
):
    nsrc = slots_ref.shape[1]
    total = src.shape[0]
    src[0:FREQ, :] = jnp.zeros((FREQ, S), F32)
    first = FREQ * (nsrc + 1)
    src[first:total, :] = jnp.zeros((total - first, S), F32)
    for k in range(nsrc):
        src[FREQ * (k + 1) : FREQ * (k + 2), :] = recv_ref[slots_ref[0, k]].astype(F32)
    limit = FREQ * (rows_ref[0, 0] + 1)
    step = img.shape[1] // 3
    for a in range(0, img.shape[1], step):
        pair = jnp.concatenate([src[a : a + step, :], src[a + FREQ : a + FREQ + step, :]], axis=1)
        out = dot(pair.astype(BF), ms_ref[...])
        at = iota(out.shape, 0) + a
        out = jnp.where((at >= FREQ) & (at < limit), out, 0.0).astype(BF)
        for dx in range(3):
            img[dx, a : a + step, :] = out[:, dx * S : (dx + 1) * S]
    for m in range(NB):
        for dx in range(3):
            xb[dx * XW : (dx + 1) * XW, m * S : (m + 1) * S] = img[
                dx, m * R * FREQ : m * R * FREQ + XW, :
            ]
    xb[3 * XW :, :] = jnp.ones((CH, LANES), BF)
    zero_edges(hb, 0)
    zero_edges(gp_ref, 0)
    bias = jnp.concatenate([bcol_ref[...], bcol_ref[...]], axis=1)
    for n in range(0, LANES, 2 * S):
        pre = dot(t1_ref[...], xb[:, n : n + 2 * S]) + bias
        gate = jax.nn.sigmoid(pre)
        hidden = (pre * gate).astype(BF)
        grad = (gh_ref[:, n : n + 2 * S] * (gate * (1.0 + pre * (1.0 - gate)))).astype(BF)
        for b in range(2):
            m = n // S + b
            lanes = slice(b * S, (b + 1) * S)
            for ref, value in ((hb, hidden), (gp_ref, grad)):
                ref[CH : CH + R * CH, m * S : (m + 1) * S] = value[:, lanes]
                if m > 0:
                    ref[(R + 1) * CH : WIN, (m - 1) * S : m * S] = value[0:CH, lanes]
                if m < NB - 1:
                    ref[0:CH, (m + 1) * S : (m + 2) * S] = value[(R - 1) * CH :, lanes]
    lane = iota((CH, 2 * S), 1)
    result = jnp.zeros((CH, 2 * S), F32)
    for dx in range(3):
        g = dot_t(cb_ref[dx * WIN + CH : dx * WIN + CH + R * CH, :], hb[...])
        g = jnp.concatenate([g, jnp.zeros((R * CH, 2 * S - WIN), F32)], axis=1)
        acc = g[0:CH, :]
        for r in range(1, R):
            acc = acc + pltpu.roll(g[r * CH : (r + 1) * CH, :], 2 * S - r * CH, 1)
        if dx:
            acc = pltpu.roll(acc, dx * 3 * CH, 1)
        result = jnp.where((lane >= dx * 3 * CH) & (lane < (dx + 1) * 3 * CH), acc, result)
    g = dot_t(gp_ref[CH : CH + R * CH, :], xb[...])
    g = jnp.concatenate([g, jnp.zeros((R * CH, 2 * S - g.shape[1]), F32)], axis=1)
    acc = g[0:CH, :]
    ones = g[0:CH, :]
    for r in range(1, R):
        part = g[r * CH : (r + 1) * CH, :]
        ones = ones + part
        acc = acc + pltpu.roll(part, 2 * S - r * FREQ, 1)
    acc = pltpu.roll(acc, 9 * CH, 1)
    ones = pltpu.roll(ones, 2 * S - 1 - 3 * XW, 1)
    result = jnp.where(lane >= 9 * CH, acc, result)
    w_ref[...] = jnp.where(lane == 2 * S - 1, ones, result)


def slots_kernel(rows_ref, gp_ref, t3_ref, mt_ref, oh_ref, out_ref, grad, gsrc):
    part = R * FREQ
    limit = rows_ref[0, 0]
    pad = 2 * FREQ
    grad[0:pad, :] = jnp.zeros((pad, S), F32)
    end = pad + S * FREQ
    grad[end:, :] = jnp.zeros((grad.shape[0] - end, S), F32)
    for n in range(0, LANES, 4 * S):
        u = dot(t3_ref[...], gp_ref[:, n : n + 4 * S])
        for b in range(4):
            m = n // S + b
            lanes = slice(b * S, (b + 1) * S)
            rows = shifted(u[0:part, lanes], 1) + u[part : 2 * part, lanes]
            rows = rows + shifted(u[2 * part : 3 * part, lanes], -1)
            y = (iota(rows.shape, 0) >> 2) + m * R
            grad[pad + m * part : pad + (m + 1) * part, :] = jnp.where(y < limit, rows, 0.0)
    step = 176
    for a in range(0, 3 * step, step):
        pair = jnp.concatenate(
            [grad[pad + a : pad + a + step, :], grad[FREQ + a : FREQ + a + step, :]], axis=1
        )
        gsrc[a : a + step, :] = dot(pair.astype(BF), mt_ref[...])
    gsrc[3 * step :, :] = jnp.zeros((gsrc.shape[0] - 3 * step, S), F32)
    for f in range(FREQ):
        rows = gsrc[pl.ds(f, SRC, stride=FREQ), :]
        high = rows.astype(BF)
        low = (rows - high.astype(F32)).astype(BF)
        out = dot(oh_ref[...], high) + dot(oh_ref[...], low)
        out_ref[:, f * S : (f + 1) * S] = out.astype(BF)


def pack_kernel(w_ref, buffer_ref, out_ref, packed, sems):
    del buffer_ref
    owners, chunk, _ = out_ref.shape
    total = w_ref[...]
    high = total.astype(BF)
    packed[:, 0 : 2 * S] = high
    packed[:, 2 * S : 4 * S] = (total - high.astype(F32)).astype(BF)
    copies = [
        pltpu.make_async_copy(packed, out_ref.at[t, pl.ds(chunk - CH, CH), :], sems.at[t])
        for t in range(owners)
    ]
    for copy in copies:
        copy.start()
    for copy in copies:
        copy.wait()


def final_kernel(scale, sel_ref, back_ref, map_ref, w_ref):
    blocks = map_ref.shape[0]
    total = dot(sel_ref[...], back_ref[...])
    for f in range(FREQ):
        map_ref[:, f, :] = total[0:blocks, f * S : (f + 1) * S]
    w_ref[...] = (total[blocks:, 0 : 2 * S] + total[blocks:, 2 * S : 4 * S]) * scale


def vmem(n):
    return [pl.BlockSpec(memory_space=pltpu.VMEM)] * n


def smem(n):
    return [pl.BlockSpec(memory_space=pltpu.SMEM)] * n


def call(kernel, out_shape, in_specs, out_specs, scratch=(), **extra):
    return pl.pallas_call(
        kernel,
        out_shape=out_shape,
        in_specs=in_specs,
        out_specs=out_specs,
        scratch_shapes=list(scratch),
        compiler_params=pltpu.CompilerParams(vmem_limit_bytes=VMEM_LIMIT),
        **extra,
    )


def arr(shape, dtype):
    return jax.ShapeDtypeStruct(shape, dtype)


def band_sum(value, count):
    if count & (count - 1):
        return lax.psum(value, "band")
    step = 1
    while step < count:
        pairs = [(i, i ^ step) for i in range(count)]
        value = value + lax.ppermute(value, "band", pairs)
        step *= 2
    return value


def shards(
    pixel_map,
    interp_bands,
    conv1_weight,
    conv1_bias,
    conv2_weight,
    send_rows,
    patch_slots,
    patch_rows,
    cotangent,
):
    tile_count = lax.axis_size("tile")
    band_count = lax.axis_size("band")
    band_index = lax.axis_index("band")
    owned = pixel_map[0]
    blocks = owned.shape[0]
    send = send_rows[0, 0]
    capacity = send.shape[1]
    chunk = capacity + CH
    slots = patch_slots[0]
    cot = cotangent.reshape(CH * S, S)

    outgoing = call(
        outgoing_kernel,
        arr((tile_count * capacity, FREQ, S), BF),
        smem(1) + vmem(1),
        vmem(1)[0],
    )(send, owned)
    received = lax.all_to_all(outgoing, "tile", split_axis=0, concat_axis=0, tiled=True)

    is_polar = jnp.logical_or(
        band_index < band_count // 4, band_index >= band_count - band_count // 4
    )
    polar = is_polar.astype(I32).reshape(1)
    w1 = conv1_weight.reshape(CH, FREQ * 9)
    w1t = jnp.transpose(conv1_weight, (1, 0, 2, 3)).reshape(FREQ, CH * 9)
    w2t = jnp.transpose(conv2_weight, (1, 0, 2, 3)).reshape(CH, CH * 9)
    cb, gh, t1, bcol, t3, ms, mt, oh, sel = call(
        prepare_kernel,
        (
            arr((3 * WIN, LANES), BF),
            arr((R * CH, LANES), F32),
            arr((R * CH, 3 * XW + CH), BF),
            arr((R * CH, S), F32),
            arr((3 * R * FREQ, WIN), BF),
            arr((2 * S, 3 * S), BF),
            arr((2 * S, S), BF),
            arr((tile_count * chunk, SRC), BF),
            arr((blocks + CH, tile_count * chunk), BF),
        ),
        smem(1) + vmem(8),
        vmem(9),
        (
            pltpu.VMEM((CH * S, S), F32),
            pltpu.VMEM((1, tile_count * chunk), I32),
            pltpu.VMEM((R * CH, 3 * WIN), BF),
        ),
        cost_estimate=pl.CostEstimate(flops=4 * 10**9, bytes_accessed=4 * 10**6, transcendentals=0),
    )(polar, cot, w1, w1t, w2t, conv1_bias.reshape(1, CH), interp_bands, slots, send)

    padded = (S + 4) * FREQ
    weights, gp = call(
        patch_kernel,
        (arr((CH, 2 * S), F32), arr((WIN, LANES), BF)),
        smem(2) + vmem(6),
        vmem(2),
        (
            pltpu.VMEM((padded + 8, S), F32),
            pltpu.VMEM((3, padded, S), BF),
            pltpu.VMEM((3 * XW + CH, LANES), BF),
            pltpu.VMEM((WIN, LANES), BF),
        ),
    )(slots, patch_rows, received, ms, t1, bcol, gh, cb)

    returning = call(
        slots_kernel,
        arr((tile_count * chunk, 4 * S), BF),
        smem(1) + vmem(4),
        vmem(1)[0],
        (pltpu.VMEM((padded + 16, S), F32), pltpu.VMEM((SRC * FREQ, S), F32)),
    )(patch_rows, gp, t3, mt, oh)
    weights = band_sum(weights, band_count)
    returning = call(
        pack_kernel,
        arr((tile_count, chunk, 4 * S), BF),
        vmem(1) + [pl.BlockSpec(memory_space=pl.ANY)],
        pl.BlockSpec(memory_space=pl.ANY),
        (pltpu.VMEM((CH, 4 * S), BF), pltpu.SemaphoreType.DMA((tile_count,))),
        input_output_aliases={1: 0},
    )(weights, returning.reshape(tile_count, chunk, 4 * S))
    returned = lax.all_to_all(returning, "tile", split_axis=0, concat_axis=0, tiled=True)
    norm_scale = float(band_count * tile_count * S * S) ** (-0.5)
    grad_map, total = call(
        functools.partial(final_kernel, norm_scale),
        (arr((blocks, FREQ, S), F32), arr((CH, 2 * S), F32)),
        vmem(2),
        vmem(2),
    )(sel, returned.reshape(tile_count * chunk, 4 * S))

    grad2 = total[:, 0 : 9 * CH].reshape(CH, 3, 3, CH)
    grad1 = jnp.stack([total[:, 9 * CH + dx * XW :][:, 0 : 3 * FREQ] for dx in range(3)], axis=1)
    grad1 = grad1.reshape(CH, 3, 3, FREQ)
    return (
        grad_map[None],
        jnp.transpose(grad1, (0, 3, 2, 1)),
        total[:, 2 * S - 1],
        jnp.transpose(grad2, (0, 3, 2, 1)),
    )


def solution(mesh):
    in_specs = (
        P("band", "tile", None, None),
        P(),
        P(),
        P(),
        P(),
        P("band", "tile", None, None),
        P("band", "tile", None),
        P("band", "tile"),
        P("band", "tile", None, None, None),
    )
    out_specs = (P("band", "tile", None, None), P(), P(), P())
    return jax.shard_map(shards, mesh=mesh, in_specs=in_specs, out_specs=out_specs, check_vma=False)
```

time: 297 us -> 50.9 us (0.17); the launches traced: 292 us -> 50.2 us
  matrix products: 167 us -> 0 us
  other arithmetic: 31.8 us -> 0.02 us
  blocking collectives: 42.3 us -> 12.3 us
  local copies, waits for them, and re-layouts: 38.8 us -> 16.2 us
  Pallas kernels: 0 us -> 7.8 us
  waiting for transfers between devices: 0.01 us -> 3.14 us
    transpose x3 -> x0, matrix products: 149 us -> none  [the longest x1 118 us: patch_grads(): grad_rows = jnp.transpose(grad_image, (0, 2, 1, 3))]
    psum x1 -> x0, blocking collectives: 42.3 us -> none  [shards(): lax.psum((grad_w1 * norm_scale, grad_b1 * norm_scale, grad_w2 * norm_scal...]
    conv_general_dilated x2 -> x0, matrix products: 17.1 us -> none  [conv_same(): lax.conv_general_dilated(images, kernel, (1, 1), ((1, 1), (1, 1)), dimens...]
    convert_element_type x5 -> x0, other arithmetic: 14.8 us -> none  [the longest x3 10.7 us: patch_grads(): hidden = (pre_act * gating).astype(jnp.bfloat16)]
    scatter-add x1 -> x0, other arithmetic: 14.4 us -> none  [shards(): jax.ops.segment_sum(flat_grads, slot_ids.reshape(-1), num_segments=tile_c...]
    all_to_all x0 -> x1, blocking collectives: none -> 12.3 us  [shards(): lax.all_to_all(returning, 'tile', split_axis=0, concat_axis=0, tiled=True)]
    convert_element_type x9 -> x0, local copies, waits for them, and re-layouts: 8.27 us -> none  [the longest x2 4.51 us: patch_grads(): hidden = (pre_act * gating).astype(jnp.bfloat16)]
    pallas_call x0 -> x6, Pallas kernels: none -> 7.8 us  [the longest x1 2.29 us: shards(): call(patch_kernel, (arr((CH, 2 * S), F32), arr((WIN, LANES), BF)), smem(2...]
  transfers between devices with their start and end apart: 2 -> 3, of which waited for: 0 -> 2; matrix products, arithmetic and copies ran while one was open for 23% -> 5% of each run, Pallas kernels for 0% -> 6%
where the time goes in v1:
time: 50.9 us; the launch traced here: 50.2 us
  local copies, waits for them, and re-layouts  16.2 us (32%)
  blocking collectives  12.3 us (24%)
  starting transfers between devices  9.39 us (18%)
  Pallas kernels  7.8 us (15%)
  waiting for transfers between devices  3.14 us (6%)
  between operations  1.39 us (3%)
    unnamed x39, local copies, waits for them, and re-layouts  13 us
    all_to_all x1, blocking collectives, shards(): lax.all_to_all(returning, 'tile', split_axis=0, concat_axis=0, tiled=True)  12.3 us
    all_to_all x1, starting transfers between devices, shards(): lax.all_to_all(outgoing, 'tile', split_axis=0, concat_axis=0, tiled=True)  5.17 us
    ppermute x2, starting transfers between devices, band_sum(): value = value + lax.ppermute(value, 'band', pairs)  4.22 us
    ppermute x2, waiting for transfers between devices, band_sum(): value = value + lax.ppermute(value, 'band', pairs)  3.14 us
    pallas_call x1, Pallas kernels, shards(): call(patch_kernel, (arr((CH, 2 * S), F32), arr((WIN, LANES), BF)), smem(2...  2.29 us
    pallas_call x1, Pallas kernels, shards(): call(prepare_kernel, (arr((3 * WIN, LANES), BF), arr((R * CH, LANES), F32...  1.79 us
    pallas_call x1, Pallas kernels, shards(): call(outgoing_kernel, arr((tile_count * capacity, FREQ, S), BF), smem(1)...  1.5 us
  transfers between devices with their start and end apart: 3, of which 2 were waited for; matrix products, arithmetic and copies ran while one was open for 5% of the time, Pallas kernels for 6%

profile of v1, /device:TPU:0, one launch (start us, length us, event | category | flops | bytes accessed | tf_op | source)
XLA Modules:
  0.0 50.2 jit_solution(13307302907130511309)
XLA Ops:
  0.6 0.0 copy-start.8
  0.6 0.8 %copy-done.8 = bf16[1,48,4,128]{3,2,1,0:T(4,128)(2,1)S(1)} copy-done((bf16[1,48,4,128]{3,2,1,0:T(4,128)(2,1)S(1)}, bf16[1,48,4,128]{3,2,1,0:T(4,128)(2,1)}, u32[]{:S(2)}) %copy-start.8) | copy-done | bytes 49176
  1.4 0.0 copy-start.11
  1.4 0.7 %copy-done.11 = s32[1,1,8,32]{3,2,1,0:T(8,128)S(1)} copy-done((s32[1,1,8,32]{3,2,1,0:T(8,128)S(1)}, s32[1,1,8,32]{3,2,1,0:T(8,128)}, u32[]{:S(2)}) %copy-start.11) | copy-done | bytes 1048
  2.1 1.5 %shard_map.121 = bf16[256,4,128]{2,1,0:T(4,128)(2,1)} custom-call(s32[8,32]{1,0:T(8,128)S(1)} %bitcast.29, bf16[48,4,128]{2,1,0:T(4,128)(2,1)S(1)} %bitcast.28), custom_call_target="tpu_custom_call" | custom-call | tf_op jit(solution)/shard_map/pallas_call | solution.py:371
  3.6 5.2 %all-to-all-start = ((bf16[256,4,128]{2,1,0:T(4,128)(2,1)}), bf16[256,4,128]{2,1,0:T(4,128)(2,1)S(1)}, u32[]{:S(2)}, u32[]{:S(2)}) async-start(bf16[256,4,128]{2,1,0:T(4,128)(2,1)} %shard_map.121), calls=%async_computation | async-start | bytes 524288 | tf_op jit(solution)/shard_map/all_to_all | solution.py:377
  9.4 0.7 %copy.21 = bf16[16,4,3,3]{0,3,2,1:T(4,128)(2,1)S(1)} copy(bf16[16,4,3,3]{0,1,3,2:T(4,128)(2,1)} %param.11) | data formatting | bytes 2304 | tf_op args[2]
  10.2 0.1 copy.24.w1_ref
  10.3 0.8 %copy.23 = bf16[16,16,3,3]{0,3,2,1:T(4,128)(2,1)S(1)} copy(bf16[16,16,3,3]{0,1,3,2:T(8,128)(2,1)} %bitcast.37) | data formatting | bytes 9216 | tf_op jit(solution)/shard_map/transpose | solution.py:385
  11.1 0.1 copy.25.w2t_ref
  11.2 0.9 %copy.22 = bf16[4,16,3,3]{3,2,1,0:T(4,128)(2,1)S(1)} copy(bf16[4,16,3,3]{1,0,3,2:T(4,128)(2,1)} %bitcast.36) | data formatting | bytes 2304 | tf_op jit(solution)/shard_map/transpose | solution.py:384
  12.0 0.1 reshape.48.w1t_ref
  12.2 0.0 copy-start.12
  12.2 0.7 %copy-done.12 = s32[1,1,8,32]{3,2,1,0:T(8,128)S(1)} copy-done((s32[1,1,8,32]{3,2,1,0:T(8,128)S(1)}, s32[1,1,8,32]{3,2,1,0:T(8,128)}, u32[]{:S(2)}) %copy-start.12) | copy-done | bytes 1048
  12.9 0.0 copy-start.13
  12.9 0.7 %copy-done.13 = s32[1,1,129]{2,1,0:T(1,128)S(1)} copy-done((s32[1,1,129]{2,1,0:T(1,128)S(1)}, s32[1,1,129]{2,1,0:T(1,128)}, u32[]{:S(2)}) %copy-start.13) | copy-done | bytes 540
  13.5 0.0 copy-start.15
  13.5 1.0 %copy-done.15 = bf16[1,1,16,128,128]{4,3,2,1,0:T(8,128)(2,1)S(1)} copy-done((bf16[1,1,16,128,128]{4,3,2,1,0:T(8,128)(2,1)S(1)}, bf16[1,1,16,128,128]{4,3,2,1,0:T(8,128)(2,1)}, u32[]{:S(2)}) %copy-start.15) | copy-done | bytes 524312
  14.6 0.0 copy-start.16
  14.6 0.9 %copy-done.16 = bf16[2,2,128,128]{3,2,1,0:T(8,128)(2,1)S(1)} copy-done((bf16[2,2,128,128]{3,2,1,0:T(8,128)(2,1)S(1)}, bf16[2,2,128,128]{3,2,1,0:T(8,128)(2,1)}, u32[]{:S(2)}) %copy-start.16) | copy-done | bytes 131096
  15.5 0.0 copy-start.17
  15.5 0.7 %copy-done.17 = f32[16]{0:T(128)S(1)} copy-done((f32[16]{0:T(128)S(1)}, f32[16]{0:T(128)}, u32[]{:S(2)}) %copy-start.17) | copy-done | bytes 88
  16.1 1.8 %shard_map.120 = (bf16[480,2048]{1,0:T(8,128)(2,1)S(1)}, f32[128,2048]{1,0:T(8,128)S(1)}, bf16[128,160]{1,0:T(8,128)(2,1)S(1)}, f32[128,128]{1,0:T(8,128)S(1)}, ...) custom-call(s32[1]{0:T(128)} %bitcast.polar_ref, ...), custom_call_target="tpu_custom_call" | custom-call | flops 4000000000 | bytes 4000000 | tf_op jit(solution)/shard_map/pallas_call | solution.py:386
  17.9 0.0 copy-start
  18.0 0.7 %copy-done = bf16[256,384]{1,0:T(8,128)(2,1)} copy-done((bf16[256,384]{1,0:T(8,128)(2,1)}, bf16[256,384]{1,0:T(8,128)(2,1)S(1)}, u32[]{:S(2)}) %copy-start) | copy-done | bytes 196632
  18.6 0.0 copy-start.2
  18.6 0.6 %copy-done.2 = f32[128,128]{1,0:T(8,128)} copy-done((f32[128,128]{1,0:T(8,128)}, f32[128,128]{1,0:T(8,128)S(1)}, u32[]{:S(2)}) %copy-start.2) | copy-done | bytes 65560
  19.2 0.0 copy-start.4
  19.3 0.6 %copy-done.4 = bf16[256,128]{1,0:T(8,128)(2,1)} copy-done((bf16[256,128]{1,0:T(8,128)(2,1)}, bf16[256,128]{1,0:T(8,128)(2,1)S(1)}, u32[]{:S(2)}) %copy-start.4) | copy-done | bytes 65560
  19.9 0.0 copy-start.6
  19.9 0.6 %copy-done.6 = bf16[96,160]{1,0:T(8,128)(2,1)} copy-done((bf16[96,160]{1,0:T(8,128)(2,1)}, bf16[96,160]{1,0:T(8,128)(2,1)S(1)}, u32[]{:S(2)}) %copy-start.6) | copy-done | bytes 30744
  20.5 0.0 copy-start.9
  20.5 0.6 %copy-done.9 = bf16[64,384]{1,0:T(8,128)(2,1)} copy-done((bf16[64,384]{1,0:T(8,128)(2,1)}, bf16[64,384]{1,0:T(8,128)(2,1)S(1)}, u32[]{:S(2)}) %copy-start.9) | copy-done | bytes 49176
  21.1 0.0 all-to-all-done.recv_ref
  21.1 0.0 copy-start.1
  21.1 0.9 %copy-done.1 = bf16[256,384]{1,0:T(8,128)(2,1)S(1)} copy-done((bf16[256,384]{1,0:T(8,128)(2,1)S(1)}, bf16[256,384]{1,0:T(8,128)(2,1)}, u32[]{:S(2)}) %copy-start.1) | copy-done | bytes 196632
  22.0 0.0 copy-start.3
  22.0 0.8 %copy-done.3 = f32[128,128]{1,0:T(8,128)S(1)} copy-done((f32[128,128]{1,0:T(8,128)S(1)}, f32[128,128]{1,0:T(8,128)}, u32[]{:S(2)}) %copy-start.3) | copy-done | bytes 65560
  22.9 0.0 copy-start.14
  22.9 0.7 %copy-done.14 = s32[1,1,129]{2,1,0:T(1,128)S(1)} copy-done((s32[1,1,129]{2,1,0:T(1,128)S(1)}, s32[1,1,129]{2,1,0:T(1,128)}, u32[]{:S(2)}) %copy-start.14) | copy-done | bytes 540
  23.6 0.0 copy-start.5
  23.6 0.0 copy-start.7
  23.6 2.3 %shard_map.122 = (f32[16,256]{1,0:T(8,128)S(1)}, bf16[160,2048]{1,0:T(8,128)(2,1)S(1)}) custom-call(s32[1,129]{1,0:T(1,128)S(1)} %bitcast.32, s32[1,1]{1,0:T(1,128)S(6)} %copy.32.rows_ref, bf16[256,4,128]{2,1,0:T(4,128)(2,1)S(1)} %all-to-all-done.recv_ref, bf16[256,384]{1,0:T(8,128)(2,1)S(1)} %copy-done.1, bf16[128,160]{1,0:T(8,128)(2,1)S(1)} %get-tuple-element.19.t1_ref, ...), custom_call_target="tpu_custom_call" | custom-call | tf_op jit(solution)/shard_map/pallas_call | solution.py:410
  25.9 0.0 copy-start.10
  25.9 1.6 %collective-permute-start = (f32[16,256]{1,0:T(8,128)S(1)}, f32[16,256]{1,0:T(8,128)S(1)}, u32[]{:S(2)}, u32[]{:S(2)}) collective-permute-start(f32[16,256]{1,0:T(8,128)S(1)} %get-tuple-element.23), channel_id=1, source_target_pairs={{0,8},{8,0},{16,24},{24,16},{1,9},{9,1},{17,25},{25,17},{2,10},{10... | collective-permute-start | bytes 49160 | tf_op jit(solution)/shard_map/ppermute | solution.py:344
  27.5 2.2 %collective-permute-done = f32[16,256]{1,0:T(8,128)S(1)} collective-permute-done((f32[16,256]{1,0:T(8,128)S(1)}, f32[16,256]{1,0:T(8,128)S(1)}, u32[]{:S(2)}, u32[]{:S(2)}) %collective-permute-start) | collective-permute-done | bytes 16416 | tf_op jit(solution)/shard_map/ppermute | solution.py:344
  29.7 2.6 %collective-permute-start.1 = (f32[16,256]{1,0:T(8,128)S(1)}, f32[16,256]{1,0:T(8,128)S(1)}, u32[]{:S(2)}, u32[]{:S(2)}) collective-permute-start(f32[16,256]{1,0:T(8,128)S(1)} %add.6), channel_id=1, source_target_pairs={{0,16},{8,24},{16,0},{24,8},{1,17},{9,25},{17,1},{25,9},{2,18},{10... | collective-permute-start | bytes 49160 | tf_op jit(solution)/shard_map/ppermute | solution.py:344
  32.3 0.0 copy-done.5
  32.3 0.0 copy-done.7
  32.3 1.1 %shard_map.123 = bf16[384,512]{1,0:T(8,128)(2,1)S(1)} custom-call(s32[1,1]{1,0:T(1,128)S(6)} %copy.32.rows_ref, bf16[160,2048]{1,0:T(8,128)(2,1)S(1)} %get-tuple-element.24.gp_ref, bf16[96,160]{1,0:T(8,128)(2,1)S(1)} %copy-done.7, bf16[256,128]{1,0:T(8,128)(2,1)S(1)} %copy-done.5, bf16[384,144]{1,0:T(8,128)(2,1)S(1)} %get-tuple-element.27.oh_ref), custom_call_target="tpu_custom_call" | custom-call | tf_op jit(solution)/shard_map/pallas_call | solution.py:423
  33.4 1.0 %collective-permute-done.1 = f32[16,256]{1,0:T(8,128)S(1)} collective-permute-done((f32[16,256]{1,0:T(8,128)S(1)}, f32[16,256]{1,0:T(8,128)S(1)}, u32[]{:S(2)}, u32[]{:S(2)}) %collective-permute-start.1) | collective-permute-done | bytes 16416 | tf_op jit(solution)/shard_map/ppermute | solution.py:344
  34.3 0.3 shard_map.124
  34.6 12.3 %all_to_all.10 = bf16[8,48,512]{2,1,0:T(8,128)(2,1)S(1)} all-to-all(bf16[8,48,512]{2,1,0:T(8,128)(2,1)S(1)} %shard_map.124), channel_id=1, replica_groups=mesh['band'=4,'tile'=8] {'tile'}, dimensions={0} | all-to-all | bytes 786432 | tf_op jit(solution)/shard_map/all_to_all | solution.py:439
  46.9 0.0 copy-done.10
  46.9 0.9 %shard_map.125 = (f32[48,4,128]{2,1,0:T(4,128)}, f32[16,256]{1,0:T(8,128)S(1)}) custom-call(bf16[64,384]{1,0:T(8,128)(2,1)S(1)} %copy-done.10, bf16[384,512]{1,0:T(8,128)(2,1)S(1)} %bitcast.26), custom_call_target="tpu_custom_call" | custom-call | tf_op jit(solution)/shard_map/pallas_call | solution.py:441
  47.8 0.7 %slice_reduce_fusion = f32[16]{0:T(128)} fusion(f32[16,256]{1,0:T(8,128)S(1)} %get-tuple-element.29), kind=kLoop, calls=%fused_computation.1 | loop fusion | bytes 128 | tf_op jit(solution)/shard_map/slice | solution.py:454
  48.5 0.1 fusion
  48.6 0.1 copy.26
  48.7 0.1 copy.28
  48.8 0.1 copy.27
  48.9 0.6 %copy.29 = f32[16,4,3,3]{0,1,3,2:T(4,128)} copy(f32[16,4,3,3]{0,1,2,3:T(4,128)S(1)} %maximum_bitcast_fusion) | data formatting | bytes 4608
  49.5 0.1 reshape.53
  49.6 0.6 %copy.30 = f32[16,16,3,3]{1,0,3,2:T(8,128)} copy(f32[16,16,3,3]{1,2,3,0:T(4,128)S(1)} %bitcast.35) | data formatting | bytes 18432
  (8 shorter events, 0.1 us)
Async XLA Ops:
  0.6 0.8 %copy-start.8 = (bf16[1,48,4,128]{3,2,1,0:T(4,128)(2,1)S(1)}, bf16[1,48,4,128]{3,2,1,0:T(4,128)(2,1)}, u32[]{:S(2)}) copy-start(bf16[1,48,4,128]{3,2,1,0:T(4,128)(2,1)} %param.9) | copy-start | bytes 147460
  1.4 0.7 %copy-start.11 = (s32[1,1,8,32]{3,2,1,0:T(8,128)S(1)}, s32[1,1,8,32]{3,2,1,0:T(8,128)}, u32[]{:S(2)}) copy-start(s32[1,1,8,32]{3,2,1,0:T(8,128)} %param.14) | copy-start | bytes 3076
  3.6 17.5 %all-to-all-start = ((bf16[256,4,128]{2,1,0:T(4,128)(2,1)}), bf16[256,4,128]{2,1,0:T(4,128)(2,1)S(1)}, u32[]{:S(2)}, u32[]{:S(2)}) async-start(bf16[256,4,128]{2,1,0:T(4,128)(2,1)} %shard_map.121), calls=%async_computation | async-start | bytes 524288 | tf_op jit(solution)/shard_map/all_to_all | solution.py:377
  12.2 0.7 %copy-start.12 = (s32[1,1,8,32]{3,2,1,0:T(8,128)S(1)}, s32[1,1,8,32]{3,2,1,0:T(8,128)}, u32[]{:S(2)}) copy-start(s32[1,1,8,32]{3,2,1,0:T(8,128)} %param.14) | copy-start | bytes 3076
  12.9 0.7 %copy-start.13 = (s32[1,1,129]{2,1,0:T(1,128)S(1)}, s32[1,1,129]{2,1,0:T(1,128)}, u32[]{:S(2)}) copy-start(s32[1,1,129]{2,1,0:T(1,128)} %param.15) | copy-start | bytes 1552
  13.5 1.0 %copy-start.15 = (bf16[1,1,16,128,128]{4,3,2,1,0:T(8,128)(2,1)S(1)}, bf16[1,1,16,128,128]{4,3,2,1,0:T(8,128)(2,1)}, u32[]{:S(2)}) copy-start(bf16[1,1,16,128,128]{4,3,2,1,0:T(8,128)(2,1)} %param.17) | copy-start | bytes 1572868
  14.6 0.9 %copy-start.16 = (bf16[2,2,128,128]{3,2,1,0:T(8,128)(2,1)S(1)}, bf16[2,2,128,128]{3,2,1,0:T(8,128)(2,1)}, u32[]{:S(2)}) copy-start(bf16[2,2,128,128]{3,2,1,0:T(8,128)(2,1)} %interp_ref.1) | copy-start | bytes 393220
  15.5 0.7 %copy-start.17 = (f32[16]{0:T(128)S(1)}, f32[16]{0:T(128)}, u32[]{:S(2)}) copy-start(f32[16]{0:T(128)} %param.12) | copy-start | bytes 196
  17.9 0.7 %copy-start = (bf16[256,384]{1,0:T(8,128)(2,1)}, bf16[256,384]{1,0:T(8,128)(2,1)S(1)}, u32[]{:S(2)}) copy-start(bf16[256,384]{1,0:T(8,128)(2,1)S(1)} %get-tuple-element.18.ms_ref) | copy-start | bytes 589828
  18.6 0.6 %copy-start.2 = (f32[128,128]{1,0:T(8,128)}, f32[128,128]{1,0:T(8,128)S(1)}, u32[]{:S(2)}) copy-start(f32[128,128]{1,0:T(8,128)S(1)} %get-tuple-element.20.bcol_ref) | copy-start | bytes 196612
  19.2 0.6 %copy-start.4 = (bf16[256,128]{1,0:T(8,128)(2,1)}, bf16[256,128]{1,0:T(8,128)(2,1)S(1)}, u32[]{:S(2)}) copy-start(bf16[256,128]{1,0:T(8,128)(2,1)S(1)} %get-tuple-element.26.mt_ref) | copy-start | bytes 196612
  19.9 0.6 %copy-start.6 = (bf16[96,160]{1,0:T(8,128)(2,1)}, bf16[96,160]{1,0:T(8,128)(2,1)S(1)}, u32[]{:S(2)}) copy-start(bf16[96,160]{1,0:T(8,128)(2,1)S(1)} %get-tuple-element.25.t3_ref) | copy-start | bytes 92164
  20.5 0.6 %copy-start.9 = (bf16[64,384]{1,0:T(8,128)(2,1)}, bf16[64,384]{1,0:T(8,128)(2,1)S(1)}, u32[]{:S(2)}) copy-start(bf16[64,384]{1,0:T(8,128)(2,1)S(1)} %get-tuple-element.17.sel_ref) | copy-start | bytes 147460
  21.1 0.9 %copy-start.1 = (bf16[256,384]{1,0:T(8,128)(2,1)S(1)}, bf16[256,384]{1,0:T(8,128)(2,1)}, u32[]{:S(2)}) copy-start(bf16[256,384]{1,0:T(8,128)(2,1)} %copy-done) | copy-start | bytes 589828
  22.0 0.8 %copy-start.3 = (f32[128,128]{1,0:T(8,128)S(1)}, f32[128,128]{1,0:T(8,128)}, u32[]{:S(2)}) copy-start(f32[128,128]{1,0:T(8,128)} %copy-done.2) | copy-start | bytes 196612
  22.9 0.7 %copy-start.14 = (s32[1,1,129]{2,1,0:T(1,128)S(1)}, s32[1,1,129]{2,1,0:T(1,128)}, u32[]{:S(2)}) copy-start(s32[1,1,129]{2,1,0:T(1,128)} %param.15) | copy-start | bytes 1552
  23.6 8.7 %copy-start.5 = (bf16[256,128]{1,0:T(8,128)(2,1)S(1)}, bf16[256,128]{1,0:T(8,128)(2,1)}, u32[]{:S(2)}) copy-start(bf16[256,128]{1,0:T(8,128)(2,1)} %copy-done.4) | copy-start | bytes 196612
  23.6 8.7 %copy-start.7 = (bf16[96,160]{1,0:T(8,128)(2,1)S(1)}, bf16[96,160]{1,0:T(8,128)(2,1)}, u32[]{:S(2)}) copy-start(bf16[96,160]{1,0:T(8,128)(2,1)} %copy-done.6) | copy-start | bytes 92164
  25.9 21.1 %copy-start.10 = (bf16[64,384]{1,0:T(8,128)(2,1)S(1)}, bf16[64,384]{1,0:T(8,128)(2,1)}, u32[]{:S(2)}) copy-start(bf16[64,384]{1,0:T(8,128)(2,1)} %copy-done.9) | copy-start | bytes 147460
  25.9 3.8 %collective-permute-start = (f32[16,256]{1,0:T(8,128)S(1)}, f32[16,256]{1,0:T(8,128)S(1)}, u32[]{:S(2)}, u32[]{:S(2)}) collective-permute-start(f32[16,256]{1,0:T(8,128)S(1)} %get-tuple-element.23), channel_id=1, source_target_pairs={{0,8},{8,0},{16,24},{24,16},{1,9},{9,1},{17,25},{25,17},{2,10},{10... | collective-permute-start | bytes 49160 | tf_op jit(solution)/shard_map/ppermute | solution.py:344
  29.7 4.6 %collective-permute-start.1 = (f32[16,256]{1,0:T(8,128)S(1)}, f32[16,256]{1,0:T(8,128)S(1)}, u32[]{:S(2)}, u32[]{:S(2)}) collective-permute-start(f32[16,256]{1,0:T(8,128)S(1)} %add.6), channel_id=1, source_target_pairs={{0,16},{8,24},{16,0},{24,8},{1,17},{9,25},{17,1},{25,9},{2,18},{10... | collective-permute-start | bytes 49160 | tf_op jit(solution)/shard_map/ppermute | solution.py:344

commit v2 on v1

--- a/solution.py
+++ b/solution.py
@@ -19,7 +19,7 @@
 XW = 48
 LANES = NB * S
 SRC = 144
-VMEM_LIMIT = 48 * 1024 * 1024
+VMEM_LIMIT = 16 * 1024 * 1024
 
 
 def iota(shape, axis):
@@ -32,10 +32,6 @@
 
 def dot_t(a, b):
     return lax.dot_general(a, b, (((1,), (1,)), ((), ())), preferred_element_type=F32)
-
-
-def third(k):
-    return (k * 171) >> 9
 
 
 def shifted(rows, step):
@@ -60,8 +56,46 @@
     ref[base + (R + 1) * CH : base + WIN, LANES - S : LANES] = zero
 
 
-def outgoing_kernel(rows_ref, map_ref, out_ref):
+class View:
+    def __init__(self, ref, row, rows, lane, lanes):
+        self.ref, self.origin, self.shape = ref, (row, lane), (rows, lanes)
+
+    def place(self, key):
+        key = (slice(None), slice(None)) if key is Ellipsis else key
+        spans = [k.indices(n) for k, n in zip(key, self.shape)]
+        return tuple(slice(o + a, o + b) for o, (a, b, _) in zip(self.origin, spans))
+
+    def __getitem__(self, key):
+        return self.ref[self.place(key)]
+
+    def __setitem__(self, key, value):
+        self.ref[self.place(key)] = value
+
+
+def early(ref):
+    return View(ref, 2 * S, R * CH, LANES, 3 * XW + CH), View(ref, 0, 2 * S, LANES, 3 * S)
+
+
+def late(ref, chunks, blocks):
+    return (
+        View(ref, 0, chunks, 0, SRC),
+        View(ref, 0, 2 * S, 2 * S, S),
+        View(ref, 2 * S, 3 * R * FREQ, 2 * S, WIN),
+        View(ref, 0, blocks + CH, 4 * S, chunks),
+    )
+
+
+def fetch(pairs, sems):
+    copies = [pltpu.make_async_copy(a, b, sems.at[i]) for i, (a, b) in enumerate(pairs)]
+    for copy in copies:
+        copy.start()
+    return copies
+
+
+def outgoing_kernel(send_hbm, map_hbm, out_ref, rows_ref, map_ref, sems):
     owners, capacity = rows_ref.shape
+    for copy in fetch(((send_hbm, rows_ref), (map_hbm, map_ref)), sems):
+        copy.wait()
     for t in range(owners):
         for c in range(capacity):
             out_ref[t * capacity + c] = map_ref[rows_ref[t, c]]
@@ -69,56 +103,46 @@
 
 def prepare_kernel(
     polar_ref,
+    cot_hbm,
+    w1_hbm,
+    w2_hbm,
+    interp_hbm,
+    big_ref,
+    gh_ref,
+    cb_ref,
+    plane,
+    t2_ref,
     cot_ref,
     w1_ref,
-    w1t_ref,
-    w2t_ref,
-    bias_ref,
+    w2_ref,
     interp_ref,
-    slots_ref,
-    send_ref,
-    cb_ref,
-    gh_ref,
-    t1_ref,
-    bcol_ref,
-    t3_ref,
-    ms_ref,
-    mt_ref,
-    oh_ref,
-    sel_ref,
-    plane,
-    lists,
-    t2_ref,
+    stack1,
+    stack2,
+    sems,
 ):
-    owners, capacity = send_ref.shape
-    chunk = capacity + CH
-    nsrc = slots_ref.shape[1]
-    for o in range(CH):
-        plane[o * S : (o + 1) * S, :] = cot_ref[o * S : (o + 1) * S, :].astype(F32)
-    for dx in range(3):
-        zero_edges(cb_ref, dx * WIN)
-    for y in range(S):
-        rows = plane[pl.ds(y, CH, stride=S), :]
-        store_window(cb_ref, 0, y, shifted(rows, 1).astype(BF))
-        store_window(cb_ref, WIN, y, rows.astype(BF))
-        store_window(cb_ref, 2 * WIN, y, shifted(rows, -1).astype(BF))
-
+    copies = fetch(
+        ((w1_hbm, w1_ref), (w2_hbm, w2_ref), (interp_hbm, interp_ref), (cot_hbm, cot_ref)), sems
+    )
+    t1_ref, ms_ref = early(big_ref)
+    for copy in copies[:-1]:
+        copy.wait()
+    for i in range(9):
+        stack1[i * FREQ : (i + 1) * FREQ, :] = w1_ref[i].astype(F32)
+        stack2[i * CH : (i + 1) * CH, :] = w2_ref[i].astype(F32)
     pick = ((iota((R * CH, CH), 0) & 15) == iota((R * CH, CH), 1)).astype(BF)
-    spread = dot(pick, w2t_ref[...]).astype(BF)
+    spread = dot_t(pick, stack2[...].astype(BF)).astype(BF)
     row, col = iota((R * CH, 3 * WIN), 0), iota((R * CH, 3 * WIN), 1)
     gap = ((col - jnp.where(col >= 2 * WIN, 2 * WIN, jnp.where(col >= WIN, WIN, 0))) >> 4) - (row >> 4)
     k, kcol = iota((CH * 9, 3 * WIN), 0), iota((CH * 9, 3 * WIN), 1)
     kdx = jnp.where(kcol >= 2 * WIN, 2, jnp.where(kcol >= WIN, 1, 0))
-    source = (kcol & 15) * 9 + kdx
+    source = kdx * CH + (kcol & 15)
     banded = jnp.zeros((R * CH, 3 * WIN), F32)
     for dy in range(3):
-        term = dot(spread, (k == source + dy * 3).astype(BF))
+        term = dot(spread, (k == source + dy * 3 * CH).astype(BF))
         banded = jnp.where(gap == 2 - dy, term, banded)
     t2_ref[...] = banded.astype(BF)
-    for n in range(0, LANES, 512):
-        gh_ref[:, n : n + 512] = dot(t2_ref[...], cb_ref[:, n : n + 512])
-
-    spread = dot(pick, w1_ref[...]).astype(BF)
+    weights1 = stack1[...].astype(BF)
+    spread = dot_t(pick, weights1).astype(BF)
     width = 3 * XW + CH
     row, col = iota((R * CH, width), 0), iota((R * CH, width), 1)
     cdx = jnp.where(col >= 3 * XW, 3, jnp.where(col >= 2 * XW, 2, jnp.where(col >= XW, 1, 0)))
@@ -126,31 +150,12 @@
     gap = jnp.where(cdx == 3, -1, gap)
     k, kcol = iota((FREQ * 9, width), 0), iota((FREQ * 9, width), 1)
     kdx = jnp.where(kcol >= 3 * XW, 3, jnp.where(kcol >= 2 * XW, 2, jnp.where(kcol >= XW, 1, 0)))
-    source = (kcol & 3) * 9 + kdx
+    source = kdx * FREQ + (kcol & 3)
     banded = jnp.zeros((R * CH, width), F32)
     for dy in range(3):
-        term = dot(spread, (k == source + dy * 3).astype(BF))
+        term = dot(spread, (k == source + dy * 3 * FREQ).astype(BF))
         banded = jnp.where(gap == dy, term, banded)
     t1_ref[...] = banded.astype(BF)
-    where_bias = (iota((R * CH, CH), 0) & 15) == iota((R * CH, CH), 1)
-    column = jnp.sum(jnp.where(where_bias, bias_ref[...], 0.0), axis=1, keepdims=True)
-    bcol_ref[...] = jnp.broadcast_to(column, (R * CH, S))
-
-    part = R * FREQ
-    tall = 3 * part
-    pick = ((iota((tall, FREQ), 0) & 3) == iota((tall, FREQ), 1)).astype(BF)
-    spread = dot(pick, w1t_ref[...])
-    row, k = iota((tall, CH * 9), 0), iota((tall, CH * 9), 1)
-    rdx = jnp.where(row >= 2 * part, 2, jnp.where(row >= part, 1, 0))
-    spread = jnp.where(k - 3 * third(k) == rdx, spread, 0.0).astype(BF)
-    row, col = iota((tall, WIN), 0), iota((tall, WIN), 1)
-    gap = (col >> 4) - ((row & (part - 1)) >> 2)
-    k, kcol = third(iota((CH * 9, WIN), 0)), iota((CH * 9, WIN), 1)
-    banded = jnp.zeros((tall, WIN), F32)
-    for dy in range(3):
-        term = dot(spread, (k == (kcol & 15) * 3 + dy).astype(BF))
-        banded = jnp.where(gap == 2 - dy, term, banded)
-    t3_ref[...] = banded.astype(BF)
 
     for half in range(2):
         matrix = jnp.where(
@@ -160,7 +165,76 @@
         ms_ref[at, 0:S] = shifted(matrix, -1).astype(BF)
         ms_ref[at, S : 2 * S] = matrix.astype(BF)
         ms_ref[at, 2 * S : 3 * S] = shifted(matrix, 1).astype(BF)
-        mt_ref[at, :] = matrix.T.astype(BF)
+
+    copies[-1].wait()
+    for o in range(CH):
+        plane[o * S : (o + 1) * S, :] = cot_ref[o * S : (o + 1) * S, :].astype(F32)
+    for dx in range(3):
+        zero_edges(cb_ref, dx * WIN)
+    for y in range(S):
+        rows = plane[pl.ds(y, CH, stride=S), :]
+        block, r = divmod(y, R)
+        for dx, tile in enumerate((shifted(rows, 1), rows, shifted(rows, -1))):
+            tile = tile.astype(BF)
+            store_window(cb_ref, dx * WIN, y, tile)
+            at = dx * S + r * CH
+            big_ref[at : at + CH, block * S : (block + 1) * S] = tile
+    for n in range(0, LANES, 512):
+        gh_ref[:, n : n + 512] = dot(t2_ref[...], cb_ref[:, n : n + 512])
+
+
+def lists_kernel(
+    blocks,
+    polar_ref,
+    w1_hbm,
+    interp_hbm,
+    slots_hbm,
+    send_hbm,
+    after_hbm,
+    big_ref,
+    lists,
+    w1_ref,
+    interp_ref,
+    slots_ref,
+    send_ref,
+    stack1,
+    sems,
+):
+    del after_hbm
+    pairs = (
+        (w1_hbm, w1_ref),
+        (interp_hbm, interp_ref),
+        (slots_hbm, slots_ref),
+        (send_hbm, send_ref),
+    )
+    for copy in fetch(pairs, sems):
+        copy.wait()
+    owners, capacity = send_ref.shape
+    chunk = capacity + CH
+    nsrc = slots_ref.shape[1]
+    oh_ref, mt_ref, t3_ref, sel_ref = late(big_ref, owners * chunk, blocks)
+    for i in range(9):
+        stack1[i * FREQ : (i + 1) * FREQ, :] = w1_ref[i].astype(F32)
+    weights1 = stack1[...].astype(BF)
+    part = R * FREQ
+    tall = 3 * part
+    row, k = iota((tall, FREQ * 9), 0), iota((tall, FREQ * 9), 1)
+    rdx = jnp.where(row >= 2 * part, 2, jnp.where(row >= part, 1, 0))
+    source = rdx * FREQ + (row & 3)
+    column = ((iota((CH, WIN), 1) & 15) == iota((CH, WIN), 0)).astype(BF)
+    row, col = iota((tall, WIN), 0), iota((tall, WIN), 1)
+    gap = (col >> 4) - ((row & (part - 1)) >> 2)
+    banded = jnp.zeros((tall, WIN), F32)
+    for dy in range(3):
+        spread = dot((k == source + dy * 3 * FREQ).astype(BF), weights1).astype(BF)
+        banded = jnp.where(gap == 2 - dy, dot(spread, column), banded)
+    t3_ref[...] = banded.astype(BF)
+
+    for half in range(2):
+        matrix = jnp.where(
+            polar_ref[0] == 1, interp_ref[0, half].astype(F32), interp_ref[1, half].astype(F32)
+        )
+        mt_ref[half * S : (half + 1) * S, :] = matrix.T.astype(BF)
 
     slots = jnp.concatenate([slots_ref[...], jnp.full((1, SRC - nsrc), -1, I32)], axis=1)
     for t in range(owners):
@@ -169,7 +243,7 @@
         oh_ref[t * chunk : (t + 1) * chunk, :] = jnp.where(hit, 1.0, 0.0).astype(BF)
         lists[0:1, t * chunk : t * chunk + capacity] = send_ref[t : t + 1, :]
         lists[0:1, t * chunk + capacity : (t + 1) * chunk] = (
-            iota((1, CH), 1) + sel_ref.shape[0] - CH
+            iota((1, CH), 1) + blocks
         )
     hit = lists[...] == iota(sel_ref.shape, 0)
     sel_ref[...] = jnp.where(hit, 1.0, 0.0).astype(BF)
@@ -178,12 +252,10 @@
 def patch_kernel(
     slots_ref,
     rows_ref,
+    bias_ref,
     recv_ref,
-    ms_ref,
-    t1_ref,
-    bcol_ref,
+    big_ref,
     gh_ref,
-    cb_ref,
     w_ref,
     gp_ref,
     src,
@@ -193,6 +265,7 @@
 ):
     nsrc = slots_ref.shape[1]
     total = src.shape[0]
+    t1_ref, ms_ref = early(big_ref)
     src[0:FREQ, :] = jnp.zeros((FREQ, S), F32)
     first = FREQ * (nsrc + 1)
     src[first:total, :] = jnp.zeros((total - first, S), F32)
@@ -215,7 +288,8 @@
     xb[3 * XW :, :] = jnp.ones((CH, LANES), BF)
     zero_edges(hb, 0)
     zero_edges(gp_ref, 0)
-    bias = jnp.concatenate([bcol_ref[...], bcol_ref[...]], axis=1)
+    own = (iota((R * CH, CH), 0) & 15) == iota((R * CH, CH), 1)
+    bias = jnp.sum(jnp.where(own, bias_ref[...], 0.0), axis=1, keepdims=True)
     for n in range(0, LANES, 2 * S):
         pre = dot(t1_ref[...], xb[:, n : n + 2 * S]) + bias
         gate = jax.nn.sigmoid(pre)
@@ -233,7 +307,7 @@
     lane = iota((CH, 2 * S), 1)
     result = jnp.zeros((CH, 2 * S), F32)
     for dx in range(3):
-        g = dot_t(cb_ref[dx * WIN + CH : dx * WIN + CH + R * CH, :], hb[...])
+        g = dot_t(big_ref[dx * S : (dx + 1) * S, 0:LANES], hb[...])
         g = jnp.concatenate([g, jnp.zeros((R * CH, 2 * S - WIN), F32)], axis=1)
         acc = g[0:CH, :]
         for r in range(1, R):
@@ -255,7 +329,8 @@
     w_ref[...] = jnp.where(lane == 2 * S - 1, ones, result)
 
 
-def slots_kernel(rows_ref, gp_ref, t3_ref, mt_ref, oh_ref, out_ref, grad, gsrc):
+def slots_kernel(rows_ref, gp_ref, big_ref, out_ref, grad, gsrc):
+    oh_ref, mt_ref, t3_ref, _ = late(big_ref, out_ref.shape[0], 0)
     part = R * FREQ
     limit = rows_ref[0, 0]
     pad = 2 * FREQ
@@ -303,16 +378,31 @@
         copy.wait()
 
 
-def final_kernel(scale, sel_ref, back_ref, map_ref, w_ref):
+def final_kernel(scale, big_ref, back_ref, map_ref, w1_ref, bias_ref, w2_ref):
     blocks = map_ref.shape[0]
+    sel_ref = late(big_ref, back_ref.shape[0], blocks)[-1]
     total = dot(sel_ref[...], back_ref[...])
     for f in range(FREQ):
         map_ref[:, f, :] = total[0:blocks, f * S : (f + 1) * S]
-    w_ref[...] = (total[blocks:, 0 : 2 * S] + total[blocks:, 2 * S : 4 * S]) * scale
+    weights = (total[blocks:, 0 : 2 * S] + total[blocks:, 2 * S : 4 * S]) * scale
+    for dy in range(3):
+        for dx in range(3):
+            at = (dx * 3 + dy) * CH
+            w2_ref[dy * 3 + dx] = weights[:, at : at + CH]
+    flat = jnp.concatenate([weights[:, S:], jnp.zeros((S - CH, S), F32)], axis=0).T
+    for dy in range(3):
+        for dx in range(3):
+            at = 9 * CH - S + dx * XW + dy * FREQ
+            w1_ref[dy * 3 + dx] = flat[at : at + FREQ, 0:CH]
+    bias_ref[...] = flat[S - 1 : S, 0:CH]
 
 
 def vmem(n):
     return [pl.BlockSpec(memory_space=pltpu.VMEM)] * n
+
+
+def hbm(n):
+    return [pl.BlockSpec(memory_space=pl.ANY)] * n
 
 
 def smem(n):
@@ -335,15 +425,25 @@
     return jax.ShapeDtypeStruct(shape, dtype)
 
 
-def band_sum(value, count):
+def in_hbm(*values):
+    return [pltpu.with_memory_space_constraint(value, pltpu.HBM) for value in values]
+
+
+def in_vmem(*values):
+    return [pltpu.with_memory_space_constraint(value, pltpu.VMEM) for value in values]
+
+
+def band_sum(value, count, beside):
     if count & (count - 1):
-        return lax.psum(value, "band")
+        return lax.psum(value, "band"), beside
     step = 1
     while step < count:
         pairs = [(i, i ^ step) for i in range(count)]
         value = value + lax.ppermute(value, "band", pairs)
+        if step == 1:
+            value, beside = lax.optimization_barrier((value, beside))
         step *= 2
-    return value
+    return value, beside
 
 
 def shards(
@@ -371,46 +471,49 @@
     outgoing = call(
         outgoing_kernel,
         arr((tile_count * capacity, FREQ, S), BF),
-        smem(1) + vmem(1),
+        hbm(2),
         vmem(1)[0],
-    )(send, owned)
+        (
+            pltpu.SMEM(send.shape, I32),
+            pltpu.VMEM(owned.shape, BF),
+            pltpu.SemaphoreType.DMA((2,)),
+        ),
+    )(*in_hbm(send, owned))
     received = lax.all_to_all(outgoing, "tile", split_axis=0, concat_axis=0, tiled=True)
 
     is_polar = jnp.logical_or(
         band_index < band_count // 4, band_index >= band_count - band_count // 4
     )
     polar = is_polar.astype(I32).reshape(1)
-    w1 = conv1_weight.reshape(CH, FREQ * 9)
-    w1t = jnp.transpose(conv1_weight, (1, 0, 2, 3)).reshape(FREQ, CH * 9)
-    w2t = jnp.transpose(conv2_weight, (1, 0, 2, 3)).reshape(CH, CH * 9)
-    cb, gh, t1, bcol, t3, ms, mt, oh, sel = call(
+    w1 = jnp.transpose(conv1_weight, (2, 3, 1, 0)).reshape(9, FREQ, CH)
+    w2 = jnp.transpose(conv2_weight, (2, 3, 0, 1)).reshape(9, CH, CH)
+    bias = conv1_bias.reshape(1, CH)
+    cost = pl.CostEstimate(flops=4 * 10**9, bytes_accessed=4 * 10**6, transcendentals=0)
+    big, gh = call(
         prepare_kernel,
+        (pltpu.VMEM((3 * S, LANES + 3 * S), BF), pltpu.VMEM((R * CH, LANES), F32)),
+        smem(1) + hbm(4),
+        vmem(2),
         (
-            arr((3 * WIN, LANES), BF),
-            arr((R * CH, LANES), F32),
-            arr((R * CH, 3 * XW + CH), BF),
-            arr((R * CH, S), F32),
-            arr((3 * R * FREQ, WIN), BF),
-            arr((2 * S, 3 * S), BF),
-            arr((2 * S, S), BF),
-            arr((tile_count * chunk, SRC), BF),
-            arr((blocks + CH, tile_count * chunk), BF),
+            pltpu.VMEM((3 * WIN, LANES), BF),
+            pltpu.VMEM((CH * S, S), F32),
+            pltpu.VMEM((R * CH, 3 * WIN), BF),
+            pltpu.VMEM(cot.shape, BF),
+            pltpu.VMEM(w1.shape, BF),
+            pltpu.VMEM(w2.shape, BF),
+            pltpu.VMEM(interp_bands.shape, BF),
+            pltpu.VMEM((9 * FREQ, CH), F32),
+            pltpu.VMEM((9 * CH, CH), F32),
+            pltpu.SemaphoreType.DMA((4,)),
         ),
-        smem(1) + vmem(8),
-        vmem(9),
-        (
-            pltpu.VMEM((CH * S, S), F32),
-            pltpu.VMEM((1, tile_count * chunk), I32),
-            pltpu.VMEM((R * CH, 3 * WIN), BF),
-        ),
-        cost_estimate=pl.CostEstimate(flops=4 * 10**9, bytes_accessed=4 * 10**6, transcendentals=0),
-    )(polar, cot, w1, w1t, w2t, conv1_bias.reshape(1, CH), interp_bands, slots, send)
+        cost_estimate=cost,
+    )(polar, *in_hbm(cot, w1, w2, interp_bands))
 
     padded = (S + 4) * FREQ
     weights, gp = call(
         patch_kernel,
-        (arr((CH, 2 * S), F32), arr((WIN, LANES), BF)),
-        smem(2) + vmem(6),
+        (pltpu.VMEM((CH, 2 * S), F32), pltpu.VMEM((WIN, LANES), BF)),
+        smem(2) + vmem(4),
         vmem(2),
         (
             pltpu.VMEM((padded + 8, S), F32),
@@ -418,16 +521,33 @@
             pltpu.VMEM((3 * XW + CH, LANES), BF),
             pltpu.VMEM((WIN, LANES), BF),
         ),
-    )(slots, patch_rows, received, ms, t1, bcol, gh, cb)
-
+    )(slots, patch_rows, bias, received, *in_vmem(big, gh))
+
+    rows = max(3 * S, tile_count * chunk)
+    lists = call(
+        functools.partial(lists_kernel, blocks),
+        pltpu.VMEM((rows, 4 * S + tile_count * chunk), BF),
+        smem(1) + hbm(5),
+        vmem(1)[0],
+        (
+            pltpu.VMEM((1, tile_count * chunk), I32),
+            pltpu.VMEM(w1.shape, BF),
+            pltpu.VMEM(interp_bands.shape, BF),
+            pltpu.VMEM(slots.shape, I32),
+            pltpu.VMEM(send.shape, I32),
+            pltpu.VMEM((9 * FREQ, CH), F32),
+            pltpu.SemaphoreType.DMA((4,)),
+        ),
+        cost_estimate=cost,
+    )(polar, *in_hbm(w1, interp_bands, slots, send), gp)
+    weights, lists = band_sum(weights, band_count, lists)
     returning = call(
         slots_kernel,
         arr((tile_count * chunk, 4 * S), BF),
-        smem(1) + vmem(4),
+        smem(1) + vmem(2),
         vmem(1)[0],
         (pltpu.VMEM((padded + 16, S), F32), pltpu.VMEM((SRC * FREQ, S), F32)),
-    )(patch_rows, gp, t3, mt, oh)
-    weights = band_sum(weights, band_count)
+    )(patch_rows, *in_vmem(gp, lists))
     returning = call(
         pack_kernel,
         arr((tile_count, chunk, 4 * S), BF),
@@ -438,21 +558,22 @@
     )(weights, returning.reshape(tile_count, chunk, 4 * S))
     returned = lax.all_to_all(returning, "tile", split_axis=0, concat_axis=0, tiled=True)
     norm_scale = float(band_count * tile_count * S * S) ** (-0.5)
-    grad_map, total = call(
+    grad_map, grad1, grad_bias, grad2 = call(
         functools.partial(final_kernel, norm_scale),
-        (arr((blocks, FREQ, S), F32), arr((CH, 2 * S), F32)),
+        (
+            arr((blocks, FREQ, S), F32),
+            arr((9, FREQ, CH), F32),
+            arr((1, CH), F32),
+            arr((9, CH, CH), F32),
+        ),
         vmem(2),
-        vmem(2),
-    )(sel, returned.reshape(tile_count * chunk, 4 * S))
-
-    grad2 = total[:, 0 : 9 * CH].reshape(CH, 3, 3, CH)
-    grad1 = jnp.stack([total[:, 9 * CH + dx * XW :][:, 0 : 3 * FREQ] for dx in range(3)], axis=1)
-    grad1 = grad1.reshape(CH, 3, 3, FREQ)
+        vmem(4),
+    )(*in_vmem(lists), returned.reshape(tile_count * chunk, 4 * S))
     return (
         grad_map[None],
-        jnp.transpose(grad1, (0, 3, 2, 1)),
-        total[:, 2 * S - 1],
-        jnp.transpose(grad2, (0, 3, 2, 1)),
+        jnp.transpose(grad1.reshape(3, 3, FREQ, CH), (3, 2, 0, 1)),
+        grad_bias.reshape(CH),
+        jnp.transpose(grad2.reshape(3, 3, CH, CH), (2, 3, 0, 1)),
     )
 
 

time: 50.9 us -> 37.6 us (0.74)
  local copies, waits for them, and re-layouts: 16.2 us -> 0.01 us
  Pallas kernels: 7.8 us -> 10.6 us
  waiting for transfers between devices: 3.14 us -> 5.07 us
  blocking collectives: 12.3 us -> 10.7 us
    unnamed x39 -> x4, local copies, waits for them, and re-layouts: 13 us -> 0.01 us
    all_to_all x1, waiting for transfers between devices: 0.01 us -> 3.36 us  [shards(): lax.all_to_all(outgoing, 'tile', split_axis=0, concat_axis=0, tiled=True)]
    pallas_call x4 -> x5, Pallas kernels: 6.67 us -> 9.41 us  [the longest x1 2.9 us: shards(): call(prepare_kernel, (pltpu.VMEM((3 * S, LANES + 3 * S), BF), pltpu.VMEM(...]
    transpose x2 -> x0, local copies, waits for them, and re-layouts: 1.67 us -> none  [the longest x1 0.88 us: shards(): w1t = jnp.transpose(conv1_weight, (1, 0, 2, 3)).reshape(FREQ, CH * 9)]
    all_to_all x1, blocking collectives: 12.3 us -> 10.7 us  [shards(): lax.all_to_all(returning, 'tile', split_axis=0, concat_axis=0, tiled=True)]
    ppermute x2, waiting for transfers between devices: 3.14 us -> 1.71 us  [band_sum(): value = value + lax.ppermute(value, 'band', pairs)]
    slice x5 -> x0, local copies, waits for them, and re-layouts: 1.01 us -> none  [the longest x1 0.69 us: shards(): total[:, 2 * S - 1]]
  transfers between devices with their start and end apart: 3 -> 3, of which waited for: 2 -> 3; matrix products, arithmetic and copies ran while one was open for 5% -> 0% of each run, Pallas kernels for 6% -> 14%
where the time goes in v2:
time: 37.6 us; the launch traced here: 37.2 us
  blocking collectives  10.7 us (28%)
  Pallas kernels  10.6 us (28%)
  starting transfers between devices  9.42 us (25%)
  waiting for transfers between devices  5.07 us (13%)
  between operations  1.35 us (4%)
    all_to_all x1, blocking collectives, shards(): lax.all_to_all(returning, 'tile', split_axis=0, concat_axis=0, tiled=True)  10.7 us
    all_to_all x1, starting transfers between devices, shards(): lax.all_to_all(outgoing, 'tile', split_axis=0, concat_axis=0, tiled=True)  5.18 us
    ppermute x2, starting transfers between devices, band_sum(): value = value + lax.ppermute(value, 'band', pairs)  4.24 us
    all_to_all x1, waiting for transfers between devices, shards(): lax.all_to_all(outgoing, 'tile', split_axis=0, concat_axis=0, tiled=True)  3.36 us
    pallas_call x1, Pallas kernels, shards(): call(prepare_kernel, (pltpu.VMEM((3 * S, LANES + 3 * S), BF), pltpu.VMEM(...  2.9 us
    pallas_call x1, Pallas kernels, shards(): call(patch_kernel, (pltpu.VMEM((CH, 2 * S), F32), pltpu.VMEM((WIN, LANES)...  2.33 us
    ppermute x2, waiting for transfers between devices, band_sum(): value = value + lax.ppermute(value, 'band', pairs)  1.71 us
    pallas_call x1, Pallas kernels, shards(): call(outgoing_kernel, arr((tile_count * capacity, FREQ, S), BF), hbm(2),...  1.71 us
  transfers between devices with their start and end apart: 3, of which 3 were waited for; matrix products, arithmetic and copies ran while one was open for 0% of the time, Pallas kernels for 14%

profile of v2, /device:TPU:0, one launch (start us, length us, event | category | flops | bytes accessed | tf_op | source)
XLA Modules:
  0.0 37.2 jit_solution(8542478236515989852)
XLA Ops:
  0.6 1.7 %shard_map.120 = bf16[256,4,128]{2,1,0:T(4,128)(2,1)} custom-call(s32[8,32]{1,0:T(8,128)} %bitcast.28, bf16[48,4,128]{2,1,0:T(4,128)(2,1)} %bitcast.27), custom_call_target="tpu_custom_call" | custom-call | tf_op jit(solution)/shard_map/pallas_call | solution.py:471
  2.3 5.2 %all-to-all-start = ((bf16[256,4,128]{2,1,0:T(4,128)(2,1)}), bf16[256,4,128]{2,1,0:T(4,128)(2,1)S(1)}, u32[]{:S(2)}, u32[]{:S(2)}) async-start(bf16[256,4,128]{2,1,0:T(4,128)(2,1)} %shard_map.120), calls=%async_computation | async-start | bytes 524288 | tf_op jit(solution)/shard_map/all_to_all | solution.py:482
  8.2 0.0 copy-start
  8.2 0.0 copy-start.1
  8.2 2.9 %shard_map.121 = (bf16[384,2432]{1,0:T(8,128)(2,1)S(1)}, f32[128,2048]{1,0:T(8,128)S(1)}) custom-call(s32[1]{0:T(128)} %bitcast.4.polar_ref, bf16[2048,128]{1,0:T(8,128)(2,1)} %bitcast.30, bf16[9,4,16]{2,1,0:T(4,128)(2,1)} %bitcast.35, bf16[9,16,16]{2,1,0:T(8,128)(2,1)} %bitcast.33, bf16[2,2,128,128]{3,2,1,0:T(8,128)(2,1)} %interp_hbm.3), custom_call_target="tpu_custom_call" | custom-call | flops 4000000000 | bytes 4000000 | tf_op jit(solution)/shard_map/pallas_call | solution.py:492
  11.1 3.4 %all-to-all-done.recv_ref = bf16[256,4,128]{2,1,0:T(4,128)(2,1)S(1)} async-done(((bf16[256,4,128]{2,1,0:T(4,128)(2,1)}), bf16[256,4,128]{2,1,0:T(4,128)(2,1)S(1)}, u32[]{:S(2)}, u32[]{:S(2)}) %all-to-all-start) | async-done | bytes 262176 | tf_op jit(solution)/shard_map/all_to_all | solution.py:482
  14.5 0.0 copy-done
  14.5 0.0 copy-done.1
  14.5 2.3 %shard_map.122 = (f32[16,256]{1,0:T(8,128)S(1)}, bf16[160,2048]{1,0:T(8,128)(2,1)S(1)}) custom-call(s32[1,129]{1,0:T(1,128)S(1)} %bitcast.25, s32[1,1]{1,0:T(1,128)S(6)} %copy.15.rows_ref, f32[1,16]{1,0:T(1,128)S(1)} %bitcast.26, bf16[256,4,128]{2,1,0:T(4,128)(2,1)S(1)} %all-to-all-done.recv_ref, bf16[384,2432]{1,0:T(8,128)(2,1)S(1)} %get-tuple-element.14.big_ref, ...), custom_call_target="tpu_custom_call" | custom-call | tf_op jit(solution)/shard_map/pallas_call | solution.py:513
  16.8 1.6 %collective-permute-start = (f32[16,256]{1,0:T(8,128)S(1)}, f32[16,256]{1,0:T(8,128)S(1)}, u32[]{:S(2)}, u32[]{:S(2)}) collective-permute-start(f32[16,256]{1,0:T(8,128)S(1)} %get-tuple-element.16), channel_id=1, source_target_pairs={{0,8},{8,0},{16,24},{24,16},{1,9},{9,1},{17,25},{25,17},{2,10},{10... | collective-permute-start | bytes 49160 | tf_op jit(solution)/shard_map/ppermute | solution.py:442
  18.5 1.4 %shard_map.123.big_ref = bf16[384,896]{1,0:T(8,128)(2,1)S(1)} custom-call(s32[1]{0:T(128)} %bitcast.4.polar_ref, bf16[9,4,16]{2,1,0:T(4,128)(2,1)} %bitcast.36, bf16[2,2,128,128]{3,2,1,0:T(8,128)(2,1)} %interp_hbm.3, s32[1,129]{1,0:T(1,128)} %bitcast.24, s32[8,32]{1,0:T(8,128)} %bitcast.29, bf16[160,2048]{1,0:T(8,128)(2,1)S(1)} %get-tuple-element.17.after_hbm.gp_ref), custom_call_target="tpu_custom_call" | custom-call | flops 4000000000 | bytes 4000000 | tf_op jit(solution)/shard_map/pallas_call | solution.py:527
  19.9 0.8 %collective-permute-done = f32[16,256]{1,0:T(8,128)S(1)} collective-permute-done((f32[16,256]{1,0:T(8,128)S(1)}, f32[16,256]{1,0:T(8,128)S(1)}, u32[]{:S(2)}, u32[]{:S(2)}) %collective-permute-start) | collective-permute-done | bytes 16416 | tf_op jit(solution)/shard_map/ppermute | solution.py:442
  20.6 2.6 %collective-permute-start.1 = (f32[16,256]{1,0:T(8,128)S(1)}, f32[16,256]{1,0:T(8,128)S(1)}, u32[]{:S(2)}, u32[]{:S(2)}) collective-permute-start(f32[16,256]{1,0:T(8,128)S(1)} %add.6), channel_id=1, source_target_pairs={{0,16},{8,24},{16,0},{24,8},{1,17},{9,25},{17,1},{25,9},{2,18},{10... | collective-permute-start | bytes 49160 | tf_op jit(solution)/shard_map/ppermute | solution.py:442
  23.2 1.1 %shard_map.124 = bf16[384,512]{1,0:T(8,128)(2,1)S(1)} custom-call(s32[1,1]{1,0:T(1,128)S(6)} %copy.15.rows_ref, bf16[160,2048]{1,0:T(8,128)(2,1)S(1)} %get-tuple-element.17.after_hbm.gp_ref, bf16[384,896]{1,0:T(8,128)(2,1)S(1)} %shard_map.123.big_ref), custom_call_target="tpu_custom_call" | custom-call | tf_op jit(solution)/shard_map/pallas_call | solution.py:544
  24.3 1.0 %collective-permute-done.1 = f32[16,256]{1,0:T(8,128)S(1)} collective-permute-done((f32[16,256]{1,0:T(8,128)S(1)}, f32[16,256]{1,0:T(8,128)S(1)}, u32[]{:S(2)}, u32[]{:S(2)}) %collective-permute-start.1) | collective-permute-done | bytes 16416 | tf_op jit(solution)/shard_map/ppermute | solution.py:442
  25.3 0.3 shard_map.125
  25.5 10.7 %all_to_all.10 = bf16[8,48,512]{2,1,0:T(8,128)(2,1)S(1)} all-to-all(bf16[8,48,512]{2,1,0:T(8,128)(2,1)S(1)} %shard_map.125), channel_id=1, replica_groups=mesh['band'=4,'tile'=8] {'tile'}, dimensions={0} | all-to-all | bytes 786432 | tf_op jit(solution)/shard_map/all_to_all | solution.py:559
  36.3 1.0 %shard_map.126 = (f32[48,4,128]{2,1,0:T(4,128)}, f32[9,4,16]{2,1,0:T(4,128)}, f32[1,16]{1,0:T(1,128)}, f32[9,16,16]{2,1,0:T(8,128)}) custom-call(bf16[384,896]{1,0:T(8,128)(2,1)S(1)} %shard_map.123.big_ref, bf16[384,512]{1,0:T(8,128)(2,1)S(1)} %bitcast.23), custom_call_target="tpu_custom_call" | custom-call | tf_op jit(solution)/shard_map/pallas_call | solution.py:561
  (2 shorter events, 0.0 us)
Async XLA Ops:
  2.3 12.1 %all-to-all-start = ((bf16[256,4,128]{2,1,0:T(4,128)(2,1)}), bf16[256,4,128]{2,1,0:T(4,128)(2,1)S(1)}, u32[]{:S(2)}, u32[]{:S(2)}) async-start(bf16[256,4,128]{2,1,0:T(4,128)(2,1)} %shard_map.120), calls=%async_computation | async-start | bytes 524288 | tf_op jit(solution)/shard_map/all_to_all | solution.py:482
  8.2 6.3 %copy-start = (s32[1,1,129]{2,1,0:T(1,128)S(1)}, s32[1,1,129]{2,1,0:T(1,128)}, u32[]{:S(2)}) copy-start(s32[1,1,129]{2,1,0:T(1,128)} %param.15) | copy-start | bytes 1552
  8.2 6.3 %copy-start.1 = (f32[16]{0:T(128)S(1)}, f32[16]{0:T(128)}, u32[]{:S(2)}) copy-start(f32[16]{0:T(128)} %param.12) | copy-start | bytes 196
  16.8 3.8 %collective-permute-start = (f32[16,256]{1,0:T(8,128)S(1)}, f32[16,256]{1,0:T(8,128)S(1)}, u32[]{:S(2)}, u32[]{:S(2)}) collective-permute-start(f32[16,256]{1,0:T(8,128)S(1)} %get-tuple-element.16), channel_id=1, source_target_pairs={{0,8},{8,0},{16,24},{24,16},{1,9},{9,1},{17,25},{25,17},{2,10},{10... | collective-permute-start | bytes 49160 | tf_op jit(solution)/shard_map/ppermute | solution.py:442
  20.6 4.6 %collective-permute-start.1 = (f32[16,256]{1,0:T(8,128)S(1)}, f32[16,256]{1,0:T(8,128)S(1)}, u32[]{:S(2)}, u32[]{:S(2)}) collective-permute-start(f32[16,256]{1,0:T(8,128)S(1)} %add.6), channel_id=1, source_target_pairs={{0,16},{8,24},{16,0},{24,8},{1,17},{9,25},{17,1},{25,9},{2,18},{10... | collective-permute-start | bytes 49160 | tf_op jit(solution)/shard_map/ppermute | solution.py:442

commit v3 on v2

--- a/solution.py
+++ b/solution.py
@@ -81,7 +81,7 @@
         View(ref, 0, chunks, 0, SRC),
         View(ref, 0, 2 * S, 2 * S, S),
         View(ref, 2 * S, 3 * R * FREQ, 2 * S, WIN),
-        View(ref, 0, blocks + CH, 4 * S, chunks),
+        View(ref, 0, blocks, 4 * S, chunks),
     )
 
 
@@ -92,23 +92,37 @@
     return copies
 
 
-def outgoing_kernel(send_hbm, map_hbm, out_ref, rows_ref, map_ref, sems):
-    owners, capacity = rows_ref.shape
+def outgoing_kernel(me_ref, send_hbm, map_hbm, *refs):
+    out_refs, (rows_ref, map_ref, sems) = refs[:-3], refs[-3:]
+    capacity = rows_ref.shape[1]
     for copy in fetch(((send_hbm, rows_ref), (map_hbm, map_ref)), sems):
         copy.wait()
-    for t in range(owners):
+    for j in range(2 * len(out_refs)):
+        t = me_ref[0] ^ j
         for c in range(capacity):
-            out_ref[t * capacity + c] = map_ref[rows_ref[t, c]]
+            out_refs[j // 2][(j % 2) * capacity + c] = map_ref[rows_ref[t, c]]
+
+
+def half_kernel(half, *refs):
+    out_ref = refs[-1]
+    capacity = refs[0].shape[0] // 2
+    for d, ref in enumerate(refs[:-1]):
+        out_ref[d * capacity : (d + 1) * capacity] = ref[half * capacity : (half + 1) * capacity]
 
 
 def prepare_kernel(
+    capacity,
     polar_ref,
+    me_ref,
     cot_hbm,
     w1_hbm,
     w2_hbm,
     interp_hbm,
+    slots_hbm,
     big_ref,
     gh_ref,
+    picks_ref,
+    slots_ref,
     cb_ref,
     plane,
     t2_ref,
@@ -121,7 +135,14 @@
     sems,
 ):
     copies = fetch(
-        ((w1_hbm, w1_ref), (w2_hbm, w2_ref), (interp_hbm, interp_ref), (cot_hbm, cot_ref)), sems
+        (
+            (w1_hbm, w1_ref),
+            (w2_hbm, w2_ref),
+            (interp_hbm, interp_ref),
+            (slots_hbm, slots_ref),
+            (cot_hbm, cot_ref),
+        ),
+        sems,
     )
     t1_ref, ms_ref = early(big_ref)
     for copy in copies[:-1]:
@@ -166,6 +187,14 @@
         ms_ref[at, S : 2 * S] = matrix.astype(BF)
         ms_ref[at, 2 * S : 3 * S] = shifted(matrix, 1).astype(BF)
 
+    half = picks_ref.shape[1] // 2
+    for k in range(slots_ref.shape[1]):
+        slot = slots_ref[0, k]
+        owner = lax.div(slot, capacity)
+        j = owner ^ me_ref[0]
+        picks_ref[0, k] = j & 1
+        picks_ref[0, half + k] = (j >> 1) * capacity + slot - owner * capacity
+
     copies[-1].wait()
     for o in range(CH):
         plane[o * S : (o + 1) * S, :] = cot_ref[o * S : (o + 1) * S, :].astype(F32)
@@ -186,6 +215,7 @@
 def lists_kernel(
     blocks,
     polar_ref,
+    me_ref,
     w1_hbm,
     interp_hbm,
     slots_hbm,
@@ -210,9 +240,8 @@
     for copy in fetch(pairs, sems):
         copy.wait()
     owners, capacity = send_ref.shape
-    chunk = capacity + CH
     nsrc = slots_ref.shape[1]
-    oh_ref, mt_ref, t3_ref, sel_ref = late(big_ref, owners * chunk, blocks)
+    oh_ref, mt_ref, t3_ref, sel_ref = late(big_ref, owners * capacity, blocks)
     for i in range(9):
         stack1[i * FREQ : (i + 1) * FREQ, :] = w1_ref[i].astype(F32)
     weights1 = stack1[...].astype(BF)
@@ -237,23 +266,24 @@
         mt_ref[half * S : (half + 1) * S, :] = matrix.T.astype(BF)
 
     slots = jnp.concatenate([slots_ref[...], jnp.full((1, SRC - nsrc), -1, I32)], axis=1)
-    for t in range(owners):
-        c = iota((chunk, SRC), 0)
-        hit = (c + t * capacity == slots) & (c < capacity)
-        oh_ref[t * chunk : (t + 1) * chunk, :] = jnp.where(hit, 1.0, 0.0).astype(BF)
-        lists[0:1, t * chunk : t * chunk + capacity] = send_ref[t : t + 1, :]
-        lists[0:1, t * chunk + capacity : (t + 1) * chunk] = (
-            iota((1, CH), 1) + blocks
-        )
+    for j in range(owners):
+        t = me_ref[0] ^ j
+        c = iota((capacity, SRC), 0)
+        hit = jnp.where(c + t * capacity == slots, 1.0, 0.0)
+        oh_ref[j * capacity : (j + 1) * capacity, :] = hit.astype(BF)
+        at = ((j % 2) * (owners // 2) + j // 2) * capacity
+        lists[0:1, at : at + capacity] = send_ref[pl.ds(t, 1), :]
     hit = lists[...] == iota(sel_ref.shape, 0)
     sel_ref[...] = jnp.where(hit, 1.0, 0.0).astype(BF)
 
 
 def patch_kernel(
-    slots_ref,
+    nsrc,
+    picks_ref,
     rows_ref,
     bias_ref,
-    recv_ref,
+    near_ref,
+    far_ref,
     big_ref,
     gh_ref,
     w_ref,
@@ -263,14 +293,16 @@
     xb,
     hb,
 ):
-    nsrc = slots_ref.shape[1]
+    half = picks_ref.shape[1] // 2
     total = src.shape[0]
     t1_ref, ms_ref = early(big_ref)
     src[0:FREQ, :] = jnp.zeros((FREQ, S), F32)
     first = FREQ * (nsrc + 1)
     src[first:total, :] = jnp.zeros((total - first, S), F32)
     for k in range(nsrc):
-        src[FREQ * (k + 1) : FREQ * (k + 2), :] = recv_ref[slots_ref[0, k]].astype(F32)
+        at = picks_ref[0, half + k]
+        block = jnp.where(picks_ref[0, k] == 0, near_ref[at].astype(F32), far_ref[at].astype(F32))
+        src[FREQ * (k + 1) : FREQ * (k + 2), :] = block
     limit = FREQ * (rows_ref[0, 0] + 1)
     step = img.shape[1] // 3
     for a in range(0, img.shape[1], step):
@@ -329,8 +361,10 @@
     w_ref[...] = jnp.where(lane == 2 * S - 1, ones, result)
 
 
-def slots_kernel(rows_ref, gp_ref, big_ref, out_ref, grad, gsrc):
-    oh_ref, mt_ref, t3_ref, _ = late(big_ref, out_ref.shape[0], 0)
+def slots_kernel(rows_ref, gp_ref, big_ref, *refs):
+    out_refs, (grad, gsrc) = refs[:-2], refs[-2:]
+    height = out_refs[0].shape[0]
+    oh_ref, mt_ref, t3_ref, _ = late(big_ref, height * len(out_refs), 0)
     part = R * FREQ
     limit = rows_ref[0, 0]
     pad = 2 * FREQ
@@ -358,33 +392,54 @@
         high = rows.astype(BF)
         low = (rows - high.astype(F32)).astype(BF)
         out = dot(oh_ref[...], high) + dot(oh_ref[...], low)
-        out_ref[:, f * S : (f + 1) * S] = out.astype(BF)
-
-
-def pack_kernel(w_ref, buffer_ref, out_ref, packed, sems):
-    del buffer_ref
-    owners, chunk, _ = out_ref.shape
+        for d, out_ref in enumerate(out_refs):
+            rows = out[d * height : (d + 1) * height, :]
+            out_ref[0:height, f * S : (f + 1) * S] = rows.astype(BF)
+
+
+def split(value):
+    high = value.astype(BF)
+    return high, (value - high.astype(F32)).astype(BF)
+
+
+def joined(rows):
+    return rows[:, 0 : 2 * S].astype(F32) + rows[:, 2 * S : 4 * S].astype(F32)
+
+
+def pack_kernel(w_ref, *refs):
+    count = (len(refs) - 2) // 2
+    out_refs, (packed, sems) = refs[count:-2], refs[-2:]
+    packed[:, 0 : 2 * S], packed[:, 2 * S : 4 * S] = split(w_ref[...])
+    pairs = [(packed, ref.at[pl.ds(ref.shape[0] - CH, CH), :]) for ref in out_refs]
+    for copy in fetch(pairs, sems):
+        copy.wait()
+
+
+def relay_kernel(w_ref, own_ref, *refs):
+    in_refs, (out_ref, sum_ref) = refs[:-2], refs[-2:]
+    pair = own_ref.shape[0]
+    capacity = pair // 2
     total = w_ref[...]
-    high = total.astype(BF)
-    packed[:, 0 : 2 * S] = high
-    packed[:, 2 * S : 4 * S] = (total - high.astype(F32)).astype(BF)
-    copies = [
-        pltpu.make_async_copy(packed, out_ref.at[t, pl.ds(chunk - CH, CH), :], sems.at[t])
-        for t in range(owners)
-    ]
-    for copy in copies:
-        copy.start()
-    for copy in copies:
-        copy.wait()
-
-
-def final_kernel(scale, big_ref, back_ref, map_ref, w1_ref, bias_ref, w2_ref):
+    for d, ref in enumerate((own_ref, *in_refs)):
+        out_ref[d * capacity : (d + 1) * capacity, :] = ref[capacity:pair, :]
+        if d:
+            total = total + joined(ref[pair : pair + CH, :])
+    sum_ref[...] = total
+    at = out_ref.shape[0] - CH
+    out_ref[at:, 0 : 2 * S], out_ref[at:, 2 * S : 4 * S] = split(total)
+
+
+def final_kernel(scale, big_ref, sum_ref, *refs):
+    in_refs, far_ref, (map_ref, w1_ref, bias_ref, w2_ref) = refs[:-5], refs[-5], refs[-4:]
     blocks = map_ref.shape[0]
-    sel_ref = late(big_ref, back_ref.shape[0], blocks)[-1]
-    total = dot(sel_ref[...], back_ref[...])
+    capacity = in_refs[0].shape[0] // 2
+    middle = capacity * len(in_refs)
+    sel = late(big_ref, 2 * middle, blocks)[-1][...]
+    near = jnp.concatenate([ref[0:capacity, :] for ref in in_refs], axis=0)
+    total = dot(sel, jnp.concatenate([near, far_ref[0:middle, :]], axis=0))
     for f in range(FREQ):
-        map_ref[:, f, :] = total[0:blocks, f * S : (f + 1) * S]
-    weights = (total[blocks:, 0 : 2 * S] + total[blocks:, 2 * S : 4 * S]) * scale
+        map_ref[:, f, :] = total[:, f * S : (f + 1) * S]
+    weights = (sum_ref[...] + joined(far_ref[middle:, :])) * scale
     for dy in range(3):
         for dx in range(3):
             at = (dx * 3 + dy) * CH
@@ -444,6 +499,17 @@
             value, beside = lax.optimization_barrier((value, beside))
         step *= 2
     return value, beside
+
+
+def to_chips(values, count):
+    return [
+        lax.ppermute(value, "tile", [(i, i ^ (2 * d)) for i in range(count)])
+        for d, value in enumerate(values, 1)
+    ]
+
+
+def to_core(value, count):
+    return lax.ppermute(value, "tile", [(i, i ^ 1) for i in range(count)])
 
 
 def shards(
@@ -464,23 +530,23 @@
     blocks = owned.shape[0]
     send = send_rows[0, 0]
     capacity = send.shape[1]
-    chunk = capacity + CH
+    chips = tile_count // 2
     slots = patch_slots[0]
     cot = cotangent.reshape(CH * S, S)
 
+    me = lax.axis_index("tile").astype(I32).reshape(1)
     outgoing = call(
         outgoing_kernel,
-        arr((tile_count * capacity, FREQ, S), BF),
-        hbm(2),
-        vmem(1)[0],
+        [arr((2 * capacity, FREQ, S), BF)] * chips,
+        smem(1) + hbm(2),
+        vmem(chips),
         (
             pltpu.SMEM(send.shape, I32),
             pltpu.VMEM(owned.shape, BF),
             pltpu.SemaphoreType.DMA((2,)),
         ),
-    )(*in_hbm(send, owned))
-    received = lax.all_to_all(outgoing, "tile", split_axis=0, concat_axis=0, tiled=True)
-
+    )(me, *in_hbm(send, owned))
+    received = [outgoing[0]] + to_chips(outgoing[1:], tile_count)
     is_polar = jnp.logical_or(
         band_index < band_count // 4, band_index >= band_count - band_count // 4
     )
@@ -489,12 +555,17 @@
     w2 = jnp.transpose(conv2_weight, (2, 3, 0, 1)).reshape(9, CH, CH)
     bias = conv1_bias.reshape(1, CH)
     cost = pl.CostEstimate(flops=4 * 10**9, bytes_accessed=4 * 10**6, transcendentals=0)
-    big, gh = call(
-        prepare_kernel,
-        (pltpu.VMEM((3 * S, LANES + 3 * S), BF), pltpu.VMEM((R * CH, LANES), F32)),
-        smem(1) + hbm(4),
-        vmem(2),
+    big, gh, picks = call(
+        functools.partial(prepare_kernel, capacity),
         (
+            pltpu.VMEM((3 * S, LANES + 3 * S), BF),
+            pltpu.VMEM((R * CH, LANES), F32),
+            pltpu.SMEM((1, 2 * SRC), I32),
+        ),
+        smem(2) + hbm(5),
+        vmem(2) + smem(1),
+        (
+            pltpu.SMEM(slots.shape, I32),
             pltpu.VMEM((3 * WIN, LANES), BF),
             pltpu.VMEM((CH * S, S), F32),
             pltpu.VMEM((R * CH, 3 * WIN), BF),
@@ -504,16 +575,22 @@
             pltpu.VMEM(interp_bands.shape, BF),
             pltpu.VMEM((9 * FREQ, CH), F32),
             pltpu.VMEM((9 * CH, CH), F32),
-            pltpu.SemaphoreType.DMA((4,)),
+            pltpu.SemaphoreType.DMA((5,)),
         ),
         cost_estimate=cost,
-    )(polar, *in_hbm(cot, w1, w2, interp_bands))
+    )(polar, me, *in_hbm(cot, w1, w2, interp_bands, slots))
+
+    big, *received = lax.optimization_barrier((big, *received))
+    blocks_half = pltpu.VMEM((chips * capacity, FREQ, S), BF)
+    relayed = call(functools.partial(half_kernel, 1), blocks_half, vmem(chips), vmem(1)[0])(*received)
+    far = to_core(relayed, tile_count)
+    near = call(functools.partial(half_kernel, 0), blocks_half, vmem(chips), vmem(1)[0])(*received)
 
     padded = (S + 4) * FREQ
     weights, gp = call(
-        patch_kernel,
+        functools.partial(patch_kernel, slots.shape[1]),
         (pltpu.VMEM((CH, 2 * S), F32), pltpu.VMEM((WIN, LANES), BF)),
-        smem(2) + vmem(4),
+        smem(2) + vmem(5),
         vmem(2),
         (
             pltpu.VMEM((padded + 8, S), F32),
@@ -521,16 +598,16 @@
             pltpu.VMEM((3 * XW + CH, LANES), BF),
             pltpu.VMEM((WIN, LANES), BF),
         ),
-    )(slots, patch_rows, bias, received, *in_vmem(big, gh))
-
-    rows = max(3 * S, tile_count * chunk)
+    )(picks, patch_rows, bias, near, far, *in_vmem(big, gh))
+
+    rows = max(3 * S, tile_count * capacity)
     lists = call(
         functools.partial(lists_kernel, blocks),
-        pltpu.VMEM((rows, 4 * S + tile_count * chunk), BF),
-        smem(1) + hbm(5),
+        pltpu.VMEM((rows, 4 * S + tile_count * capacity), BF),
+        smem(2) + hbm(5),
         vmem(1)[0],
         (
-            pltpu.VMEM((1, tile_count * chunk), I32),
+            pltpu.VMEM((1, tile_count * capacity), I32),
             pltpu.VMEM(w1.shape, BF),
             pltpu.VMEM(interp_bands.shape, BF),
             pltpu.VMEM(slots.shape, I32),
@@ -539,24 +616,34 @@
             pltpu.SemaphoreType.DMA((4,)),
         ),
         cost_estimate=cost,
-    )(polar, *in_hbm(w1, interp_bands, slots, send), gp)
+    )(polar, me, *in_hbm(w1, interp_bands, slots, send), gp)
     weights, lists = band_sum(weights, band_count, lists)
+    pair = 2 * capacity
+    full = arr((pair + CH, 4 * S), BF)
     returning = call(
         slots_kernel,
-        arr((tile_count * chunk, 4 * S), BF),
+        [arr((pair, 4 * S), BF)] + [full] * (chips - 1),
         smem(1) + vmem(2),
-        vmem(1)[0],
+        vmem(chips),
         (pltpu.VMEM((padded + 16, S), F32), pltpu.VMEM((SRC * FREQ, S), F32)),
     )(patch_rows, *in_vmem(gp, lists))
-    returning = call(
+    own = returning[0]
+    packed = call(
         pack_kernel,
-        arr((tile_count, chunk, 4 * S), BF),
-        vmem(1) + [pl.BlockSpec(memory_space=pl.ANY)],
-        pl.BlockSpec(memory_space=pl.ANY),
-        (pltpu.VMEM((CH, 4 * S), BF), pltpu.SemaphoreType.DMA((tile_count,))),
-        input_output_aliases={1: 0},
-    )(weights, returning.reshape(tile_count, chunk, 4 * S))
-    returned = lax.all_to_all(returning, "tile", split_axis=0, concat_axis=0, tiled=True)
+        [full] * (chips - 1),
+        vmem(1) + hbm(chips - 1),
+        hbm(chips - 1),
+        (pltpu.VMEM((CH, 4 * S), BF), pltpu.SemaphoreType.DMA((chips - 1,))),
+        input_output_aliases={i: i - 1 for i in range(1, chips)},
+    )(weights, *returning[1:])
+    returned = to_chips(packed, tile_count)
+    relayed, total = call(
+        relay_kernel,
+        (arr((chips * capacity + CH, 4 * S), BF), arr((CH, 2 * S), F32)),
+        vmem(1 + chips),
+        vmem(2),
+    )(weights, own, *returned)
+    back = to_core(relayed, tile_count)
     norm_scale = float(band_count * tile_count * S * S) ** (-0.5)
     grad_map, grad1, grad_bias, grad2 = call(
         functools.partial(final_kernel, norm_scale),
@@ -566,9 +653,9 @@
             arr((1, CH), F32),
             arr((9, CH, CH), F32),
         ),
-        vmem(2),
+        vmem(3 + chips),
         vmem(4),
-    )(*in_vmem(lists), returned.reshape(tile_count * chunk, 4 * S))
+    )(*in_vmem(lists), total, own, *returned, back)
     return (
         grad_map[None],
         jnp.transpose(grad1.reshape(3, 3, FREQ, CH), (3, 2, 0, 1)),

time: 37.6 us -> 33.1 us (0.88)
  blocking collectives: 10.7 us -> 0 us
  waiting for transfers between devices: 5.07 us -> 9.25 us
  starting transfers between devices: 9.42 us -> 12.5 us
  Pallas kernels: 10.6 us -> 9.78 us
    all_to_all x1 -> x0, blocking collectives: 10.7 us -> none  [shards(): lax.all_to_all(returning, 'tile', split_axis=0, concat_axis=0, tiled=True)]
    ppermute x0 -> x8, starting transfers between devices: none -> 8.24 us  [the longest x6 8.1 us: to_chips(): lax.ppermute(value, 'tile', [(i, i ^ 2 * d) for i in range(count)])]
    ppermute x0 -> x8, waiting for transfers between devices: none -> 7.37 us  [the longest x6 5.34 us: to_chips(): lax.ppermute(value, 'tile', [(i, i ^ 2 * d) for i in range(count)])]
    all_to_all x1 -> x0, starting transfers between devices: 5.18 us -> none  [shards(): lax.all_to_all(outgoing, 'tile', split_axis=0, concat_axis=0, tiled=True)]
    all_to_all x1 -> x0, waiting for transfers between devices: 3.36 us -> none  [shards(): lax.all_to_all(outgoing, 'tile', split_axis=0, concat_axis=0, tiled=True)]
    pallas_call x5 -> x8, Pallas kernels: 8.26 us -> 7.55 us  [the longest x1 3.37 us: shards(): call(functools.partial(prepare_kernel, capacity), (pltpu.VMEM((3 * S, LAN...]
  transfers between devices with their start and end apart: 3 -> 10, of which waited for: 3 -> 8; matrix products, arithmetic and copies ran while one was open for 0% -> 0% of each run, Pallas kernels for 14% -> 17%
where the time goes in v3:
time: 33.1 us; the launch traced here: 32.9 us
  starting transfers between devices  12.5 us (38%)
  Pallas kernels  9.78 us (30%)
  waiting for transfers between devices  9.25 us (28%)
  between operations  1.38 us (4%)
    ppermute x6, starting transfers between devices, to_chips(): lax.ppermute(value, 'tile', [(i, i ^ 2 * d) for i in range(count)])  8.1 us
    ppermute x6, waiting for transfers between devices, to_chips(): lax.ppermute(value, 'tile', [(i, i ^ 2 * d) for i in range(count)])  5.34 us
    ppermute x2, starting transfers between devices, band_sum(): value = value + lax.ppermute(value, 'band', pairs)  4.22 us
    pallas_call x1, Pallas kernels, shards(): call(functools.partial(prepare_kernel, capacity), (pltpu.VMEM((3 * S, LAN...  3.37 us
    ppermute x2, waiting for transfers between devices, to_core(): return lax.ppermute(value, 'tile', [(i, i ^ 1) for i in range(count)])  2.03 us
    pallas_call x1, Pallas kernels, shards(): call(functools.partial(patch_kernel, slots.shape[1]), (pltpu.VMEM((CH, 2...  2.01 us
    ppermute x2, waiting for transfers between devices, band_sum(): value = value + lax.ppermute(value, 'band', pairs)  1.88 us
    pallas_call x1, Pallas kernels, shards(): call(functools.partial(lists_kernel, blocks), pltpu.VMEM((rows, 4 * S + t...  1.39 us
  transfers between devices with their start and end apart: 10, of which 8 were waited for; matrix products, arithmetic and copies ran while one was open for 0% of the time, Pallas kernels for 17%

profile of v3, /device:TPU:0, one launch (start us, length us, event | category | flops | bytes accessed | tf_op | source)
XLA Modules:
  0.0 32.9 jit_solution(17821009668437066973)
XLA Ops:
  0.6 1.1 %shard_map.121 = (bf16[64,4,128]{2,1,0:T(4,128)(2,1)S(1)}, bf16[64,4,128]{2,1,0:T(4,128)(2,1)S(1)}, bf16[64,4,128]{2,1,0:T(4,128)(2,1)S(1)}, bf16[64,4,128]{2,1,0:T(4,128)(2,1)S(1)}) custom-call(s32[1]{0:T(128)} %bitcast.1.me_ref, s32[8,32]{1,0:T(8,128)} %bitcast.23, bf16[48,4,128]{2,1,0:T(4,128)(2,1)} %bitcast.22), custom_call_target="tpu_custom_call" | custom-call | tf_op jit(solution)/shard_map/pallas_call | solution.py:538
  1.7 3.0 %collective-permute-start = (bf16[64,4,128]{2,1,0:T(4,128)(2,1)S(1)}, bf16[64,4,128]{2,1,0:T(4,128)(2,1)S(1)}, u32[]{:S(2)}, u32[]{:S(2)}) collective-permute-start(bf16[64,4,128]{2,1,0:T(4,128)(2,1)S(1)} %get-tuple-element.36), channel_id=1, source_target_pairs={{0,2},{1,3},{2,0},{3,1},{4,6},{5,7},{6,4},{7,5},{8,10},{9,11},{10,... | collective-permute-start | bytes 196616 | tf_op jit(solution)/shard_map/ppermute | solution.py:506
  4.7 1.5 %collective-permute-start.1 = (bf16[64,4,128]{2,1,0:T(4,128)(2,1)S(1)}, bf16[64,4,128]{2,1,0:T(4,128)(2,1)S(1)}, u32[]{:S(2)}, u32[]{:S(2)}) collective-permute-start(bf16[64,4,128]{2,1,0:T(4,128)(2,1)S(1)} %get-tuple-element.37), channel_id=1, source_target_pairs={{0,4},{1,5},{2,6},{3,7},{4,0},{5,1},{6,2},{7,3},{8,12},{9,13},{10,... | collective-permute-start | bytes 196616 | tf_op jit(solution)/shard_map/ppermute | solution.py:506
  6.2 0.0 collective-permute-start.2
  6.3 0.0 copy-start
  6.3 3.4 %shard_map.120 = (bf16[384,2432]{1,0:T(8,128)(2,1)S(1)}, f32[128,2048]{1,0:T(8,128)S(1)}, s32[1,288]{1,0:T(1,128)S(4)}) custom-call(s32[1]{0:T(128)} %bitcast.polar_ref, s32[1]{0:T(128)} %bitcast.1.me_ref, bf16[2048,128]{1,0:T(8,128)(2,1)} %bitcast.25, bf16[9,4,16]{2,1,0:T(4,128)(2,1)} %bitcast.30, bf16[9,16,16]{2,1,0:T(8,128)(2,1)} %bitcast.28, ...), custom_call_target="tpu_custom_call" | custom-call | flops 4000000000 | bytes 4000000 | tf_op jit(solution)/shard_map/pallas_call | solution.py:558
  9.7 0.0 collective-permute-done.refs_1_
  9.7 0.0 collective-permute-done.1.refs_2_
  9.7 1.7 %collective-permute-done.2.refs_3_ = bf16[64,4,128]{2,1,0:T(4,128)(2,1)S(1)} collective-permute-done((bf16[64,4,128]{2,1,0:T(4,128)(2,1)S(1)}, bf16[64,4,128]{2,1,0:T(4,128)(2,1)S(1)}, u32[]{:S(2)}, u32[]{:S(2)}) %collective-permute-start.2) | collective-permute-done | bytes 65568 | tf_op jit(solution)/shard_map/ppermute | solution.py:506
  11.4 0.1 collective-permute-start.3
  12.2 0.7 %collective-permute-done.3.far_ref = bf16[128,4,128]{2,1,0:T(4,128)(2,1)S(1)} collective-permute-done((bf16[128,4,128]{2,1,0:T(4,128)(2,1)S(1)}, bf16[128,4,128]{2,1,0:T(4,128)(2,1)S(1)}, u32[]{:S(2)}, u32[]{:S(2)}) %collective-permute-start.3) | collective-permute-done | bytes 131104 | tf_op jit(solution)/shard_map/ppermute | solution.py:512
  12.8 0.0 copy-done
  12.8 2.0 %shard_map.124 = (f32[16,256]{1,0:T(8,128)S(1)}, bf16[160,2048]{1,0:T(8,128)(2,1)S(1)}) custom-call(s32[1,288]{1,0:T(1,128)S(4)} %get-tuple-element.33.picks_ref, s32[1,1]{1,0:T(1,128)S(6)} %copy.19.rows_ref, f32[1,16]{1,0:T(1,128)S(1)} %bitcast.21, bf16[128,4,128]{2,1,0:T(4,128)(2,1)S(1)} %shard_map.122.near_ref, ...), custom_call_target="tpu_custom_call" | custom-call | tf_op jit(solution)/shard_map/pallas_call | solution.py:590
  14.9 1.6 %collective-permute-start.4 = (f32[16,256]{1,0:T(8,128)S(1)}, f32[16,256]{1,0:T(8,128)S(1)}, u32[]{:S(2)}, u32[]{:S(2)}) collective-permute-start(f32[16,256]{1,0:T(8,128)S(1)} %get-tuple-element.45), channel_id=1, source_target_pairs={{0,8},{8,0},{16,24},{24,16},{1,9},{9,1},{17,25},{25,17},{2,10},{10... | collective-permute-start | bytes 49160 | tf_op jit(solution)/shard_map/ppermute | solution.py:497
  16.5 1.4 %shard_map.125.big_ref = bf16[384,768]{1,0:T(8,128)(2,1)S(1)} custom-call(s32[1]{0:T(128)} %bitcast.polar_ref, s32[1]{0:T(128)} %bitcast.1.me_ref, bf16[9,4,16]{2,1,0:T(4,128)(2,1)} %bitcast.31, bf16[2,2,128,128]{3,2,1,0:T(8,128)(2,1)} %interp_hbm.3, s32[1,129]{1,0:T(1,128)} %bitcast.33, s32[8,32]{1,0:T(8,128)} %bitcast.24, ...), custom_call_target="tpu_custom_call" | custom-call | flops 4000000000 | bytes 4000000 | tf_op jit(solution)/shard_map/pallas_call | solution.py:604
  17.9 0.8 %collective-permute-done.4 = f32[16,256]{1,0:T(8,128)S(1)} collective-permute-done((f32[16,256]{1,0:T(8,128)S(1)}, f32[16,256]{1,0:T(8,128)S(1)}, u32[]{:S(2)}, u32[]{:S(2)}) %collective-permute-start.4) | collective-permute-done | bytes 16416 | tf_op jit(solution)/shard_map/ppermute | solution.py:497
  18.7 2.6 %collective-permute-start.5 = (f32[16,256]{1,0:T(8,128)S(1)}, f32[16,256]{1,0:T(8,128)S(1)}, u32[]{:S(2)}, u32[]{:S(2)}) collective-permute-start(f32[16,256]{1,0:T(8,128)S(1)} %add.6), channel_id=1, source_target_pairs={{0,16},{8,24},{16,0},{24,8},{1,17},{9,25},{17,1},{25,9},{2,18},{10... | collective-permute-start | bytes 49160 | tf_op jit(solution)/shard_map/ppermute | solution.py:497
  21.3 0.9 %shard_map.126 = (bf16[64,512]{1,0:T(8,128)(2,1)S(1)}, bf16[80,512]{1,0:T(8,128)(2,1)S(1)}, bf16[80,512]{1,0:T(8,128)(2,1)S(1)}, bf16[80,512]{1,0:T(8,128)(2,1)S(1)}) custom-call(s32[1,1]{1,0:T(1,128)S(6)} %copy.19.rows_ref, bf16[160,2048]{1,0:T(8,128)(2,1)S(1)} %get-tuple-element.46.after_hbm.gp_ref, bf16[384,768]{1,0:T(8,128)(2,1)S(1)} %shard_map.125.big_ref), custom_call_target="tpu_custom_call" | custom-call | tf_op jit(solution)/shard_map/pallas_call | solution.py:623
  22.2 1.1 %collective-permute-done.5 = f32[16,256]{1,0:T(8,128)S(1)} collective-permute-done((f32[16,256]{1,0:T(8,128)S(1)}, f32[16,256]{1,0:T(8,128)S(1)}, u32[]{:S(2)}, u32[]{:S(2)}) %collective-permute-start.5) | collective-permute-done | bytes 16416 | tf_op jit(solution)/shard_map/ppermute | solution.py:497
  23.3 0.1 shard_map.127
  23.4 0.6 %collective-permute-start.6 = (bf16[80,512]{1,0:T(8,128)(2,1)S(1)}, bf16[80,512]{1,0:T(8,128)(2,1)S(1)}, u32[]{:S(2)}, u32[]{:S(2)}) collective-permute-start(bf16[80,512]{1,0:T(8,128)(2,1)S(1)} %get-tuple-element.53), channel_id=1, source_target_pairs={{0,2},{1,3},{2,0},{3,1},{4,6},{5,7},{6,4},{7,5},{8,10},{9,11},{10,... | collective-permute-start | bytes 245768 | tf_op jit(solution)/shard_map/ppermute | solution.py:506
  24.0 1.2 %collective-permute-start.7 = (bf16[80,512]{1,0:T(8,128)(2,1)S(1)}, bf16[80,512]{1,0:T(8,128)(2,1)S(1)}, u32[]{:S(2)}, u32[]{:S(2)}) collective-permute-start(bf16[80,512]{1,0:T(8,128)(2,1)S(1)} %get-tuple-element.54), channel_id=1, source_target_pairs={{0,4},{1,5},{2,6},{3,7},{4,0},{5,1},{6,2},{7,3},{8,12},{9,13},{10,... | collective-permute-start | bytes 245768 | tf_op jit(solution)/shard_map/ppermute | solution.py:506
  25.2 1.7 %collective-permute-start.8 = (bf16[80,512]{1,0:T(8,128)(2,1)S(1)}, bf16[80,512]{1,0:T(8,128)(2,1)S(1)}, u32[]{:S(2)}, u32[]{:S(2)}) collective-permute-start(bf16[80,512]{1,0:T(8,128)(2,1)S(1)} %get-tuple-element.55), channel_id=1, source_target_pairs={{0,6},{1,7},{2,4},{3,5},{4,2},{5,3},{6,0},{7,1},{8,14},{9,15},{10,... | collective-permute-start | bytes 245768 | tf_op jit(solution)/shard_map/ppermute | solution.py:506
  27.0 1.0 %collective-permute-done.6.refs_0_.refs_1_ = bf16[80,512]{1,0:T(8,128)(2,1)S(1)} collective-permute-done((bf16[80,512]{1,0:T(8,128)(2,1)S(1)}, bf16[80,512]{1,0:T(8,128)(2,1)S(1)}, u32[]{:S(2)}, u32[]{:S(2)}) %collective-permute-start.6) | collective-permute-done | bytes 81952 | tf_op jit(solution)/shard_map/ppermute | solution.py:506
  27.9 0.5 %collective-permute-done.7.refs_1_.refs_2_ = bf16[80,512]{1,0:T(8,128)(2,1)S(1)} collective-permute-done((bf16[80,512]{1,0:T(8,128)(2,1)S(1)}, bf16[80,512]{1,0:T(8,128)(2,1)S(1)}, u32[]{:S(2)}, u32[]{:S(2)}) %collective-permute-start.7) | collective-permute-done | bytes 81952 | tf_op jit(solution)/shard_map/ppermute | solution.py:506
  28.5 2.1 %collective-permute-done.8.refs_2_.refs_3_ = bf16[80,512]{1,0:T(8,128)(2,1)S(1)} collective-permute-done((bf16[80,512]{1,0:T(8,128)(2,1)S(1)}, bf16[80,512]{1,0:T(8,128)(2,1)S(1)}, u32[]{:S(2)}, u32[]{:S(2)}) %collective-permute-start.8) | collective-permute-done | bytes 81952 | tf_op jit(solution)/shard_map/ppermute | solution.py:506
  30.6 0.1 collective-permute-start.9
  30.7 1.4 %collective-permute-done.9.refs_4_ = bf16[144,512]{1,0:T(8,128)(2,1)S(1)} collective-permute-done((bf16[144,512]{1,0:T(8,128)(2,1)S(1)}, bf16[144,512]{1,0:T(8,128)(2,1)S(1)}, u32[]{:S(2)}, u32[]{:S(2)}) %collective-permute-start.9) | collective-permute-done | bytes 147488 | tf_op jit(solution)/shard_map/ppermute | solution.py:512
  32.0 0.8 %shard_map.129 = (f32[48,4,128]{2,1,0:T(4,128)}, f32[9,4,16]{2,1,0:T(4,128)}, f32[1,16]{1,0:T(1,128)}, f32[9,16,16]{2,1,0:T(8,128)}) custom-call(bf16[384,768]{1,0:T(8,128)(2,1)S(1)} %shard_map.125.big_ref, f32[16,256]{1,0:T(8,128)S(1)} %get-tuple-element.56.sum_ref, bf16[64,512]{1,0:T(8,128)(2,1)S(1)} %get-tuple-element.49.own_ref.refs_0_, ...), custom_call_target="tpu_custom_call" | custom-call | tf_op jit(solution)/shard_map/pallas_call | solution.py:648
  (5 shorter events, 0.1 us)
Async XLA Ops:
  1.7 7.9 %collective-permute-start = (bf16[64,4,128]{2,1,0:T(4,128)(2,1)S(1)}, bf16[64,4,128]{2,1,0:T(4,128)(2,1)S(1)}, u32[]{:S(2)}, u32[]{:S(2)}) collective-permute-start(bf16[64,4,128]{2,1,0:T(4,128)(2,1)S(1)} %get-tuple-element.36), channel_id=1, source_target_pairs={{0,2},{1,3},{2,0},{3,1},{4,6},{5,7},{6,4},{7,5},{8,10},{9,11},{10,... | collective-permute-start | bytes 196616 | tf_op jit(solution)/shard_map/ppermute | solution.py:506
  4.7 4.9 %collective-permute-start.1 = (bf16[64,4,128]{2,1,0:T(4,128)(2,1)S(1)}, bf16[64,4,128]{2,1,0:T(4,128)(2,1)S(1)}, u32[]{:S(2)}, u32[]{:S(2)}) collective-permute-start(bf16[64,4,128]{2,1,0:T(4,128)(2,1)S(1)} %get-tuple-element.37), channel_id=1, source_target_pairs={{0,4},{1,5},{2,6},{3,7},{4,0},{5,1},{6,2},{7,3},{8,12},{9,13},{10,... | collective-permute-start | bytes 196616 | tf_op jit(solution)/shard_map/ppermute | solution.py:506
  6.2 5.2 %collective-permute-start.2 = (bf16[64,4,128]{2,1,0:T(4,128)(2,1)S(1)}, bf16[64,4,128]{2,1,0:T(4,128)(2,1)S(1)}, u32[]{:S(2)}, u32[]{:S(2)}) collective-permute-start(bf16[64,4,128]{2,1,0:T(4,128)(2,1)S(1)} %get-tuple-element.38), channel_id=1, source_target_pairs={{0,6},{1,7},{2,4},{3,5},{4,2},{5,3},{6,0},{7,1},{8,14},{9,15},{10,... | collective-permute-start | bytes 196616 | tf_op jit(solution)/shard_map/ppermute | solution.py:506
  6.3 6.6 %copy-start = (f32[16]{0:T(128)S(1)}, f32[16]{0:T(128)}, u32[]{:S(2)}) copy-start(f32[16]{0:T(128)} %param.12) | copy-start | bytes 196
  11.4 1.4 %collective-permute-start.3 = (bf16[128,4,128]{2,1,0:T(4,128)(2,1)S(1)}, bf16[128,4,128]{2,1,0:T(4,128)(2,1)S(1)}, u32[]{:S(2)}, u32[]{:S(2)}) collective-permute-start(bf16[128,4,128]{2,1,0:T(4,128)(2,1)S(1)} %shard_map.123), channel_id=1, source_target_pairs={{0,1},{1,0},{2,3},{3,2},{4,5},{5,4},{6,7},{7,6},{8,9},{9,8},{10,11... | collective-permute-start | bytes 393224 | tf_op jit(solution)/shard_map/ppermute | solution.py:512
  14.9 3.8 %collective-permute-start.4 = (f32[16,256]{1,0:T(8,128)S(1)}, f32[16,256]{1,0:T(8,128)S(1)}, u32[]{:S(2)}, u32[]{:S(2)}) collective-permute-start(f32[16,256]{1,0:T(8,128)S(1)} %get-tuple-element.45), channel_id=1, source_target_pairs={{0,8},{8,0},{16,24},{24,16},{1,9},{9,1},{17,25},{25,17},{2,10},{10... | collective-permute-start | bytes 49160 | tf_op jit(solution)/shard_map/ppermute | solution.py:497
  18.7 4.6 %collective-permute-start.5 = (f32[16,256]{1,0:T(8,128)S(1)}, f32[16,256]{1,0:T(8,128)S(1)}, u32[]{:S(2)}, u32[]{:S(2)}) collective-permute-start(f32[16,256]{1,0:T(8,128)S(1)} %add.6), channel_id=1, source_target_pairs={{0,16},{8,24},{16,0},{24,8},{1,17},{9,25},{17,1},{25,9},{2,18},{10... | collective-permute-start | bytes 49160 | tf_op jit(solution)/shard_map/ppermute | solution.py:497
  23.4 4.5 %collective-permute-start.6 = (bf16[80,512]{1,0:T(8,128)(2,1)S(1)}, bf16[80,512]{1,0:T(8,128)(2,1)S(1)}, u32[]{:S(2)}, u32[]{:S(2)}) collective-permute-start(bf16[80,512]{1,0:T(8,128)(2,1)S(1)} %get-tuple-element.53), channel_id=1, source_target_pairs={{0,2},{1,3},{2,0},{3,1},{4,6},{5,7},{6,4},{7,5},{8,10},{9,11},{10,... | collective-permute-start | bytes 245768 | tf_op jit(solution)/shard_map/ppermute | solution.py:506
  24.0 4.4 %collective-permute-start.7 = (bf16[80,512]{1,0:T(8,128)(2,1)S(1)}, bf16[80,512]{1,0:T(8,128)(2,1)S(1)}, u32[]{:S(2)}, u32[]{:S(2)}) collective-permute-start(bf16[80,512]{1,0:T(8,128)(2,1)S(1)} %get-tuple-element.54), channel_id=1, source_target_pairs={{0,4},{1,5},{2,6},{3,7},{4,0},{5,1},{6,2},{7,3},{8,12},{9,13},{10,... | collective-permute-start | bytes 245768 | tf_op jit(solution)/shard_map/ppermute | solution.py:506
  25.2 5.3 %collective-permute-start.8 = (bf16[80,512]{1,0:T(8,128)(2,1)S(1)}, bf16[80,512]{1,0:T(8,128)(2,1)S(1)}, u32[]{:S(2)}, u32[]{:S(2)}) collective-permute-start(bf16[80,512]{1,0:T(8,128)(2,1)S(1)} %get-tuple-element.55), channel_id=1, source_target_pairs={{0,6},{1,7},{2,4},{3,5},{4,2},{5,3},{6,0},{7,1},{8,14},{9,15},{10,... | collective-permute-start | bytes 245768 | tf_op jit(solution)/shard_map/ppermute | solution.py:506
  30.6 1.4 %collective-permute-start.9 = (bf16[144,512]{1,0:T(8,128)(2,1)S(1)}, bf16[144,512]{1,0:T(8,128)(2,1)S(1)}, u32[]{:S(2)}, u32[]{:S(2)}) collective-permute-start(bf16[144,512]{1,0:T(8,128)(2,1)S(1)} %get-tuple-element.57), channel_id=1, source_target_pairs={{0,1},{1,0},{2,3},{3,2},{4,5},{5,4},{6,7},{7,6},{8,9},{9,8},{10,11... | collective-permute-start | bytes 442376 | tf_op jit(solution)/shard_map/ppermute | solution.py:512

commit v4 on v3

--- a/solution.py
+++ b/solution.py
@@ -85,6 +85,10 @@
     )
 
 
+def spot(d, chips):
+    return -d & (chips - 1)
+
+
 def fetch(pairs, sems):
     copies = [pltpu.make_async_copy(a, b, sems.at[i]) for i, (a, b) in enumerate(pairs)]
     for copy in copies:
@@ -97,10 +101,11 @@
     capacity = rows_ref.shape[1]
     for copy in fetch(((send_hbm, rows_ref), (map_hbm, map_ref)), sems):
         copy.wait()
-    for j in range(2 * len(out_refs)):
+    chips = len(out_refs)
+    for j in range(2 * chips):
         t = me_ref[0] ^ j
         for c in range(capacity):
-            out_refs[j // 2][(j % 2) * capacity + c] = map_ref[rows_ref[t, c]]
+            out_refs[spot(j // 2, chips)][(j % 2) * capacity + c] = map_ref[rows_ref[t, c]]
 
 
 def half_kernel(half, *refs):
@@ -111,6 +116,7 @@
 
 
 def prepare_kernel(
+    chips,
     capacity,
     polar_ref,
     me_ref,
@@ -190,10 +196,13 @@
     half = picks_ref.shape[1] // 2
     for k in range(slots_ref.shape[1]):
         slot = slots_ref[0, k]
-        owner = lax.div(slot, capacity)
+        if capacity & (capacity - 1):
+            owner = lax.div(slot, capacity)
+        else:
+            owner = slot >> (capacity.bit_length() - 1)
         j = owner ^ me_ref[0]
         picks_ref[0, k] = j & 1
-        picks_ref[0, half + k] = (j >> 1) * capacity + slot - owner * capacity
+        picks_ref[0, half + k] = (spot(j >> 1, chips) - owner) * capacity + slot
 
     copies[-1].wait()
     for o in range(CH):
@@ -270,8 +279,10 @@
         t = me_ref[0] ^ j
         c = iota((capacity, SRC), 0)
         hit = jnp.where(c + t * capacity == slots, 1.0, 0.0)
-        oh_ref[j * capacity : (j + 1) * capacity, :] = hit.astype(BF)
-        at = ((j % 2) * (owners // 2) + j // 2) * capacity
+        place = spot(j // 2, owners // 2)
+        at = (2 * place + j % 2) * capacity
+        oh_ref[at : at + capacity, :] = hit.astype(BF)
+        at = ((j % 2) * (owners // 2) + place) * capacity
         lists[0:1, at : at + capacity] = send_ref[pl.ds(t, 1), :]
     hit = lists[...] == iota(sel_ref.shape, 0)
     sel_ref[...] = jnp.where(hit, 1.0, 0.0).astype(BF)
@@ -322,11 +333,13 @@
     zero_edges(gp_ref, 0)
     own = (iota((R * CH, CH), 0) & 15) == iota((R * CH, CH), 1)
     bias = jnp.sum(jnp.where(own, bias_ref[...], 0.0), axis=1, keepdims=True)
+    pairs = jnp.zeros((R * CH, 3 * XW + CH), F32)
     for n in range(0, LANES, 2 * S):
         pre = dot(t1_ref[...], xb[:, n : n + 2 * S]) + bias
         gate = jax.nn.sigmoid(pre)
         hidden = (pre * gate).astype(BF)
         grad = (gh_ref[:, n : n + 2 * S] * (gate * (1.0 + pre * (1.0 - gate)))).astype(BF)
+        pairs = pairs + dot_t(grad, xb[:, n : n + 2 * S])
         for b in range(2):
             m = n // S + b
             lanes = slice(b * S, (b + 1) * S)
@@ -338,8 +351,9 @@
                     ref[0:CH, (m + 1) * S : (m + 2) * S] = value[(R - 1) * CH :, lanes]
     lane = iota((CH, 2 * S), 1)
     result = jnp.zeros((CH, 2 * S), F32)
+    every = dot_t(big_ref[:, 0:LANES], hb[...])
     for dx in range(3):
-        g = dot_t(big_ref[dx * S : (dx + 1) * S, 0:LANES], hb[...])
+        g = every[dx * S : (dx + 1) * S, :]
         g = jnp.concatenate([g, jnp.zeros((R * CH, 2 * S - WIN), F32)], axis=1)
         acc = g[0:CH, :]
         for r in range(1, R):
@@ -347,8 +361,7 @@
         if dx:
             acc = pltpu.roll(acc, dx * 3 * CH, 1)
         result = jnp.where((lane >= dx * 3 * CH) & (lane < (dx + 1) * 3 * CH), acc, result)
-    g = dot_t(gp_ref[CH : CH + R * CH, :], xb[...])
-    g = jnp.concatenate([g, jnp.zeros((R * CH, 2 * S - g.shape[1]), F32)], axis=1)
+    g = jnp.concatenate([pairs, jnp.zeros((R * CH, 2 * S - pairs.shape[1]), F32)], axis=1)
     acc = g[0:CH, :]
     ones = g[0:CH, :]
     for r in range(1, R):
@@ -419,14 +432,20 @@
     in_refs, (out_ref, sum_ref) = refs[:-2], refs[-2:]
     pair = own_ref.shape[0]
     capacity = pair // 2
-    total = w_ref[...]
+    high, low = split(w_ref[...])
+    terms = [high.astype(F32) + low.astype(F32)]
     for d, ref in enumerate((own_ref, *in_refs)):
         out_ref[d * capacity : (d + 1) * capacity, :] = ref[capacity:pair, :]
         if d:
-            total = total + joined(ref[pair : pair + CH, :])
-    sum_ref[...] = total
+            terms.append(joined(ref[pair : pair + CH, :]))
+    terms[1:] = terms[:0:-1]
+    while len(terms) > 1:
+        terms = [a + b for a, b in zip(terms[0::2], terms[1::2])]
+    high, low = split(terms[0])
+    sum_ref[...] = high.astype(F32) + low.astype(F32)
     at = out_ref.shape[0] - CH
-    out_ref[at:, 0 : 2 * S], out_ref[at:, 2 * S : 4 * S] = split(total)
+    out_ref[at:, 0 : 2 * S] = high
+    out_ref[at:, 2 * S : 4 * S] = low
 
 
 def final_kernel(scale, big_ref, sum_ref, *refs):
@@ -502,9 +521,10 @@
 
 
 def to_chips(values, count):
+    chips = count // 2
     return [
-        lax.ppermute(value, "tile", [(i, i ^ (2 * d)) for i in range(count)])
-        for d, value in enumerate(values, 1)
+        lax.ppermute(value, "tile", [(i, i ^ (2 * (chips - p))) for i in range(count)])
+        for p, value in enumerate(values, 1)
     ]
 
 
@@ -556,7 +576,7 @@
     bias = conv1_bias.reshape(1, CH)
     cost = pl.CostEstimate(flops=4 * 10**9, bytes_accessed=4 * 10**6, transcendentals=0)
     big, gh, picks = call(
-        functools.partial(prepare_kernel, capacity),
+        functools.partial(prepare_kernel, chips, capacity),
         (
             pltpu.VMEM((3 * S, LANES + 3 * S), BF),
             pltpu.VMEM((R * CH, LANES), F32),

time: 33.1 us -> 31.8 us (0.961)
  waiting for transfers between devices: 9.25 us -> 8.21 us
  Pallas kernels: 9.78 us -> 9.41 us
    ppermute x6, waiting for transfers between devices: 5.34 us -> 4.33 us  [to_chips(): lax.ppermute(value, 'tile', [(i, i ^ 2 * (chips - p)) for i in range(coun...]
  transfers between devices with their start and end apart: 10 -> 10, of which waited for: 8 -> 9; matrix products, arithmetic and copies ran while one was open for 0% -> 0% of each run, Pallas kernels for 17% -> 18%
where the time goes in v4:
time: 31.8 us; the launch traced here: 31.5 us
  starting transfers between devices  12.5 us (39%)
  Pallas kernels  9.41 us (30%)
  waiting for transfers between devices  8.21 us (26%)
  between operations  1.38 us (4%)
    ppermute x6, starting transfers between devices, to_chips(): lax.ppermute(value, 'tile', [(i, i ^ 2 * (chips - p)) for i in range(coun...  8.16 us
    ppermute x6, waiting for transfers between devices, to_chips(): lax.ppermute(value, 'tile', [(i, i ^ 2 * (chips - p)) for i in range(coun...  4.33 us
    ppermute x2, starting transfers between devices, band_sum(): value = value + lax.ppermute(value, 'band', pairs)  4.23 us
    pallas_call x1, Pallas kernels, shards(): call(functools.partial(prepare_kernel, chips, capacity), (pltpu.VMEM((3 *...  3.2 us
    ppermute x2, waiting for transfers between devices, to_core(): return lax.ppermute(value, 'tile', [(i, i ^ 1) for i in range(count)])  2.03 us
    ppermute x2, waiting for transfers between devices, band_sum(): value = value + lax.ppermute(value, 'band', pairs)  1.86 us
    pallas_call x1, Pallas kernels, shards(): call(functools.partial(patch_kernel, slots.shape[1]), (pltpu.VMEM((CH, 2...  1.8 us
    pallas_call x1, Pallas kernels, shards(): call(functools.partial(lists_kernel, blocks), pltpu.VMEM((rows, 4 * S + t...  1.39 us
  transfers between devices with their start and end apart: 10, of which 9 were waited for; matrix products, arithmetic and copies ran while one was open for 0% of the time, Pallas kernels for 18%

profile of v4, /device:TPU:0, one launch (start us, length us, event | category | flops | bytes accessed | tf_op | source)
XLA Modules:
  0.0 31.5 jit_solution(1591357485344035961)
XLA Ops:
  0.6 1.1 %shard_map.121 = (bf16[64,4,128]{2,1,0:T(4,128)(2,1)S(1)}, bf16[64,4,128]{2,1,0:T(4,128)(2,1)S(1)}, bf16[64,4,128]{2,1,0:T(4,128)(2,1)S(1)}, bf16[64,4,128]{2,1,0:T(4,128)(2,1)S(1)}) custom-call(s32[1]{0:T(128)} %bitcast.1.me_ref, s32[8,32]{1,0:T(8,128)} %bitcast.23, bf16[48,4,128]{2,1,0:T(4,128)(2,1)} %bitcast.22), custom_call_target="tpu_custom_call" | custom-call | tf_op jit(solution)/shard_map/pallas_call | solution.py:558
  1.7 4.0 %collective-permute-start = (bf16[64,4,128]{2,1,0:T(4,128)(2,1)S(1)}, bf16[64,4,128]{2,1,0:T(4,128)(2,1)S(1)}, u32[]{:S(2)}, u32[]{:S(2)}) collective-permute-start(bf16[64,4,128]{2,1,0:T(4,128)(2,1)S(1)} %get-tuple-element.36), channel_id=1, source_target_pairs={{0,6},{1,7},{2,4},{3,5},{4,2},{5,3},{6,0},{7,1},{8,14},{9,15},{10,... | collective-permute-start | bytes 196616 | tf_op jit(solution)/shard_map/ppermute | solution.py:526
  5.7 0.5 %collective-permute-start.1 = (bf16[64,4,128]{2,1,0:T(4,128)(2,1)S(1)}, bf16[64,4,128]{2,1,0:T(4,128)(2,1)S(1)}, u32[]{:S(2)}, u32[]{:S(2)}) collective-permute-start(bf16[64,4,128]{2,1,0:T(4,128)(2,1)S(1)} %get-tuple-element.37), channel_id=1, source_target_pairs={{0,4},{1,5},{2,6},{3,7},{4,0},{5,1},{6,2},{7,3},{8,12},{9,13},{10,... | collective-permute-start | bytes 196616 | tf_op jit(solution)/shard_map/ppermute | solution.py:526
  6.2 0.1 collective-permute-start.2
  6.3 0.0 copy-start
  6.3 3.2 %shard_map.120 = (bf16[384,2432]{1,0:T(8,128)(2,1)S(1)}, f32[128,2048]{1,0:T(8,128)S(1)}, s32[1,288]{1,0:T(1,128)S(4)}) custom-call(s32[1]{0:T(128)} %bitcast.polar_ref, s32[1]{0:T(128)} %bitcast.1.me_ref, bf16[2048,128]{1,0:T(8,128)(2,1)} %bitcast.25, bf16[9,4,16]{2,1,0:T(4,128)(2,1)} %bitcast.30, bf16[9,16,16]{2,1,0:T(8,128)(2,1)} %bitcast.28, ...), custom_call_target="tpu_custom_call" | custom-call | flops 4000000000 | bytes 4000000 | tf_op jit(solution)/shard_map/pallas_call | solution.py:578
  9.5 0.0 collective-permute-done.refs_1_
  9.6 0.4 %collective-permute-done.1.refs_2_ = bf16[64,4,128]{2,1,0:T(4,128)(2,1)S(1)} collective-permute-done((bf16[64,4,128]{2,1,0:T(4,128)(2,1)S(1)}, bf16[64,4,128]{2,1,0:T(4,128)(2,1)S(1)}, u32[]{:S(2)}, u32[]{:S(2)}) %collective-permute-start.1) | collective-permute-done | bytes 65568 | tf_op jit(solution)/shard_map/ppermute | solution.py:526
  9.9 0.5 %collective-permute-done.2.refs_3_ = bf16[64,4,128]{2,1,0:T(4,128)(2,1)S(1)} collective-permute-done((bf16[64,4,128]{2,1,0:T(4,128)(2,1)S(1)}, bf16[64,4,128]{2,1,0:T(4,128)(2,1)S(1)}, u32[]{:S(2)}, u32[]{:S(2)}) %collective-permute-start.2) | collective-permute-done | bytes 65568 | tf_op jit(solution)/shard_map/ppermute | solution.py:526
  10.5 0.1 collective-permute-start.3
  11.2 0.7 %collective-permute-done.3.far_ref = bf16[128,4,128]{2,1,0:T(4,128)(2,1)S(1)} collective-permute-done((bf16[128,4,128]{2,1,0:T(4,128)(2,1)S(1)}, bf16[128,4,128]{2,1,0:T(4,128)(2,1)S(1)}, u32[]{:S(2)}, u32[]{:S(2)}) %collective-permute-start.3) | collective-permute-done | bytes 131104 | tf_op jit(solution)/shard_map/ppermute | solution.py:532
  11.9 0.0 copy-done
  11.9 1.8 %shard_map.124 = (f32[16,256]{1,0:T(8,128)S(1)}, bf16[160,2048]{1,0:T(8,128)(2,1)S(1)}) custom-call(s32[1,288]{1,0:T(1,128)S(4)} %get-tuple-element.33.picks_ref, s32[1,1]{1,0:T(1,128)S(6)} %copy.19.rows_ref, f32[1,16]{1,0:T(1,128)S(1)} %bitcast.21, bf16[128,4,128]{2,1,0:T(4,128)(2,1)S(1)} %shard_map.122.near_ref, ...), custom_call_target="tpu_custom_call" | custom-call | tf_op jit(solution)/shard_map/pallas_call | solution.py:610
  13.7 1.6 %collective-permute-start.4 = (f32[16,256]{1,0:T(8,128)S(1)}, f32[16,256]{1,0:T(8,128)S(1)}, u32[]{:S(2)}, u32[]{:S(2)}) collective-permute-start(f32[16,256]{1,0:T(8,128)S(1)} %get-tuple-element.45), channel_id=1, source_target_pairs={{0,8},{8,0},{16,24},{24,16},{1,9},{9,1},{17,25},{25,17},{2,10},{10... | collective-permute-start | bytes 49160 | tf_op jit(solution)/shard_map/ppermute | solution.py:516
  15.3 1.4 %shard_map.125.big_ref = bf16[384,768]{1,0:T(8,128)(2,1)S(1)} custom-call(s32[1]{0:T(128)} %bitcast.polar_ref, s32[1]{0:T(128)} %bitcast.1.me_ref, bf16[9,4,16]{2,1,0:T(4,128)(2,1)} %bitcast.31, bf16[2,2,128,128]{3,2,1,0:T(8,128)(2,1)} %interp_hbm.3, s32[1,129]{1,0:T(1,128)} %bitcast.33, s32[8,32]{1,0:T(8,128)} %bitcast.24, ...), custom_call_target="tpu_custom_call" | custom-call | flops 4000000000 | bytes 4000000 | tf_op jit(solution)/shard_map/pallas_call | solution.py:624
  16.7 0.8 %collective-permute-done.4 = f32[16,256]{1,0:T(8,128)S(1)} collective-permute-done((f32[16,256]{1,0:T(8,128)S(1)}, f32[16,256]{1,0:T(8,128)S(1)}, u32[]{:S(2)}, u32[]{:S(2)}) %collective-permute-start.4) | collective-permute-done | bytes 16416 | tf_op jit(solution)/shard_map/ppermute | solution.py:516
  17.5 2.6 %collective-permute-start.5 = (f32[16,256]{1,0:T(8,128)S(1)}, f32[16,256]{1,0:T(8,128)S(1)}, u32[]{:S(2)}, u32[]{:S(2)}) collective-permute-start(f32[16,256]{1,0:T(8,128)S(1)} %add.6), channel_id=1, source_target_pairs={{0,16},{8,24},{16,0},{24,8},{1,17},{9,25},{17,1},{25,9},{2,18},{10... | collective-permute-start | bytes 49160 | tf_op jit(solution)/shard_map/ppermute | solution.py:516
  20.1 0.9 %shard_map.126 = (bf16[64,512]{1,0:T(8,128)(2,1)S(1)}, bf16[80,512]{1,0:T(8,128)(2,1)S(1)}, bf16[80,512]{1,0:T(8,128)(2,1)S(1)}, bf16[80,512]{1,0:T(8,128)(2,1)S(1)}) custom-call(s32[1,1]{1,0:T(1,128)S(6)} %copy.19.rows_ref, bf16[160,2048]{1,0:T(8,128)(2,1)S(1)} %get-tuple-element.46.after_hbm.gp_ref, bf16[384,768]{1,0:T(8,128)(2,1)S(1)} %shard_map.125.big_ref), custom_call_target="tpu_custom_call" | custom-call | tf_op jit(solution)/shard_map/pallas_call | solution.py:643
  21.0 1.1 %collective-permute-done.5 = f32[16,256]{1,0:T(8,128)S(1)} collective-permute-done((f32[16,256]{1,0:T(8,128)S(1)}, f32[16,256]{1,0:T(8,128)S(1)}, u32[]{:S(2)}, u32[]{:S(2)}) %collective-permute-start.5) | collective-permute-done | bytes 16416 | tf_op jit(solution)/shard_map/ppermute | solution.py:516
  22.1 0.1 shard_map.127
  22.3 2.0 %collective-permute-start.6 = (bf16[80,512]{1,0:T(8,128)(2,1)S(1)}, bf16[80,512]{1,0:T(8,128)(2,1)S(1)}, u32[]{:S(2)}, u32[]{:S(2)}) collective-permute-start(bf16[80,512]{1,0:T(8,128)(2,1)S(1)} %get-tuple-element.53), channel_id=1, source_target_pairs={{0,6},{1,7},{2,4},{3,5},{4,2},{5,3},{6,0},{7,1},{8,14},{9,15},{10,... | collective-permute-start | bytes 245768 | tf_op jit(solution)/shard_map/ppermute | solution.py:526
  24.3 0.5 %collective-permute-start.7 = (bf16[80,512]{1,0:T(8,128)(2,1)S(1)}, bf16[80,512]{1,0:T(8,128)(2,1)S(1)}, u32[]{:S(2)}, u32[]{:S(2)}) collective-permute-start(bf16[80,512]{1,0:T(8,128)(2,1)S(1)} %get-tuple-element.54), channel_id=1, source_target_pairs={{0,4},{1,5},{2,6},{3,7},{4,0},{5,1},{6,2},{7,3},{8,12},{9,13},{10,... | collective-permute-start | bytes 245768 | tf_op jit(solution)/shard_map/ppermute | solution.py:526
  24.8 1.0 %collective-permute-start.8 = (bf16[80,512]{1,0:T(8,128)(2,1)S(1)}, bf16[80,512]{1,0:T(8,128)(2,1)S(1)}, u32[]{:S(2)}, u32[]{:S(2)}) collective-permute-start(bf16[80,512]{1,0:T(8,128)(2,1)S(1)} %get-tuple-element.55), channel_id=1, source_target_pairs={{0,2},{1,3},{2,0},{3,1},{4,6},{5,7},{6,4},{7,5},{8,10},{9,11},{10,... | collective-permute-start | bytes 245768 | tf_op jit(solution)/shard_map/ppermute | solution.py:526
  25.8 1.9 %collective-permute-done.6.refs_0_.refs_1_ = bf16[80,512]{1,0:T(8,128)(2,1)S(1)} collective-permute-done((bf16[80,512]{1,0:T(8,128)(2,1)S(1)}, bf16[80,512]{1,0:T(8,128)(2,1)S(1)}, u32[]{:S(2)}, u32[]{:S(2)}) %collective-permute-start.6) | collective-permute-done | bytes 81952 | tf_op jit(solution)/shard_map/ppermute | solution.py:526
  27.7 1.1 %collective-permute-done.7.refs_1_.refs_2_ = bf16[80,512]{1,0:T(8,128)(2,1)S(1)} collective-permute-done((bf16[80,512]{1,0:T(8,128)(2,1)S(1)}, bf16[80,512]{1,0:T(8,128)(2,1)S(1)}, u32[]{:S(2)}, u32[]{:S(2)}) %collective-permute-start.7) | collective-permute-done | bytes 81952 | tf_op jit(solution)/shard_map/ppermute | solution.py:526
  28.7 0.5 %collective-permute-done.8.refs_2_.refs_3_ = bf16[80,512]{1,0:T(8,128)(2,1)S(1)} collective-permute-done((bf16[80,512]{1,0:T(8,128)(2,1)S(1)}, bf16[80,512]{1,0:T(8,128)(2,1)S(1)}, u32[]{:S(2)}, u32[]{:S(2)}) %collective-permute-start.8) | collective-permute-done | bytes 81952 | tf_op jit(solution)/shard_map/ppermute | solution.py:526
  29.3 0.1 collective-permute-start.9
  29.3 1.4 %collective-permute-done.9.refs_4_ = bf16[144,512]{1,0:T(8,128)(2,1)S(1)} collective-permute-done((bf16[144,512]{1,0:T(8,128)(2,1)S(1)}, bf16[144,512]{1,0:T(8,128)(2,1)S(1)}, u32[]{:S(2)}, u32[]{:S(2)}) %collective-permute-start.9) | collective-permute-done | bytes 147488 | tf_op jit(solution)/shard_map/ppermute | solution.py:532
  30.7 0.8 %shard_map.129 = (f32[48,4,128]{2,1,0:T(4,128)}, f32[9,4,16]{2,1,0:T(4,128)}, f32[1,16]{1,0:T(1,128)}, f32[9,16,16]{2,1,0:T(8,128)}) custom-call(bf16[384,768]{1,0:T(8,128)(2,1)S(1)} %shard_map.125.big_ref, f32[16,256]{1,0:T(8,128)S(1)} %get-tuple-element.56.sum_ref, bf16[64,512]{1,0:T(8,128)(2,1)S(1)} %get-tuple-element.49.own_ref.refs_0_, ...), custom_call_target="tpu_custom_call" | custom-call | tf_op jit(solution)/shard_map/pallas_call | solution.py:668
  (5 shorter events, 0.1 us)
Async XLA Ops:
  1.7 7.8 %collective-permute-start = (bf16[64,4,128]{2,1,0:T(4,128)(2,1)S(1)}, bf16[64,4,128]{2,1,0:T(4,128)(2,1)S(1)}, u32[]{:S(2)}, u32[]{:S(2)}) collective-permute-start(bf16[64,4,128]{2,1,0:T(4,128)(2,1)S(1)} %get-tuple-element.36), channel_id=1, source_target_pairs={{0,6},{1,7},{2,4},{3,5},{4,2},{5,3},{6,0},{7,1},{8,14},{9,15},{10,... | collective-permute-start | bytes 196616 | tf_op jit(solution)/shard_map/ppermute | solution.py:526
  5.7 4.3 %collective-permute-start.1 = (bf16[64,4,128]{2,1,0:T(4,128)(2,1)S(1)}, bf16[64,4,128]{2,1,0:T(4,128)(2,1)S(1)}, u32[]{:S(2)}, u32[]{:S(2)}) collective-permute-start(bf16[64,4,128]{2,1,0:T(4,128)(2,1)S(1)} %get-tuple-element.37), channel_id=1, source_target_pairs={{0,4},{1,5},{2,6},{3,7},{4,0},{5,1},{6,2},{7,3},{8,12},{9,13},{10,... | collective-permute-start | bytes 196616 | tf_op jit(solution)/shard_map/ppermute | solution.py:526
  6.2 4.3 %collective-permute-start.2 = (bf16[64,4,128]{2,1,0:T(4,128)(2,1)S(1)}, bf16[64,4,128]{2,1,0:T(4,128)(2,1)S(1)}, u32[]{:S(2)}, u32[]{:S(2)}) collective-permute-start(bf16[64,4,128]{2,1,0:T(4,128)(2,1)S(1)} %get-tuple-element.38), channel_id=1, source_target_pairs={{0,2},{1,3},{2,0},{3,1},{4,6},{5,7},{6,4},{7,5},{8,10},{9,11},{10,... | collective-permute-start | bytes 196616 | tf_op jit(solution)/shard_map/ppermute | solution.py:526
  6.3 5.6 %copy-start = (f32[16]{0:T(128)S(1)}, f32[16]{0:T(128)}, u32[]{:S(2)}) copy-start(f32[16]{0:T(128)} %param.12) | copy-start | bytes 196
  10.5 1.4 %collective-permute-start.3 = (bf16[128,4,128]{2,1,0:T(4,128)(2,1)S(1)}, bf16[128,4,128]{2,1,0:T(4,128)(2,1)S(1)}, u32[]{:S(2)}, u32[]{:S(2)}) collective-permute-start(bf16[128,4,128]{2,1,0:T(4,128)(2,1)S(1)} %shard_map.123), channel_id=1, source_target_pairs={{0,1},{1,0},{2,3},{3,2},{4,5},{5,4},{6,7},{7,6},{8,9},{9,8},{10,11... | collective-permute-start | bytes 393224 | tf_op jit(solution)/shard_map/ppermute | solution.py:532
  13.7 3.8 %collective-permute-start.4 = (f32[16,256]{1,0:T(8,128)S(1)}, f32[16,256]{1,0:T(8,128)S(1)}, u32[]{:S(2)}, u32[]{:S(2)}) collective-permute-start(f32[16,256]{1,0:T(8,128)S(1)} %get-tuple-element.45), channel_id=1, source_target_pairs={{0,8},{8,0},{16,24},{24,16},{1,9},{9,1},{17,25},{25,17},{2,10},{10... | collective-permute-start | bytes 49160 | tf_op jit(solution)/shard_map/ppermute | solution.py:516
  17.5 4.6 %collective-permute-start.5 = (f32[16,256]{1,0:T(8,128)S(1)}, f32[16,256]{1,0:T(8,128)S(1)}, u32[]{:S(2)}, u32[]{:S(2)}) collective-permute-start(f32[16,256]{1,0:T(8,128)S(1)} %add.6), channel_id=1, source_target_pairs={{0,16},{8,24},{16,0},{24,8},{1,17},{9,25},{17,1},{25,9},{2,18},{10... | collective-permute-start | bytes 49160 | tf_op jit(solution)/shard_map/ppermute | solution.py:516
  22.3 5.4 %collective-permute-start.6 = (bf16[80,512]{1,0:T(8,128)(2,1)S(1)}, bf16[80,512]{1,0:T(8,128)(2,1)S(1)}, u32[]{:S(2)}, u32[]{:S(2)}) collective-permute-start(bf16[80,512]{1,0:T(8,128)(2,1)S(1)} %get-tuple-element.53), channel_id=1, source_target_pairs={{0,6},{1,7},{2,4},{3,5},{4,2},{5,3},{6,0},{7,1},{8,14},{9,15},{10,... | collective-permute-start | bytes 245768 | tf_op jit(solution)/shard_map/ppermute | solution.py:526
  24.3 4.4 %collective-permute-start.7 = (bf16[80,512]{1,0:T(8,128)(2,1)S(1)}, bf16[80,512]{1,0:T(8,128)(2,1)S(1)}, u32[]{:S(2)}, u32[]{:S(2)}) collective-permute-start(bf16[80,512]{1,0:T(8,128)(2,1)S(1)} %get-tuple-element.54), channel_id=1, source_target_pairs={{0,4},{1,5},{2,6},{3,7},{4,0},{5,1},{6,2},{7,3},{8,12},{9,13},{10,... | collective-permute-start | bytes 245768 | tf_op jit(solution)/shard_map/ppermute | solution.py:526
  24.8 4.4 %collective-permute-start.8 = (bf16[80,512]{1,0:T(8,128)(2,1)S(1)}, bf16[80,512]{1,0:T(8,128)(2,1)S(1)}, u32[]{:S(2)}, u32[]{:S(2)}) collective-permute-start(bf16[80,512]{1,0:T(8,128)(2,1)S(1)} %get-tuple-element.55), channel_id=1, source_target_pairs={{0,2},{1,3},{2,0},{3,1},{4,6},{5,7},{6,4},{7,5},{8,10},{9,11},{10,... | collective-permute-start | bytes 245768 | tf_op jit(solution)/shard_map/ppermute | solution.py:526
  29.3 1.4 %collective-permute-start.9 = (bf16[144,512]{1,0:T(8,128)(2,1)S(1)}, bf16[144,512]{1,0:T(8,128)(2,1)S(1)}, u32[]{:S(2)}, u32[]{:S(2)}) collective-permute-start(bf16[144,512]{1,0:T(8,128)(2,1)S(1)} %get-tuple-element.57), channel_id=1, source_target_pairs={{0,1},{1,0},{2,3},{3,2},{4,5},{5,4},{6,7},{7,6},{8,9},{9,8},{10,11... | collective-permute-start | bytes 442376 | tf_op jit(solution)/shard_map/ppermute | solution.py:532

commit v5 on v4

--- a/solution.py
+++ b/solution.py
@@ -73,7 +73,11 @@
 
 
 def early(ref):
-    return View(ref, 2 * S, R * CH, LANES, 3 * XW + CH), View(ref, 0, 2 * S, LANES, 3 * S)
+    return (
+        View(ref, 2 * S, R * CH, LANES, 3 * XW + CH),
+        View(ref, 0, 2 * S, LANES, 3 * S),
+        View(ref, 0, R * CH, LANES + 3 * S, 3 * WIN),
+    )
 
 
 def late(ref, chunks, blocks):
@@ -126,12 +130,9 @@
     interp_hbm,
     slots_hbm,
     big_ref,
-    gh_ref,
     picks_ref,
     slots_ref,
-    cb_ref,
     plane,
-    t2_ref,
     cot_ref,
     w1_ref,
     w2_ref,
@@ -150,7 +151,7 @@
         ),
         sems,
     )
-    t1_ref, ms_ref = early(big_ref)
+    t1_ref, ms_ref, t2_ref = early(big_ref)
     for copy in copies[:-1]:
         copy.wait()
     for i in range(9):
@@ -208,17 +209,17 @@
     for o in range(CH):
         plane[o * S : (o + 1) * S, :] = cot_ref[o * S : (o + 1) * S, :].astype(F32)
     for dx in range(3):
-        zero_edges(cb_ref, dx * WIN)
+        zero_edges(big_ref, dx * WIN)
     for y in range(S):
         rows = plane[pl.ds(y, CH, stride=S), :]
-        block, r = divmod(y, R)
         for dx, tile in enumerate((shifted(rows, 1), rows, shifted(rows, -1))):
-            tile = tile.astype(BF)
-            store_window(cb_ref, dx * WIN, y, tile)
-            at = dx * S + r * CH
-            big_ref[at : at + CH, block * S : (block + 1) * S] = tile
+            store_window(big_ref, dx * WIN, y, tile.astype(BF))
+
+
+def hidden_kernel(big_ref, gh_ref):
+    banded = early(big_ref)[-1][...]
     for n in range(0, LANES, 512):
-        gh_ref[:, n : n + 512] = dot(t2_ref[...], cb_ref[:, n : n + 512])
+        gh_ref[:, n : n + 512] = dot(banded, big_ref[0 : 3 * WIN, n : n + 512])
 
 
 def lists_kernel(
@@ -306,7 +307,7 @@
 ):
     half = picks_ref.shape[1] // 2
     total = src.shape[0]
-    t1_ref, ms_ref = early(big_ref)
+    t1_ref, ms_ref, _ = early(big_ref)
     src[0:FREQ, :] = jnp.zeros((FREQ, S), F32)
     first = FREQ * (nsrc + 1)
     src[first:total, :] = jnp.zeros((total - first, S), F32)
@@ -351,7 +352,8 @@
                     ref[0:CH, (m + 1) * S : (m + 2) * S] = value[(R - 1) * CH :, lanes]
     lane = iota((CH, 2 * S), 1)
     result = jnp.zeros((CH, 2 * S), F32)
-    every = dot_t(big_ref[:, 0:LANES], hb[...])
+    middle = [big_ref[dx * WIN + CH : (dx + 1) * WIN - CH, 0:LANES] for dx in range(3)]
+    every = dot_t(jnp.concatenate(middle, axis=0), hb[...])
     for dx in range(3):
         g = every[dx * S : (dx + 1) * S, :]
         g = jnp.concatenate([g, jnp.zeros((R * CH, 2 * S - WIN), F32)], axis=1)
@@ -575,20 +577,17 @@
     w2 = jnp.transpose(conv2_weight, (2, 3, 0, 1)).reshape(9, CH, CH)
     bias = conv1_bias.reshape(1, CH)
     cost = pl.CostEstimate(flops=4 * 10**9, bytes_accessed=4 * 10**6, transcendentals=0)
-    big, gh, picks = call(
+    big, picks = call(
         functools.partial(prepare_kernel, chips, capacity),
         (
-            pltpu.VMEM((3 * S, LANES + 3 * S), BF),
-            pltpu.VMEM((R * CH, LANES), F32),
+            pltpu.VMEM((3 * WIN, LANES + 7 * S), BF),
             pltpu.SMEM((1, 2 * SRC), I32),
         ),
         smem(2) + hbm(5),
-        vmem(2) + smem(1),
+        vmem(1) + smem(1),
         (
             pltpu.SMEM(slots.shape, I32),
-            pltpu.VMEM((3 * WIN, LANES), BF),
             pltpu.VMEM((CH * S, S), F32),
-            pltpu.VMEM((R * CH, 3 * WIN), BF),
             pltpu.VMEM(cot.shape, BF),
             pltpu.VMEM(w1.shape, BF),
             pltpu.VMEM(w2.shape, BF),
@@ -606,6 +605,9 @@
     far = to_core(relayed, tile_count)
     near = call(functools.partial(half_kernel, 0), blocks_half, vmem(chips), vmem(1)[0])(*received)
 
+    gh = call(
+        hidden_kernel, pltpu.VMEM((R * CH, LANES), F32), vmem(1), vmem(1)[0]
+    )(*in_vmem(big))
     padded = (S + 4) * FREQ
     weights, gp = call(
         functools.partial(patch_kernel, slots.shape[1]),

time: 31.8 us -> 31.4 us (0.987)
  waiting for transfers between devices: 8.21 us -> 7.76 us
    pallas_call x1, Pallas kernels: 3.2 us -> 2.73 us  [shards(): call(functools.partial(prepare_kernel, chips, capacity), (pltpu.VMEM((3 *...]
    ppermute x2, waiting for transfers between devices: 2.03 us -> 1.57 us  [to_core(): return lax.ppermute(value, 'tile', [(i, i ^ 1) for i in range(count)])]
    pallas_call x0 -> x1, Pallas kernels: none -> 0.45 us  [shards(): call(hidden_kernel, pltpu.VMEM((R * CH, LANES), F32), vmem(1), vmem(1)[0])]
where the time goes in v5:
time: 31.4 us; the launch traced here: 31.1 us
  starting transfers between devices  12.5 us (40%)
  Pallas kernels  9.41 us (30%)
  waiting for transfers between devices  7.76 us (25%)
  between operations  1.39 us (4%)
    ppermute x6, starting transfers between devices, to_chips(): lax.ppermute(value, 'tile', [(i, i ^ 2 * (chips - p)) for i in range(coun...  8.16 us
    ppermute x6, waiting for transfers between devices, to_chips(): lax.ppermute(value, 'tile', [(i, i ^ 2 * (chips - p)) for i in range(coun...  4.33 us
    ppermute x2, starting transfers between devices, band_sum(): value = value + lax.ppermute(value, 'band', pairs)  4.23 us
    pallas_call x1, Pallas kernels, shards(): call(functools.partial(prepare_kernel, chips, capacity), (pltpu.VMEM((3 *...  2.73 us
    ppermute x2, waiting for transfers between devices, band_sum(): value = value + lax.ppermute(value, 'band', pairs)  1.86 us
    pallas_call x1, Pallas kernels, shards(): call(functools.partial(patch_kernel, slots.shape[1]), (pltpu.VMEM((CH, 2...  1.82 us
    ppermute x2, waiting for transfers between devices, to_core(): return lax.ppermute(value, 'tile', [(i, i ^ 1) for i in range(count)])  1.57 us
    pallas_call x1, Pallas kernels, shards(): call(functools.partial(lists_kernel, blocks), pltpu.VMEM((rows, 4 * S + t...  1.39 us
  transfers between devices with their start and end apart: 10, of which 9 were waited for; matrix products, arithmetic and copies ran while one was open for 0% of the time, Pallas kernels for 18%

profile of v5, /device:TPU:0, one launch (start us, length us, event | category | flops | bytes accessed | tf_op | source)
XLA Modules:
  0.0 31.1 jit_solution(9440106179064809177)
XLA Ops:
  0.6 1.1 %shard_map.121 = (bf16[64,4,128]{2,1,0:T(4,128)(2,1)S(1)}, bf16[64,4,128]{2,1,0:T(4,128)(2,1)S(1)}, bf16[64,4,128]{2,1,0:T(4,128)(2,1)S(1)}, bf16[64,4,128]{2,1,0:T(4,128)(2,1)S(1)}) custom-call(s32[1]{0:T(128)} %bitcast.1.me_ref, s32[8,32]{1,0:T(8,128)} %bitcast.23, bf16[48,4,128]{2,1,0:T(4,128)(2,1)} %bitcast.22), custom_call_target="tpu_custom_call" | custom-call | tf_op jit(solution)/shard_map/pallas_call | solution.py:560
  1.7 4.0 %collective-permute-start = (bf16[64,4,128]{2,1,0:T(4,128)(2,1)S(1)}, bf16[64,4,128]{2,1,0:T(4,128)(2,1)S(1)}, u32[]{:S(2)}, u32[]{:S(2)}) collective-permute-start(bf16[64,4,128]{2,1,0:T(4,128)(2,1)S(1)} %get-tuple-element.35), channel_id=1, source_target_pairs={{0,6},{1,7},{2,4},{3,5},{4,2},{5,3},{6,0},{7,1},{8,14},{9,15},{10,... | collective-permute-start | bytes 196616 | tf_op jit(solution)/shard_map/ppermute | solution.py:528
  5.7 0.5 %collective-permute-start.1 = (bf16[64,4,128]{2,1,0:T(4,128)(2,1)S(1)}, bf16[64,4,128]{2,1,0:T(4,128)(2,1)S(1)}, u32[]{:S(2)}, u32[]{:S(2)}) collective-permute-start(bf16[64,4,128]{2,1,0:T(4,128)(2,1)S(1)} %get-tuple-element.36), channel_id=1, source_target_pairs={{0,4},{1,5},{2,6},{3,7},{4,0},{5,1},{6,2},{7,3},{8,12},{9,13},{10,... | collective-permute-start | bytes 196616 | tf_op jit(solution)/shard_map/ppermute | solution.py:528
  6.2 0.1 collective-permute-start.2
  6.3 2.7 %shard_map.120 = (bf16[480,2944]{1,0:T(8,128)(2,1)S(1)}, s32[1,288]{1,0:T(1,128)S(4)}) custom-call(s32[1]{0:T(128)} %bitcast.polar_ref, s32[1]{0:T(128)} %bitcast.1.me_ref, bf16[2048,128]{1,0:T(8,128)(2,1)} %bitcast.25, bf16[9,4,16]{2,1,0:T(4,128)(2,1)} %bitcast.30, bf16[9,16,16]{2,1,0:T(8,128)(2,1)} %bitcast.28, bf16[2,2,128,128]{3,2,1,0:T(8,128)(2,1)} %interp_hbm.3, ...), custom_call_target="tpu_custom_call" | custom-call | flops 4000000000 | bytes 4000000 | tf_op jit(solution)/shard_map/pallas_call | solution.py:580
  9.1 0.0 copy-start
  9.1 0.0 collective-permute-done.refs_1_
  9.1 0.9 %collective-permute-done.1.refs_2_ = bf16[64,4,128]{2,1,0:T(4,128)(2,1)S(1)} collective-permute-done((bf16[64,4,128]{2,1,0:T(4,128)(2,1)S(1)}, bf16[64,4,128]{2,1,0:T(4,128)(2,1)S(1)}, u32[]{:S(2)}, u32[]{:S(2)}) %collective-permute-start.1) | collective-permute-done | bytes 65568 | tf_op jit(solution)/shard_map/ppermute | solution.py:528
  9.9 0.5 %collective-permute-done.2.refs_3_ = bf16[64,4,128]{2,1,0:T(4,128)(2,1)S(1)} collective-permute-done((bf16[64,4,128]{2,1,0:T(4,128)(2,1)S(1)}, bf16[64,4,128]{2,1,0:T(4,128)(2,1)S(1)}, u32[]{:S(2)}, u32[]{:S(2)}) %collective-permute-start.2) | collective-permute-done | bytes 65568 | tf_op jit(solution)/shard_map/ppermute | solution.py:528
  10.5 0.1 collective-permute-start.3
  11.2 0.5 %shard_map.124.gh_ref = f32[128,2048]{1,0:T(8,128)S(1)} custom-call(bf16[480,2944]{1,0:T(8,128)(2,1)S(1)} %get-tuple-element.42.big_ref), custom_call_target="tpu_custom_call" | custom-call | tf_op jit(solution)/shard_map/pallas_call | solution.py:608
  11.7 0.2 collective-permute-done.3.far_ref
  11.9 0.0 copy-done
  11.9 1.8 %shard_map.125 = (f32[16,256]{1,0:T(8,128)S(1)}, bf16[160,2048]{1,0:T(8,128)(2,1)S(1)}) custom-call(s32[1,288]{1,0:T(1,128)S(4)} %get-tuple-element.32.picks_ref, s32[1,1]{1,0:T(1,128)S(6)} %copy.19.rows_ref, f32[1,16]{1,0:T(1,128)S(1)} %bitcast.21, bf16[128,4,128]{2,1,0:T(4,128)(2,1)S(1)} %shard_map.122.near_ref, ...), custom_call_target="tpu_custom_call" | custom-call | tf_op jit(solution)/shard_map/pallas_call | solution.py:612
  13.7 1.6 %collective-permute-start.4 = (f32[16,256]{1,0:T(8,128)S(1)}, f32[16,256]{1,0:T(8,128)S(1)}, u32[]{:S(2)}, u32[]{:S(2)}) collective-permute-start(f32[16,256]{1,0:T(8,128)S(1)} %get-tuple-element.43), channel_id=1, source_target_pairs={{0,8},{8,0},{16,24},{24,16},{1,9},{9,1},{17,25},{25,17},{2,10},{10... | collective-permute-start | bytes 49160 | tf_op jit(solution)/shard_map/ppermute | solution.py:518
  15.4 1.4 %shard_map.126.big_ref = bf16[384,768]{1,0:T(8,128)(2,1)S(1)} custom-call(s32[1]{0:T(128)} %bitcast.polar_ref, s32[1]{0:T(128)} %bitcast.1.me_ref, bf16[9,4,16]{2,1,0:T(4,128)(2,1)} %bitcast.31, bf16[2,2,128,128]{3,2,1,0:T(8,128)(2,1)} %interp_hbm.3, s32[1,129]{1,0:T(1,128)} %bitcast.33, s32[8,32]{1,0:T(8,128)} %bitcast.24, ...), custom_call_target="tpu_custom_call" | custom-call | flops 4000000000 | bytes 4000000 | tf_op jit(solution)/shard_map/pallas_call | solution.py:626
  16.8 0.8 %collective-permute-done.4 = f32[16,256]{1,0:T(8,128)S(1)} collective-permute-done((f32[16,256]{1,0:T(8,128)S(1)}, f32[16,256]{1,0:T(8,128)S(1)}, u32[]{:S(2)}, u32[]{:S(2)}) %collective-permute-start.4) | collective-permute-done | bytes 16416 | tf_op jit(solution)/shard_map/ppermute | solution.py:518
  17.5 2.6 %collective-permute-start.5 = (f32[16,256]{1,0:T(8,128)S(1)}, f32[16,256]{1,0:T(8,128)S(1)}, u32[]{:S(2)}, u32[]{:S(2)}) collective-permute-start(f32[16,256]{1,0:T(8,128)S(1)} %add.6), channel_id=1, source_target_pairs={{0,16},{8,24},{16,0},{24,8},{1,17},{9,25},{17,1},{25,9},{2,18},{10... | collective-permute-start | bytes 49160 | tf_op jit(solution)/shard_map/ppermute | solution.py:518
  20.1 0.9 %shard_map.127 = (bf16[64,512]{1,0:T(8,128)(2,1)S(1)}, bf16[80,512]{1,0:T(8,128)(2,1)S(1)}, bf16[80,512]{1,0:T(8,128)(2,1)S(1)}, bf16[80,512]{1,0:T(8,128)(2,1)S(1)}) custom-call(s32[1,1]{1,0:T(1,128)S(6)} %copy.19.rows_ref, bf16[160,2048]{1,0:T(8,128)(2,1)S(1)} %get-tuple-element.44.after_hbm.gp_ref, bf16[384,768]{1,0:T(8,128)(2,1)S(1)} %shard_map.126.big_ref), custom_call_target="tpu_custom_call" | custom-call | tf_op jit(solution)/shard_map/pallas_call | solution.py:645
  21.1 1.1 %collective-permute-done.5 = f32[16,256]{1,0:T(8,128)S(1)} collective-permute-done((f32[16,256]{1,0:T(8,128)S(1)}, f32[16,256]{1,0:T(8,128)S(1)}, u32[]{:S(2)}, u32[]{:S(2)}) %collective-permute-start.5) | collective-permute-done | bytes 16416 | tf_op jit(solution)/shard_map/ppermute | solution.py:518
  22.2 0.1 shard_map.128
  22.3 1.6 %collective-permute-start.6 = (bf16[80,512]{1,0:T(8,128)(2,1)S(1)}, bf16[80,512]{1,0:T(8,128)(2,1)S(1)}, u32[]{:S(2)}, u32[]{:S(2)}) collective-permute-start(bf16[80,512]{1,0:T(8,128)(2,1)S(1)} %get-tuple-element.51), channel_id=1, source_target_pairs={{0,6},{1,7},{2,4},{3,5},{4,2},{5,3},{6,0},{7,1},{8,14},{9,15},{10,... | collective-permute-start | bytes 245768 | tf_op jit(solution)/shard_map/ppermute | solution.py:528
  23.8 0.5 %collective-permute-start.7 = (bf16[80,512]{1,0:T(8,128)(2,1)S(1)}, bf16[80,512]{1,0:T(8,128)(2,1)S(1)}, u32[]{:S(2)}, u32[]{:S(2)}) collective-permute-start(bf16[80,512]{1,0:T(8,128)(2,1)S(1)} %get-tuple-element.52), channel_id=1, source_target_pairs={{0,4},{1,5},{2,6},{3,7},{4,0},{5,1},{6,2},{7,3},{8,12},{9,13},{10,... | collective-permute-start | bytes 245768 | tf_op jit(solution)/shard_map/ppermute | solution.py:528
  24.3 1.5 %collective-permute-start.8 = (bf16[80,512]{1,0:T(8,128)(2,1)S(1)}, bf16[80,512]{1,0:T(8,128)(2,1)S(1)}, u32[]{:S(2)}, u32[]{:S(2)}) collective-permute-start(bf16[80,512]{1,0:T(8,128)(2,1)S(1)} %get-tuple-element.53), channel_id=1, source_target_pairs={{0,2},{1,3},{2,0},{3,1},{4,6},{5,7},{6,4},{7,5},{8,10},{9,11},{10,... | collective-permute-start | bytes 245768 | tf_op jit(solution)/shard_map/ppermute | solution.py:528
  25.8 1.9 %collective-permute-done.6.refs_0_.refs_1_ = bf16[80,512]{1,0:T(8,128)(2,1)S(1)} collective-permute-done((bf16[80,512]{1,0:T(8,128)(2,1)S(1)}, bf16[80,512]{1,0:T(8,128)(2,1)S(1)}, u32[]{:S(2)}, u32[]{:S(2)}) %collective-permute-start.6) | collective-permute-done | bytes 81952 | tf_op jit(solution)/shard_map/ppermute | solution.py:528
  27.7 0.8 %collective-permute-done.7.refs_1_.refs_2_ = bf16[80,512]{1,0:T(8,128)(2,1)S(1)} collective-permute-done((bf16[80,512]{1,0:T(8,128)(2,1)S(1)}, bf16[80,512]{1,0:T(8,128)(2,1)S(1)}, u32[]{:S(2)}, u32[]{:S(2)}) %collective-permute-start.7) | collective-permute-done | bytes 81952 | tf_op jit(solution)/shard_map/ppermute | solution.py:528
  28.6 0.2 collective-permute-done.8.refs_2_.refs_3_
  28.8 0.1 collective-permute-start.9
  28.9 1.4 %collective-permute-done.9.refs_4_ = bf16[144,512]{1,0:T(8,128)(2,1)S(1)} collective-permute-done((bf16[144,512]{1,0:T(8,128)(2,1)S(1)}, bf16[144,512]{1,0:T(8,128)(2,1)S(1)}, u32[]{:S(2)}, u32[]{:S(2)}) %collective-permute-start.9) | collective-permute-done | bytes 147488 | tf_op jit(solution)/shard_map/ppermute | solution.py:534
  30.3 0.8 %shard_map.130 = (f32[48,4,128]{2,1,0:T(4,128)}, f32[9,4,16]{2,1,0:T(4,128)}, f32[1,16]{1,0:T(1,128)}, f32[9,16,16]{2,1,0:T(8,128)}) custom-call(bf16[384,768]{1,0:T(8,128)(2,1)S(1)} %shard_map.126.big_ref, f32[16,256]{1,0:T(8,128)S(1)} %get-tuple-element.54.sum_ref, bf16[64,512]{1,0:T(8,128)(2,1)S(1)} %get-tuple-element.47.own_ref.refs_0_, ...), custom_call_target="tpu_custom_call" | custom-call | tf_op jit(solution)/shard_map/pallas_call | solution.py:670
  (5 shorter events, 0.1 us)
Async XLA Ops:
  1.7 7.4 %collective-permute-start = (bf16[64,4,128]{2,1,0:T(4,128)(2,1)S(1)}, bf16[64,4,128]{2,1,0:T(4,128)(2,1)S(1)}, u32[]{:S(2)}, u32[]{:S(2)}) collective-permute-start(bf16[64,4,128]{2,1,0:T(4,128)(2,1)S(1)} %get-tuple-element.35), channel_id=1, source_target_pairs={{0,6},{1,7},{2,4},{3,5},{4,2},{5,3},{6,0},{7,1},{8,14},{9,15},{10,... | collective-permute-start | bytes 196616 | tf_op jit(solution)/shard_map/ppermute | solution.py:528
  5.7 4.3 %collective-permute-start.1 = (bf16[64,4,128]{2,1,0:T(4,128)(2,1)S(1)}, bf16[64,4,128]{2,1,0:T(4,128)(2,1)S(1)}, u32[]{:S(2)}, u32[]{:S(2)}) collective-permute-start(bf16[64,4,128]{2,1,0:T(4,128)(2,1)S(1)} %get-tuple-element.36), channel_id=1, source_target_pairs={{0,4},{1,5},{2,6},{3,7},{4,0},{5,1},{6,2},{7,3},{8,12},{9,13},{10,... | collective-permute-start | bytes 196616 | tf_op jit(solution)/shard_map/ppermute | solution.py:528
  6.2 4.3 %collective-permute-start.2 = (bf16[64,4,128]{2,1,0:T(4,128)(2,1)S(1)}, bf16[64,4,128]{2,1,0:T(4,128)(2,1)S(1)}, u32[]{:S(2)}, u32[]{:S(2)}) collective-permute-start(bf16[64,4,128]{2,1,0:T(4,128)(2,1)S(1)} %get-tuple-element.37), channel_id=1, source_target_pairs={{0,2},{1,3},{2,0},{3,1},{4,6},{5,7},{6,4},{7,5},{8,10},{9,11},{10,... | collective-permute-start | bytes 196616 | tf_op jit(solution)/shard_map/ppermute | solution.py:528
  9.1 2.8 %copy-start = (f32[16]{0:T(128)S(1)}, f32[16]{0:T(128)}, u32[]{:S(2)}) copy-start(f32[16]{0:T(128)} %param.12) | copy-start | bytes 196
  10.5 1.4 %collective-permute-start.3 = (bf16[128,4,128]{2,1,0:T(4,128)(2,1)S(1)}, bf16[128,4,128]{2,1,0:T(4,128)(2,1)S(1)}, u32[]{:S(2)}, u32[]{:S(2)}) collective-permute-start(bf16[128,4,128]{2,1,0:T(4,128)(2,1)S(1)} %shard_map.123), channel_id=1, source_target_pairs={{0,1},{1,0},{2,3},{3,2},{4,5},{5,4},{6,7},{7,6},{8,9},{9,8},{10,11... | collective-permute-start | bytes 393224 | tf_op jit(solution)/shard_map/ppermute | solution.py:534
  13.7 3.8 %collective-permute-start.4 = (f32[16,256]{1,0:T(8,128)S(1)}, f32[16,256]{1,0:T(8,128)S(1)}, u32[]{:S(2)}, u32[]{:S(2)}) collective-permute-start(f32[16,256]{1,0:T(8,128)S(1)} %get-tuple-element.43), channel_id=1, source_target_pairs={{0,8},{8,0},{16,24},{24,16},{1,9},{9,1},{17,25},{25,17},{2,10},{10... | collective-permute-start | bytes 49160 | tf_op jit(solution)/shard_map/ppermute | solution.py:518
  17.5 4.6 %collective-permute-start.5 = (f32[16,256]{1,0:T(8,128)S(1)}, f32[16,256]{1,0:T(8,128)S(1)}, u32[]{:S(2)}, u32[]{:S(2)}) collective-permute-start(f32[16,256]{1,0:T(8,128)S(1)} %add.6), channel_id=1, source_target_pairs={{0,16},{8,24},{16,0},{24,8},{1,17},{9,25},{17,1},{25,9},{2,18},{10... | collective-permute-start | bytes 49160 | tf_op jit(solution)/shard_map/ppermute | solution.py:518
  22.3 5.4 %collective-permute-start.6 = (bf16[80,512]{1,0:T(8,128)(2,1)S(1)}, bf16[80,512]{1,0:T(8,128)(2,1)S(1)}, u32[]{:S(2)}, u32[]{:S(2)}) collective-permute-start(bf16[80,512]{1,0:T(8,128)(2,1)S(1)} %get-tuple-element.51), channel_id=1, source_target_pairs={{0,6},{1,7},{2,4},{3,5},{4,2},{5,3},{6,0},{7,1},{8,14},{9,15},{10,... | collective-permute-start | bytes 245768 | tf_op jit(solution)/shard_map/ppermute | solution.py:528
  23.8 4.7 %collective-permute-start.7 = (bf16[80,512]{1,0:T(8,128)(2,1)S(1)}, bf16[80,512]{1,0:T(8,128)(2,1)S(1)}, u32[]{:S(2)}, u32[]{:S(2)}) collective-permute-start(bf16[80,512]{1,0:T(8,128)(2,1)S(1)} %get-tuple-element.52), channel_id=1, source_target_pairs={{0,4},{1,5},{2,6},{3,7},{4,0},{5,1},{6,2},{7,3},{8,12},{9,13},{10,... | collective-permute-start | bytes 245768 | tf_op jit(solution)/shard_map/ppermute | solution.py:528
  24.3 4.4 %collective-permute-start.8 = (bf16[80,512]{1,0:T(8,128)(2,1)S(1)}, bf16[80,512]{1,0:T(8,128)(2,1)S(1)}, u32[]{:S(2)}, u32[]{:S(2)}) collective-permute-start(bf16[80,512]{1,0:T(8,128)(2,1)S(1)} %get-tuple-element.53), channel_id=1, source_target_pairs={{0,2},{1,3},{2,0},{3,1},{4,6},{5,7},{6,4},{7,5},{8,10},{9,11},{10,... | collective-permute-start | bytes 245768 | tf_op jit(solution)/shard_map/ppermute | solution.py:528
  28.8 1.4 %collective-permute-start.9 = (bf16[144,512]{1,0:T(8,128)(2,1)S(1)}, bf16[144,512]{1,0:T(8,128)(2,1)S(1)}, u32[]{:S(2)}, u32[]{:S(2)}) collective-permute-start(bf16[144,512]{1,0:T(8,128)(2,1)S(1)} %get-tuple-element.55), channel_id=1, source_target_pairs={{0,1},{1,0},{2,3},{3,2},{4,5},{5,4},{6,7},{7,6},{8,9},{9,8},{10,11... | collective-permute-start | bytes 442376 | tf_op jit(solution)/shard_map/ppermute | solution.py:534

commit v6 on v5

--- a/solution.py
+++ b/solution.py
@@ -41,13 +41,12 @@
     return jnp.where(lane == 0, 0.0, pltpu.roll(rows, 1, 1))
 
 
-def store_window(ref, base, y, tile):
-    block, r = divmod(y, R)
-    ref[base + (r + 1) * CH : base + (r + 2) * CH, block * S : (block + 1) * S] = tile
-    if r == 0 and block > 0:
-        ref[base + (R + 1) * CH : base + WIN, (block - 1) * S : block * S] = tile
-    if r == R - 1 and block < NB - 1:
-        ref[base : base + CH, (block + 1) * S : (block + 2) * S] = tile
+def put_block(ref, base, m, tile):
+    ref[base + CH : base + CH + R * CH, m * S : (m + 1) * S] = tile
+    if m > 0:
+        ref[base + (R + 1) * CH : base + WIN, (m - 1) * S : m * S] = tile[0:CH, :]
+    if m < NB - 1:
+        ref[base : base + CH, (m + 1) * S : (m + 2) * S] = tile[(R - 1) * CH :, :]
 
 
 def zero_edges(ref, base):
@@ -132,7 +131,6 @@
     big_ref,
     picks_ref,
     slots_ref,
-    plane,
     cot_ref,
     w1_ref,
     w2_ref,
@@ -206,14 +204,15 @@
         picks_ref[0, half + k] = (spot(j >> 1, chips) - owner) * capacity + slot
 
     copies[-1].wait()
-    for o in range(CH):
-        plane[o * S : (o + 1) * S, :] = cot_ref[o * S : (o + 1) * S, :].astype(F32)
     for dx in range(3):
         zero_edges(big_ref, dx * WIN)
-    for y in range(S):
-        rows = plane[pl.ds(y, CH, stride=S), :]
+    row, col = iota((R * CH, R * CH), 0), iota((R * CH, R * CH), 1)
+    order = (col == (row & 15) * R + (row >> 4)).astype(BF)
+    for m in range(NB):
+        parts = [cot_ref[o * S + m * R : o * S + (m + 1) * R, :] for o in range(CH)]
+        rows = dot(order, jnp.concatenate(parts, axis=0))
         for dx, tile in enumerate((shifted(rows, 1), rows, shifted(rows, -1))):
-            store_window(big_ref, dx * WIN, y, tile.astype(BF))
+            put_block(big_ref, dx * WIN, m, tile.astype(BF))
 
 
 def hidden_kernel(big_ref, gh_ref):
@@ -514,7 +513,7 @@
         return lax.psum(value, "band"), beside
     step = 1
     while step < count:
-        pairs = [(i, i ^ step) for i in range(count)]
+        pairs = [(i, i ^ (count // 2 // step)) for i in range(count)]
         value = value + lax.ppermute(value, "band", pairs)
         if step == 1:
             value, beside = lax.optimization_barrier((value, beside))
@@ -587,7 +586,6 @@
         vmem(1) + smem(1),
         (
             pltpu.SMEM(slots.shape, I32),
-            pltpu.VMEM((CH * S, S), F32),
             pltpu.VMEM(cot.shape, BF),
             pltpu.VMEM(w1.shape, BF),
             pltpu.VMEM(w2.shape, BF),

time: 31.4 us -> 31.4 us (level)
  Pallas kernels: 9.41 us -> 9.08 us
    pallas_call x1, Pallas kernels: 2.73 us -> 2.4 us  [shards(): call(functools.partial(prepare_kernel, chips, capacity), (pltpu.VMEM((3 *...]
  transfers between devices with their start and end apart: 10 -> 10, of which waited for: 9 -> 9; matrix products, arithmetic and copies ran while one was open for 0% -> 0% of each run, Pallas kernels for 18% -> 17%
where the time goes in v6:
time: 31.4 us; the launch traced here: 31 us
  starting transfers between devices  12.5 us (40%)
  Pallas kernels  9.08 us (29%)
  waiting for transfers between devices  8.02 us (26%)
  between operations  1.39 us (4%)
    ppermute x6, starting transfers between devices, to_chips(): lax.ppermute(value, 'tile', [(i, i ^ 2 * (chips - p)) for i in range(coun...  8.16 us
    ppermute x6, waiting for transfers between devices, to_chips(): lax.ppermute(value, 'tile', [(i, i ^ 2 * (chips - p)) for i in range(coun...  4.58 us
    ppermute x2, starting transfers between devices, band_sum(): value = value + lax.ppermute(value, 'band', pairs)  4.22 us
    pallas_call x1, Pallas kernels, shards(): call(functools.partial(prepare_kernel, chips, capacity), (pltpu.VMEM((3 *...  2.4 us
    ppermute x2, waiting for transfers between devices, band_sum(): value = value + lax.ppermute(value, 'band', pairs)  1.87 us
    pallas_call x1, Pallas kernels, shards(): call(functools.partial(patch_kernel, slots.shape[1]), (pltpu.VMEM((CH, 2...  1.82 us
    ppermute x2, waiting for transfers between devices, to_core(): return lax.ppermute(value, 'tile', [(i, i ^ 1) for i in range(count)])  1.57 us
    pallas_call x1, Pallas kernels, shards(): call(functools.partial(lists_kernel, blocks), pltpu.VMEM((rows, 4 * S + t...  1.39 us
  transfers between devices with their start and end apart: 10, of which 9 were waited for; matrix products, arithmetic and copies ran while one was open for 0% of the time, Pallas kernels for 17%

profile of v6, /device:TPU:0, one launch (start us, length us, event | category | flops | bytes accessed | tf_op | source)
XLA Modules:
  0.0 31.0 jit_solution(3305398844334004205)
XLA Ops:
  0.6 1.1 %shard_map.121 = (bf16[64,4,128]{2,1,0:T(4,128)(2,1)S(1)}, bf16[64,4,128]{2,1,0:T(4,128)(2,1)S(1)}, bf16[64,4,128]{2,1,0:T(4,128)(2,1)S(1)}, bf16[64,4,128]{2,1,0:T(4,128)(2,1)S(1)}) custom-call(s32[1]{0:T(128)} %bitcast.1.me_ref, s32[8,32]{1,0:T(8,128)} %bitcast.23, bf16[48,4,128]{2,1,0:T(4,128)(2,1)} %bitcast.22), custom_call_target="tpu_custom_call" | custom-call | tf_op jit(solution)/shard_map/pallas_call | solution.py:559
  1.7 4.0 %collective-permute-start = (bf16[64,4,128]{2,1,0:T(4,128)(2,1)S(1)}, bf16[64,4,128]{2,1,0:T(4,128)(2,1)S(1)}, u32[]{:S(2)}, u32[]{:S(2)}) collective-permute-start(bf16[64,4,128]{2,1,0:T(4,128)(2,1)S(1)} %get-tuple-element.35), channel_id=1, source_target_pairs={{0,6},{1,7},{2,4},{3,5},{4,2},{5,3},{6,0},{7,1},{8,14},{9,15},{10,... | collective-permute-start | bytes 196616 | tf_op jit(solution)/shard_map/ppermute | solution.py:527
  5.7 0.5 %collective-permute-start.1 = (bf16[64,4,128]{2,1,0:T(4,128)(2,1)S(1)}, bf16[64,4,128]{2,1,0:T(4,128)(2,1)S(1)}, u32[]{:S(2)}, u32[]{:S(2)}) collective-permute-start(bf16[64,4,128]{2,1,0:T(4,128)(2,1)S(1)} %get-tuple-element.36), channel_id=1, source_target_pairs={{0,4},{1,5},{2,6},{3,7},{4,0},{5,1},{6,2},{7,3},{8,12},{9,13},{10,... | collective-permute-start | bytes 196616 | tf_op jit(solution)/shard_map/ppermute | solution.py:527
  6.2 0.1 collective-permute-start.2
  6.3 2.4 %shard_map.120 = (bf16[480,2944]{1,0:T(8,128)(2,1)S(1)}, s32[1,288]{1,0:T(1,128)S(4)}) custom-call(s32[1]{0:T(128)} %bitcast.polar_ref, s32[1]{0:T(128)} %bitcast.1.me_ref, bf16[2048,128]{1,0:T(8,128)(2,1)} %bitcast.25, bf16[9,4,16]{2,1,0:T(4,128)(2,1)} %bitcast.30, bf16[9,16,16]{2,1,0:T(8,128)(2,1)} %bitcast.28, bf16[2,2,128,128]{3,2,1,0:T(8,128)(2,1)} %interp_hbm.3, ...), custom_call_target="tpu_custom_call" | custom-call | flops 4000000000 | bytes 4000000 | tf_op jit(solution)/shard_map/pallas_call | solution.py:579
  8.7 0.0 copy-start
  8.7 0.0 collective-permute-done.refs_1_
  8.8 1.2 %collective-permute-done.1.refs_2_ = bf16[64,4,128]{2,1,0:T(4,128)(2,1)S(1)} collective-permute-done((bf16[64,4,128]{2,1,0:T(4,128)(2,1)S(1)}, bf16[64,4,128]{2,1,0:T(4,128)(2,1)S(1)}, u32[]{:S(2)}, u32[]{:S(2)}) %collective-permute-start.1) | collective-permute-done | bytes 65568 | tf_op jit(solution)/shard_map/ppermute | solution.py:527
  9.9 0.5 %collective-permute-done.2.refs_3_ = bf16[64,4,128]{2,1,0:T(4,128)(2,1)S(1)} collective-permute-done((bf16[64,4,128]{2,1,0:T(4,128)(2,1)S(1)}, bf16[64,4,128]{2,1,0:T(4,128)(2,1)S(1)}, u32[]{:S(2)}, u32[]{:S(2)}) %collective-permute-start.2) | collective-permute-done | bytes 65568 | tf_op jit(solution)/shard_map/ppermute | solution.py:527
  10.5 0.1 collective-permute-start.3
  11.2 0.5 %shard_map.124.gh_ref = f32[128,2048]{1,0:T(8,128)S(1)} custom-call(bf16[480,2944]{1,0:T(8,128)(2,1)S(1)} %get-tuple-element.42.big_ref), custom_call_target="tpu_custom_call" | custom-call | tf_op jit(solution)/shard_map/pallas_call | solution.py:606
  11.7 0.2 collective-permute-done.3.far_ref
  11.9 0.0 copy-done
  11.9 1.8 %shard_map.125 = (f32[16,256]{1,0:T(8,128)S(1)}, bf16[160,2048]{1,0:T(8,128)(2,1)S(1)}) custom-call(s32[1,288]{1,0:T(1,128)S(4)} %get-tuple-element.32.picks_ref, s32[1,1]{1,0:T(1,128)S(6)} %copy.19.rows_ref, f32[1,16]{1,0:T(1,128)S(1)} %bitcast.21, bf16[128,4,128]{2,1,0:T(4,128)(2,1)S(1)} %shard_map.122.near_ref, ...), custom_call_target="tpu_custom_call" | custom-call | tf_op jit(solution)/shard_map/pallas_call | solution.py:610
  13.7 2.6 %collective-permute-start.4 = (f32[16,256]{1,0:T(8,128)S(1)}, f32[16,256]{1,0:T(8,128)S(1)}, u32[]{:S(2)}, u32[]{:S(2)}) collective-permute-start(f32[16,256]{1,0:T(8,128)S(1)} %get-tuple-element.43), channel_id=1, source_target_pairs={{0,16},{8,24},{16,0},{24,8},{1,17},{9,25},{17,1},{25,9},{2,18},{10... | collective-permute-start | bytes 49160 | tf_op jit(solution)/shard_map/ppermute | solution.py:517
  16.4 1.4 %shard_map.126.big_ref = bf16[384,768]{1,0:T(8,128)(2,1)S(1)} custom-call(s32[1]{0:T(128)} %bitcast.polar_ref, s32[1]{0:T(128)} %bitcast.1.me_ref, bf16[9,4,16]{2,1,0:T(4,128)(2,1)} %bitcast.31, bf16[2,2,128,128]{3,2,1,0:T(8,128)(2,1)} %interp_hbm.3, s32[1,129]{1,0:T(1,128)} %bitcast.33, s32[8,32]{1,0:T(8,128)} %bitcast.24, ...), custom_call_target="tpu_custom_call" | custom-call | flops 4000000000 | bytes 4000000 | tf_op jit(solution)/shard_map/pallas_call | solution.py:624
  17.8 0.7 %collective-permute-done.4 = f32[16,256]{1,0:T(8,128)S(1)} collective-permute-done((f32[16,256]{1,0:T(8,128)S(1)}, f32[16,256]{1,0:T(8,128)S(1)}, u32[]{:S(2)}, u32[]{:S(2)}) %collective-permute-start.4) | collective-permute-done | bytes 16416 | tf_op jit(solution)/shard_map/ppermute | solution.py:517
  18.4 1.6 %collective-permute-start.5 = (f32[16,256]{1,0:T(8,128)S(1)}, f32[16,256]{1,0:T(8,128)S(1)}, u32[]{:S(2)}, u32[]{:S(2)}) collective-permute-start(f32[16,256]{1,0:T(8,128)S(1)} %add.6), channel_id=1, source_target_pairs={{0,8},{8,0},{16,24},{24,16},{1,9},{9,1},{17,25},{25,17},{2,10},{10... | collective-permute-start | bytes 49160 | tf_op jit(solution)/shard_map/ppermute | solution.py:517
  20.0 0.9 %shard_map.127 = (bf16[64,512]{1,0:T(8,128)(2,1)S(1)}, bf16[80,512]{1,0:T(8,128)(2,1)S(1)}, bf16[80,512]{1,0:T(8,128)(2,1)S(1)}, bf16[80,512]{1,0:T(8,128)(2,1)S(1)}) custom-call(s32[1,1]{1,0:T(1,128)S(6)} %copy.19.rows_ref, bf16[160,2048]{1,0:T(8,128)(2,1)S(1)} %get-tuple-element.44.after_hbm.gp_ref, bf16[384,768]{1,0:T(8,128)(2,1)S(1)} %shard_map.126.big_ref), custom_call_target="tpu_custom_call" | custom-call | tf_op jit(solution)/shard_map/pallas_call | solution.py:643
  20.9 1.2 %collective-permute-done.5 = f32[16,256]{1,0:T(8,128)S(1)} collective-permute-done((f32[16,256]{1,0:T(8,128)S(1)}, f32[16,256]{1,0:T(8,128)S(1)}, u32[]{:S(2)}, u32[]{:S(2)}) %collective-permute-start.5) | collective-permute-done | bytes 16416 | tf_op jit(solution)/shard_map/ppermute | solution.py:517
  22.2 0.1 shard_map.128
  22.3 1.5 %collective-permute-start.6 = (bf16[80,512]{1,0:T(8,128)(2,1)S(1)}, bf16[80,512]{1,0:T(8,128)(2,1)S(1)}, u32[]{:S(2)}, u32[]{:S(2)}) collective-permute-start(bf16[80,512]{1,0:T(8,128)(2,1)S(1)} %get-tuple-element.51), channel_id=1, source_target_pairs={{0,6},{1,7},{2,4},{3,5},{4,2},{5,3},{6,0},{7,1},{8,14},{9,15},{10,... | collective-permute-start | bytes 245768 | tf_op jit(solution)/shard_map/ppermute | solution.py:527
  23.8 0.4 %collective-permute-start.7 = (bf16[80,512]{1,0:T(8,128)(2,1)S(1)}, bf16[80,512]{1,0:T(8,128)(2,1)S(1)}, u32[]{:S(2)}, u32[]{:S(2)}) collective-permute-start(bf16[80,512]{1,0:T(8,128)(2,1)S(1)} %get-tuple-element.52), channel_id=1, source_target_pairs={{0,4},{1,5},{2,6},{3,7},{4,0},{5,1},{6,2},{7,3},{8,12},{9,13},{10,... | collective-permute-start | bytes 245768 | tf_op jit(solution)/shard_map/ppermute | solution.py:527
  24.3 1.6 %collective-permute-start.8 = (bf16[80,512]{1,0:T(8,128)(2,1)S(1)}, bf16[80,512]{1,0:T(8,128)(2,1)S(1)}, u32[]{:S(2)}, u32[]{:S(2)}) collective-permute-start(bf16[80,512]{1,0:T(8,128)(2,1)S(1)} %get-tuple-element.53), channel_id=1, source_target_pairs={{0,2},{1,3},{2,0},{3,1},{4,6},{5,7},{6,4},{7,5},{8,10},{9,11},{10,... | collective-permute-start | bytes 245768 | tf_op jit(solution)/shard_map/ppermute | solution.py:527
  25.8 1.9 %collective-permute-done.6.refs_0_.refs_1_ = bf16[80,512]{1,0:T(8,128)(2,1)S(1)} collective-permute-done((bf16[80,512]{1,0:T(8,128)(2,1)S(1)}, bf16[80,512]{1,0:T(8,128)(2,1)S(1)}, u32[]{:S(2)}, u32[]{:S(2)}) %collective-permute-start.6) | collective-permute-done | bytes 81952 | tf_op jit(solution)/shard_map/ppermute | solution.py:527
  27.7 0.8 %collective-permute-done.7.refs_1_.refs_2_ = bf16[80,512]{1,0:T(8,128)(2,1)S(1)} collective-permute-done((bf16[80,512]{1,0:T(8,128)(2,1)S(1)}, bf16[80,512]{1,0:T(8,128)(2,1)S(1)}, u32[]{:S(2)}, u32[]{:S(2)}) %collective-permute-start.7) | collective-permute-done | bytes 81952 | tf_op jit(solution)/shard_map/ppermute | solution.py:527
  28.6 0.1 collective-permute-done.8.refs_2_.refs_3_
  28.7 0.1 collective-permute-start.9
  28.8 1.4 %collective-permute-done.9.refs_4_ = bf16[144,512]{1,0:T(8,128)(2,1)S(1)} collective-permute-done((bf16[144,512]{1,0:T(8,128)(2,1)S(1)}, bf16[144,512]{1,0:T(8,128)(2,1)S(1)}, u32[]{:S(2)}, u32[]{:S(2)}) %collective-permute-start.9) | collective-permute-done | bytes 147488 | tf_op jit(solution)/shard_map/ppermute | solution.py:533
  30.2 0.8 %shard_map.130 = (f32[48,4,128]{2,1,0:T(4,128)}, f32[9,4,16]{2,1,0:T(4,128)}, f32[1,16]{1,0:T(1,128)}, f32[9,16,16]{2,1,0:T(8,128)}) custom-call(bf16[384,768]{1,0:T(8,128)(2,1)S(1)} %shard_map.126.big_ref, f32[16,256]{1,0:T(8,128)S(1)} %get-tuple-element.54.sum_ref, bf16[64,512]{1,0:T(8,128)(2,1)S(1)} %get-tuple-element.47.own_ref.refs_0_, ...), custom_call_target="tpu_custom_call" | custom-call | tf_op jit(solution)/shard_map/pallas_call | solution.py:668
  (5 shorter events, 0.1 us)
Async XLA Ops:
  1.7 7.0 %collective-permute-start = (bf16[64,4,128]{2,1,0:T(4,128)(2,1)S(1)}, bf16[64,4,128]{2,1,0:T(4,128)(2,1)S(1)}, u32[]{:S(2)}, u32[]{:S(2)}) collective-permute-start(bf16[64,4,128]{2,1,0:T(4,128)(2,1)S(1)} %get-tuple-element.35), channel_id=1, source_target_pairs={{0,6},{1,7},{2,4},{3,5},{4,2},{5,3},{6,0},{7,1},{8,14},{9,15},{10,... | collective-permute-start | bytes 196616 | tf_op jit(solution)/shard_map/ppermute | solution.py:527
  5.7 4.3 %collective-permute-start.1 = (bf16[64,4,128]{2,1,0:T(4,128)(2,1)S(1)}, bf16[64,4,128]{2,1,0:T(4,128)(2,1)S(1)}, u32[]{:S(2)}, u32[]{:S(2)}) collective-permute-start(bf16[64,4,128]{2,1,0:T(4,128)(2,1)S(1)} %get-tuple-element.36), channel_id=1, source_target_pairs={{0,4},{1,5},{2,6},{3,7},{4,0},{5,1},{6,2},{7,3},{8,12},{9,13},{10,... | collective-permute-start | bytes 196616 | tf_op jit(solution)/shard_map/ppermute | solution.py:527
  6.2 4.3 %collective-permute-start.2 = (bf16[64,4,128]{2,1,0:T(4,128)(2,1)S(1)}, bf16[64,4,128]{2,1,0:T(4,128)(2,1)S(1)}, u32[]{:S(2)}, u32[]{:S(2)}) collective-permute-start(bf16[64,4,128]{2,1,0:T(4,128)(2,1)S(1)} %get-tuple-element.37), channel_id=1, source_target_pairs={{0,2},{1,3},{2,0},{3,1},{4,6},{5,7},{6,4},{7,5},{8,10},{9,11},{10,... | collective-permute-start | bytes 196616 | tf_op jit(solution)/shard_map/ppermute | solution.py:527
  8.7 3.2 %copy-start = (f32[16]{0:T(128)S(1)}, f32[16]{0:T(128)}, u32[]{:S(2)}) copy-start(f32[16]{0:T(128)} %param.12) | copy-start | bytes 196
  10.5 1.4 %collective-permute-start.3 = (bf16[128,4,128]{2,1,0:T(4,128)(2,1)S(1)}, bf16[128,4,128]{2,1,0:T(4,128)(2,1)S(1)}, u32[]{:S(2)}, u32[]{:S(2)}) collective-permute-start(bf16[128,4,128]{2,1,0:T(4,128)(2,1)S(1)} %shard_map.123), channel_id=1, source_target_pairs={{0,1},{1,0},{2,3},{3,2},{4,5},{5,4},{6,7},{7,6},{8,9},{9,8},{10,11... | collective-permute-start | bytes 393224 | tf_op jit(solution)/shard_map/ppermute | solution.py:533
  13.7 4.7 %collective-permute-start.4 = (f32[16,256]{1,0:T(8,128)S(1)}, f32[16,256]{1,0:T(8,128)S(1)}, u32[]{:S(2)}, u32[]{:S(2)}) collective-permute-start(f32[16,256]{1,0:T(8,128)S(1)} %get-tuple-element.43), channel_id=1, source_target_pairs={{0,16},{8,24},{16,0},{24,8},{1,17},{9,25},{17,1},{25,9},{2,18},{10... | collective-permute-start | bytes 49160 | tf_op jit(solution)/shard_map/ppermute | solution.py:517
  18.4 3.7 %collective-permute-start.5 = (f32[16,256]{1,0:T(8,128)S(1)}, f32[16,256]{1,0:T(8,128)S(1)}, u32[]{:S(2)}, u32[]{:S(2)}) collective-permute-start(f32[16,256]{1,0:T(8,128)S(1)} %add.6), channel_id=1, source_target_pairs={{0,8},{8,0},{16,24},{24,16},{1,9},{9,1},{17,25},{25,17},{2,10},{10... | collective-permute-start | bytes 49160 | tf_op jit(solution)/shard_map/ppermute | solution.py:517
  22.3 5.4 %collective-permute-start.6 = (bf16[80,512]{1,0:T(8,128)(2,1)S(1)}, bf16[80,512]{1,0:T(8,128)(2,1)S(1)}, u32[]{:S(2)}, u32[]{:S(2)}) collective-permute-start(bf16[80,512]{1,0:T(8,128)(2,1)S(1)} %get-tuple-element.51), channel_id=1, source_target_pairs={{0,6},{1,7},{2,4},{3,5},{4,2},{5,3},{6,0},{7,1},{8,14},{9,15},{10,... | collective-permute-start | bytes 245768 | tf_op jit(solution)/shard_map/ppermute | solution.py:527
  23.8 4.7 %collective-permute-start.7 = (bf16[80,512]{1,0:T(8,128)(2,1)S(1)}, bf16[80,512]{1,0:T(8,128)(2,1)S(1)}, u32[]{:S(2)}, u32[]{:S(2)}) collective-permute-start(bf16[80,512]{1,0:T(8,128)(2,1)S(1)} %get-tuple-element.52), channel_id=1, source_target_pairs={{0,4},{1,5},{2,6},{3,7},{4,0},{5,1},{6,2},{7,3},{8,12},{9,13},{10,... | collective-permute-start | bytes 245768 | tf_op jit(solution)/shard_map/ppermute | solution.py:527
  24.3 4.4 %collective-permute-start.8 = (bf16[80,512]{1,0:T(8,128)(2,1)S(1)}, bf16[80,512]{1,0:T(8,128)(2,1)S(1)}, u32[]{:S(2)}, u32[]{:S(2)}) collective-permute-start(bf16[80,512]{1,0:T(8,128)(2,1)S(1)} %get-tuple-element.53), channel_id=1, source_target_pairs={{0,2},{1,3},{2,0},{3,1},{4,6},{5,7},{6,4},{7,5},{8,10},{9,11},{10,... | collective-permute-start | bytes 245768 | tf_op jit(solution)/shard_map/ppermute | solution.py:527
  28.7 1.4 %collective-permute-start.9 = (bf16[144,512]{1,0:T(8,128)(2,1)S(1)}, bf16[144,512]{1,0:T(8,128)(2,1)S(1)}, u32[]{:S(2)}, u32[]{:S(2)}) collective-permute-start(bf16[144,512]{1,0:T(8,128)(2,1)S(1)} %get-tuple-element.55), channel_id=1, source_target_pairs={{0,1},{1,0},{2,3},{3,2},{4,5},{5,4},{6,7},{7,6},{8,9},{9,8},{10,11... | collective-permute-start | bytes 442376 | tf_op jit(solution)/shard_map/ppermute | solution.py:533
